TPU v7x, 256 devices: a whole 4x4x8 slice. The times are simulated.
256 devices in a mesh: dp: 16 (over z, core), expert: 16 (over y, x).
Axes of the slice: x: 4, y: 4, z: 8, core: 2. Of those that a mesh axis runs over, the one named last changes fastest.
Arguments:
- activations: bfloat16 [32768, 2048], P(('dp', 'expert')), may hold values from -6 to 6
- routes: int32 [32768, 8], P(('dp', 'expert')), may hold values from 0 to 127, as said below
- gates: float32 [32768, 8], P(('dp', 'expert')), may hold values from 0.05 to 1
- gate_levels: bfloat16 [16, 2048, 768], P('expert'), may hold values from -8 to 7, as said below
- gate_scales: float32 [16, 16, 768], P('expert'), may hold values from 0.0022097088 to 0.008838835
- up_levels: bfloat16 [16, 2048, 768], P('expert'), may hold values from -8 to 7, as said below
- up_scales: float32 [16, 16, 768], P('expert'), may hold values from 0.0022097088 to 0.008838835
- down_levels: bfloat16 [16, 768, 2048], P('expert'), may hold values from -8 to 7, as said below
- down_scales: float32 [16, 6, 2048], P('expert'), may hold values from 0.0036084391 to 0.0144337565
- gate_adapter_first: bfloat16 [16, 16, 2048], P('expert'), may hold values from -0.125 to 0.125
- gate_adapter_second: bfloat16 [16, 16, 768], P('expert'), may hold values from -1.5 to 1.5
- up_adapter_first: bfloat16 [16, 16, 2048], P('expert'), may hold values from -0.125 to 0.125
- up_adapter_second: bfloat16 [16, 16, 768], P('expert'), may hold values from -1.5 to 1.5
- down_adapter_first: bfloat16 [16, 16, 768], P('expert'), may hold values from -0.21875 to 0.21875
- down_adapter_second: bfloat16 [16, 16, 2048], P('expert'), may hold values from -1.5 to 1.5
- upstream: bfloat16 [32768, 2048], P(('dp', 'expert')), may hold values from -6 to 6
Outputs:
- mixed: bfloat16 [32768, 2048], P(('dp', 'expert'))
- input_grad: bfloat16 [32768, 2048], P(('dp', 'expert'))
- grad_wide: float32 [16, 3, 16, 2048], P('expert', None, None, 'dp')
- grad_narrow: float32 [16, 3, 16, 768], P('expert', None, 'dp')
Inputs may be any that keep to these rules, and one draw needn't show every extreme that they name: `routes`: each row names 8 different experts. No expert is named by more than 16 rows of one device, and some expert below 16 is named by exactly 16 rows of every device. `gate_levels`: whole numbers. `up_levels`: whole numbers. `down_levels`: whole numbers.
All inputs are finite; a program needn't handle non-finite values.
Results may differ from a plain program's by a relative error of at most 0.011.
Values may be sent and summed in bfloat16 or wider, within the bound.
No kernel may reach another device: no remote copies, remote signals or barrier semaphores. Data moves between devices by JAX's collectives and lax.ppermute only.
A program may use at most 128 MiB of HBM per device.

v0:
```python
import jax
import jax.numpy as jnp
from jax import lax
from jax.sharding import PartitionSpec as P

GROUP = 128
CAP = 16


ADAPTER_SCALING = 0.5


def matrix_product(left_operand, right_operand):
    return lax.dot_general(
        left_operand, right_operand, (((1,), (1,)), ((), ())), preferred_element_type=jnp.float32
    )


def product_result(left_operand, right_operand):
    return jnp.dot(left_operand, right_operand, preferred_element_type=jnp.float32)


def rank_grad(left_operand, right_operand):
    return ADAPTER_SCALING * lax.dot_general(
        left_operand, right_operand, (((0,), (0,)), ((), ())), preferred_element_type=jnp.float32
    )


def dequantize(levels, scales):
    return (levels.astype(jnp.float32) * jnp.repeat(scales, GROUP, axis=0)).astype(jnp.bfloat16)


def forward_part(input_rows, params):
    (
        gate_base_weight,
        up_base_weight,
        down_base_weight,
        gate_adapter_first,
        gate_adapter_second,
        up_adapter_first,
        up_adapter_second,
        down_adapter_first,
        down_adapter_second,
    ) = params
    gate_lowrank = matrix_product(input_rows, gate_adapter_first).astype(jnp.bfloat16)
    up_lowrank = matrix_product(input_rows, up_adapter_first).astype(jnp.bfloat16)
    gate_preactivation = product_result(
        input_rows, gate_base_weight
    ) + ADAPTER_SCALING * product_result(gate_lowrank, gate_adapter_second)
    up_preactivation = product_result(
        input_rows, up_base_weight
    ) + ADAPTER_SCALING * product_result(up_lowrank, up_adapter_second)
    logistic = jax.nn.sigmoid(gate_preactivation)
    activated = gate_preactivation * logistic
    hidden_state = (activated * up_preactivation).astype(jnp.bfloat16)
    down_lowrank = matrix_product(hidden_state, down_adapter_first).astype(jnp.bfloat16)
    output_rows = (
        product_result(hidden_state, down_base_weight)
        + ADAPTER_SCALING * product_result(down_lowrank, down_adapter_second)
    ).astype(jnp.bfloat16)
    return (
        output_rows,
        (
            gate_lowrank,
            up_lowrank,
            gate_preactivation,
            up_preactivation,
            logistic,
            activated,
            hidden_state,
            down_lowrank,
        ),
    )


def backward_down(output_gradient, stored, params):
    (
        gate_base_weight,
        up_base_weight,
        down_base_weight,
        gate_adapter_first,
        gate_adapter_second,
        up_adapter_first,
        up_adapter_second,
        down_adapter_first,
        down_adapter_second,
    ) = params
    hidden_state, down_lowrank = (stored[6], stored[7])
    down_backprop = matrix_product(output_gradient, down_adapter_second).astype(jnp.bfloat16)
    hidden_gradient = matrix_product(
        output_gradient, down_base_weight
    ) + ADAPTER_SCALING * product_result(down_backprop, down_adapter_first)
    return (
        hidden_gradient,
        rank_grad(down_lowrank, output_gradient),
        rank_grad(down_backprop, hidden_state),
    )


def backward_rest(input_rows, hidden_gradient, stored, params):
    (
        gate_base_weight,
        up_base_weight,
        down_base_weight,
        gate_adapter_first,
        gate_adapter_second,
        up_adapter_first,
        up_adapter_second,
        down_adapter_first,
        down_adapter_second,
    ) = params
    gate_lowrank, up_lowrank, gate_preactivation, up_preactivation, logistic, activated = stored[:6]
    d_gate = (
        hidden_gradient
        * up_preactivation
        * logistic
        * (1.0 + gate_preactivation * (1.0 - logistic))
    ).astype(jnp.bfloat16)
    d_up = (hidden_gradient * activated).astype(jnp.bfloat16)
    gate_backprop = matrix_product(d_gate, gate_adapter_second).astype(jnp.bfloat16)
    up_backprop = matrix_product(d_up, up_adapter_second).astype(jnp.bfloat16)
    row_gradient = matrix_product(d_gate, gate_base_weight) + matrix_product(d_up, up_base_weight)
    row_gradient = (
        row_gradient
        + ADAPTER_SCALING
        * (
            product_result(gate_backprop, gate_adapter_first)
            + product_result(up_backprop, up_adapter_first)
        )
    ).astype(jnp.bfloat16)
    grads = (
        rank_grad(gate_backprop, input_rows),
        rank_grad(up_backprop, input_rows),
        rank_grad(gate_lowrank, d_gate),
        rank_grad(up_lowrank, d_up),
    )
    return (row_gradient, grads)


def shards(
    activations,
    routes,
    gates,
    gate_levels,
    gate_scales,
    up_levels,
    up_scales,
    down_levels,
    down_scales,
    gate_adapter_first,
    gate_adapter_second,
    up_adapter_first,
    up_adapter_second,
    down_adapter_first,
    down_adapter_second,
    upstream,
):
    experts = lax.axis_size("expert")
    tok_rows = activations.shape[0]
    per_token = routes.shape[1]
    slot_count = experts * CAP
    flat_routes = routes.reshape(-1)
    columns = jnp.arange(experts, dtype=jnp.int32)
    onehot = (flat_routes[:, None] == columns[None, :]).astype(jnp.int32)
    before = jnp.cumsum(onehot, axis=0) - onehot
    place = jnp.sum(before * onehot, axis=1)
    slot_of = jnp.where(flat_routes < experts, flat_routes * CAP + place, slot_count)
    owner_row = jnp.arange(flat_routes.shape[0], dtype=jnp.int32) // per_token
    source_of = (
        jnp.full((slot_count + 1,), tok_rows, jnp.int32).at[slot_of].set(owner_row)[:slot_count]
    )
    weight_of = (
        jnp.zeros((slot_count + 1,), jnp.float32).at[slot_of].set(gates.reshape(-1))[:slot_count]
    )
    zero_row = jnp.zeros((1, activations.shape[1]), jnp.bfloat16)
    send_rows = jnp.concatenate([activations, zero_row], axis=0)[source_of].reshape(
        experts, CAP, -1
    )
    upstream_rows = jnp.concatenate([upstream, zero_row], axis=0)[source_of].astype(jnp.float32)
    send_grad = (weight_of[:, None] * upstream_rows).astype(jnp.bfloat16).reshape(experts, CAP, -1)
    frozen = (
        dequantize(gate_levels[0], gate_scales[0]),
        dequantize(up_levels[0], up_scales[0]),
        dequantize(down_levels[0], down_scales[0]),
    )
    params = frozen + tuple(
        (
            weight[0]
            for weight in (
                gate_adapter_first,
                gate_adapter_second,
                up_adapter_first,
                up_adapter_second,
                down_adapter_first,
                down_adapter_second,
            )
        )
    )
    got_rows = lax.all_to_all(send_rows, "expert", split_axis=0, concat_axis=0, tiled=True)
    input_rows = got_rows.reshape(slot_count, -1)
    output_rows, stored = forward_part(input_rows, params)
    returned = lax.all_to_all(
        output_rows.reshape(experts, CAP, -1), "expert", split_axis=0, concat_axis=0, tiled=True
    )
    got_grad = lax.all_to_all(send_grad, "expert", split_axis=0, concat_axis=0, tiled=True)
    output_gradient = got_grad.reshape(slot_count, -1)
    hidden_gradient, grad_down_outer, grad_down_inner = backward_down(
        output_gradient, stored, params
    )
    row_gradient, grads = backward_rest(input_rows, hidden_gradient, stored, params)
    back_rows = lax.all_to_all(
        row_gradient.reshape(experts, CAP, -1), "expert", split_axis=0, concat_axis=0, tiled=True
    )
    grad_wide = jnp.stack([grads[0], grads[1], grad_down_outer])
    grad_narrow = jnp.stack([grads[2], grads[3], grad_down_inner])
    grad_wide, grad_narrow = (
        lax.psum_scatter(grad_wide, "dp", scatter_dimension=2, tiled=True),
        lax.psum_scatter(grad_narrow, "dp", scatter_dimension=1, tiled=True),
    )
    output_pad = jnp.concatenate([returned.reshape(slot_count, -1), zero_row], axis=0)
    back_pad = jnp.concatenate([back_rows.reshape(slot_count, -1), zero_row], axis=0)
    token_slots = slot_of.reshape(tok_rows, per_token)
    mixed = jnp.zeros((tok_rows, activations.shape[1]), jnp.float32)
    input_grad = jnp.zeros((tok_rows, activations.shape[1]), jnp.float32)
    for column in range(per_token):
        column_slot = token_slots[:, column]
        mixed = mixed + gates[:, column : column + 1] * output_pad[column_slot].astype(jnp.float32)
        input_grad = input_grad + back_pad[column_slot].astype(jnp.float32)
    return (
        mixed.astype(jnp.bfloat16),
        input_grad.astype(jnp.bfloat16),
        grad_wide[None],
        grad_narrow[None],
    )


def solution(mesh):
    placed = (
        P(("dp", "expert"), None),
        P(("dp", "expert"), None),
        P(("dp", "expert"), None),
        P("expert", None, None),
        P("expert", None, None),
        P("expert", None, None),
        P("expert", None, None),
        P("expert", None, None),
        P("expert", None, None),
        P("expert", None, None),
        P("expert", None, None),
        P("expert", None, None),
        P("expert", None, None),
        P("expert", None, None),
        P("expert", None, None),
        P(("dp", "expert"), None),
    )
    return jax.shard_map(
        shards,
        mesh=mesh,
        in_specs=placed,
        out_specs=(
            P(("dp", "expert"), None),
            P(("dp", "expert"), None),
            P("expert", None, None, "dp"),
            P("expert", None, "dp", None),
        ),
        check_vma=False,
    )
```

profile of v0, /device:TPU:32, one launch (start us, length us, event | category | flops | bytes accessed | tf_op | source)
XLA Modules:
  0.0 288.4 jit_solution(10252061598000084285)
XLA Ops:
  7.2 0.8 copy.36
  8.2 4.5 %reduce-window.6 = s32[16,8,128]{2,1,0:T(8,128)S(1)} reduce-window(s32[16,8,128]{2,1,0:T(8,128)S(1)} %fusion.37, s32[]{:T(128)} %constant.17.clone.1), window={size=1x1x128 pad=0_0x0_0x127_0}, to_apply=%region_0.0 | reduce-window | flops 2080768 | bytes 131076 | tf_op jit(solution)/shard_map/reduce-window
  13.5 4.3 %scatter_custom_fusion = s32[257]{0:T(512)S(1)} fusion(s32[1024]{0:T(1024)S(1)} %bitcast.190, s32[1024]{0:T(1024)S(1)} %add_select_fusion.1, s32[]{:T(128)} %constant.15.clone.1), kind=kCustom, calls=%fused_computation.134 | custom fusion | bytes 1032 | tf_op jit(solution)/shard_map/scatter | solution.py:170
  17.9 1.1 concatenate.12
  19.0 2.3 gather_fusion
  21.3 7.0 %all-to-all-start = ((bf16[16,16,2048]{2,1,0:T(8,128)(2,1)}), bf16[16,16,2048]{2,1,0:T(8,128)(2,1)S(1)}, u32[]{:S(2)}, u32[]{:S(2)}) async-start(bf16[16,16,2048]{2,1,0:T(8,128)(2,1)} %bitcast.5), calls=%async_computation | async-start | bytes 2097152 | tf_op jit(solution)/shard_map/all_to_all | solution.py:199
  28.5 0.6 slice_bitcast_fusion.7
  29.1 4.3 %fusion = bf16[2048,768]{1,0:T(8,128)(2,1)} fusion(f32[16,768]{1,0:T(8,128)S(1)} %bitcast.184, bf16[1,2048,768]{2,1,0:T(8,128)(2,1)} %param.21), kind=kLoop, calls=%fused_computation.21 | loop fusion | flops 4718592 | bytes 6340608 | tf_op jit(solution)/shard_map/convert_element_type | solution.py:30
  33.4 2.3 multiply_convert_fusion.1
  35.8 1.4 gather_fusion.9
  37.3 4.3 %scatter_custom_fusion.1 = f32[257]{0:T(512)S(1)} fusion(s32[1024]{0:T(1024)S(1)} %bitcast.191, f32[1024]{0:T(1024)S(1)} %reshape.342, f32[]{:T(128)} %constant.47.clone.1), kind=kCustom, calls=%fused_computation.132 | custom fusion | bytes 1032 | tf_op jit(solution)/shard_map/scatter | solution.py:173
  42.1 1.3 fusion.11
  43.9 4.3 %fusion.1 = bf16[2048,768]{1,0:T(8,128)(2,1)} fusion(f32[16,768]{1,0:T(8,128)S(1)} %bitcast.186, bf16[1,2048,768]{2,1,0:T(8,128)(2,1)} %param.19), kind=kLoop, calls=%fused_computation.23 | loop fusion | flops 4718592 | bytes 6340608 | tf_op jit(solution)/shard_map/convert_element_type | solution.py:30
  48.2 0.6 pad_clamp_fusion.6
  48.8 0.6 pad_clamp_fusion.4
  49.4 0.6 pad_clamp_fusion.2
  50.0 0.6 pad_clamp_fusion
  50.6 2.5 fusion.2
  53.2 2.3 multiply_convert_fusion.2
  55.5 2.5 multiply_convert_fusion
  58.0 7.2 %all-to-all-start.2 = ((bf16[16,16,2048]{2,1,0:T(8,128)(2,1)}), bf16[16,16,2048]{2,1,0:T(8,128)(2,1)S(1)}, u32[]{:S(2)}, u32[]{:S(2)}) async-start(bf16[16,16,2048]{2,1,0:T(8,128)(2,1)} %fusion.11), calls=%async_computation.2 | async-start | bytes 2097152 | tf_op jit(solution)/shard_map/all_to_all | solution.py:205
  66.0 3.1 %fusion.52 = f32[256,768]{1,0:T(8,128)S(1)} fusion(bf16[256,2048]{1,0:T(8,128)(2,1)S(1)} %bitcast.165, bf16[2048,768]{1,0:T(8,128)(2,1)} %bitcast.178), kind=kOutput, calls=%fused_computation.145 | convolution fusion | flops 805306368 | bytes 4980736 | tf_op jit(solution)/shard_map/dot_general | solution.py:20
  69.1 1.9 fusion.51
  70.9 11.2 %all-to-all-done.2 = bf16[16,16,2048]{2,1,0:T(8,128)(2,1)S(1)} async-done(((bf16[16,16,2048]{2,1,0:T(8,128)(2,1)}), bf16[16,16,2048]{2,1,0:T(8,128)(2,1)S(1)}, u32[]{:S(2)}, u32[]{:S(2)}) %all-to-all-start.2) | async-done | bytes 1048608 | tf_op jit(solution)/shard_map/all_to_all | solution.py:205
  82.1 3.3 %fusion.54 = f32[256,768]{1,0:T(8,128)S(1)} fusion(bf16[256,2048]{1,0:T(8,128)(2,1)S(1)} %bitcast.172, bf16[768,2048]{1,0:T(8,128)(2,1)} %bitcast.179), kind=kOutput, calls=%fused_computation.147 | convolution fusion | flops 805306368 | bytes 4980736 | tf_op jit(solution)/shard_map/dot_general | solution.py:14
  86.5 0.6 multiply_convert_fusion.3
  87.1 0.8 fusion.15
  87.9 0.8 convolution_convert_fusion.5
  90.3 1.0 fusion.55
  91.3 0.6 copy-done.5
  91.9 1.0 convolution_add_fusion.1
  92.9 1.4 fusion.6
  94.3 4.6 %all-to-all-start.3 = ((bf16[16,16,2048]{2,1,0:T(8,128)(2,1)}), bf16[16,16,2048]{2,1,0:T(8,128)(2,1)}, u32[]{:S(2)}, u32[]{:S(2)}) async-start(bf16[16,16,2048]{2,1,0:T(8,128)(2,1)} %bitcast.177), calls=%async_computation.3 | async-start | bytes 2097152 | tf_op jit(solution)/shard_map/all_to_all | solution.py:211
  98.9 1.8 fusion.16
  100.7 1.8 fusion.17
  102.5 2.1 fusion.8
  104.7 2.0 fusion.53
  106.7 1.4 fusion.7
  108.1 6.6 %all-to-all-done.3 = bf16[16,16,2048]{2,1,0:T(8,128)(2,1)} async-done(((bf16[16,16,2048]{2,1,0:T(8,128)(2,1)}), bf16[16,16,2048]{2,1,0:T(8,128)(2,1)}, u32[]{:S(2)}, u32[]{:S(2)}) %all-to-all-start.3) | async-done | bytes 1048608 | tf_op jit(solution)/shard_map/all_to_all | solution.py:211
  114.8 3.7 %all-to-all-start.1 = ((bf16[16,16,2048]{2,1,0:T(8,128)(2,1)}), bf16[16,16,2048]{2,1,0:T(8,128)(2,1)S(1)}, u32[]{:S(2)}, u32[]{:S(2)}) async-start(bf16[16,16,2048]{2,1,0:T(8,128)(2,1)} %bitcast.21), calls=%async_computation.1 | async-start | bytes 2097152 | tf_op jit(solution)/shard_map/all_to_all | solution.py:202
  118.5 0.7 pad_maximum_fusion.1
  119.5 0.8 pad_maximum_fusion
  120.3 104.2 %all-reduce.7.cloned.1.call-done = f32[3,16,768]{2,1,0:T(8,128)} async-done(((f32[3,16,768]{2,1,0:T(8,128)}), f32[3,16,768]{2,1,0:T(8,128)}) %all-reduce.7.cloned.1.call-update) | async-done | bytes 147472
  224.5 2.1 dynamic-slice_bitcast_fusion
  226.5 1.3 concatenate.15
  227.9 1.1 gather_fusion.10
  228.9 1.1 gather_fusion.11
  230.0 1.9 gather_fusion.12
  231.8 1.9 gather_fusion.13
  233.7 1.9 gather_fusion.14
  235.6 1.9 gather_fusion.15
  237.4 1.8 gather_fusion.16
  239.3 1.8 gather_fusion.17
  241.1 3.3 %add_convert_fusion = bf16[128,2048]{1,0:T(8,128)(2,1)} fusion(bf16[128,2048]{1,0:T(8,128)(2,1)} %gather_fusion.17, bf16[128,2048]{1,0:T(8,128)(2,1)} %gather_fusion.16, bf16[128,2048]{1,0:T(8,128)(2,1)} %gather_fusion.15, bf16[128,2048]{1,0:T(8,128)(2,1)} %gather_fusion.14, bf16[128,2048]{1,0:T(8,128)(2,1)} %gather_fusion.13, ...), kind=kLoop, calls=%fused_computation.63 | loop fusion | flops 4194304 | bytes 4718592 | tf_op jit(solution)/shard_map/convert_element_type | solution.py:231
  244.6 1.1 gather_fusion.1
  245.6 1.1 gather_fusion.2
  246.7 1.1 gather_fusion.3
  247.7 1.1 gather_fusion.4
  248.8 1.8 gather_fusion.5
  250.6 1.9 gather_fusion.6
  252.5 1.9 gather_fusion.7
  254.4 2.0 gather_fusion.8
  256.5 3.2 %add_convert_fusion.1 = bf16[128,2048]{1,0:T(8,128)(2,1)} fusion(bf16[128,2048]{1,0:T(8,128)(2,1)} %gather_fusion.8, bf16[128,2048]{1,0:T(8,128)(2,1)} %gather_fusion.7, bf16[128,2048]{1,0:T(8,128)(2,1)} %gather_fusion.6, bf16[128,2048]{1,0:T(8,128)(2,1)} %gather_fusion.5, bf16[128,2048]{1,0:T(8,128)(2,1)S(1)} %gather_fusion.4, ...), kind=kLoop, calls=%fused_computation.64 | loop fusion | flops 6291456 | bytes 4722688 | tf_op jit(solution)/shard_map/convert_element_type | solution.py:230
  259.7 21.9 %reduce-scatter.3.cloned.1.call-done = f32[3,16,128]{2,1,0:T(8,128)} async-done(((f32[3,16,2048]{2,1,0:T(8,128)}), f32[3,16,128]{2,1,0:T(8,128)}) %reduce-scatter.3.cloned.1.call-update) | async-done | bytes 24592 | tf_op jit(solution)/shard_map/reduce_scatter | solution.py:217
  (118 shorter events, 6.0 us)
Async XLA Ops:
  7.2 58.4 %copy-start = (bf16[1,16,2048]{2,1,0:T(8,128)(2,1)S(1)}, bf16[1,16,2048]{2,1,0:T(8,128)(2,1)}, u32[]{:S(2)}) copy-start(bf16[1,16,2048]{2,1,0:T(8,128)(2,1)} %param.25) | copy-start | bytes 196612
  18.9 9.4 %copy-start.28 = (f32[128,8]{0,1:T(8,128)S(1)}, f32[128,8]{0,1:T(8,128)}, u32[]{:S(2)}) copy-start(f32[128,8]{0,1:T(8,128)} %param.18) | copy-start | bytes 12292
  19.0 10.1 %copy-start.18 = (f32[1,16,768]{2,1,0:T(8,128)S(1)}, f32[1,16,768]{2,1,0:T(8,128)}, u32[]{:S(2)}) copy-start(f32[1,16,768]{2,1,0:T(8,128)} %param.22) | copy-start | bytes 147460
  21.3 36.7 %all-to-all-start = ((bf16[16,16,2048]{2,1,0:T(8,128)(2,1)}), bf16[16,16,2048]{2,1,0:T(8,128)(2,1)S(1)}, u32[]{:S(2)}, u32[]{:S(2)}) async-start(bf16[16,16,2048]{2,1,0:T(8,128)(2,1)} %bitcast.5), calls=%async_computation | async-start | bytes 2097152 | tf_op jit(solution)/shard_map/all_to_all | solution.py:199
  29.1 4.3 %copy-start.2 = (bf16[1,2048,768]{2,1,0:T(8,128)(2,1)S(1)}, bf16[1,2048,768]{2,1,0:T(8,128)(2,1)}, u32[]{:S(2)}) copy-start(bf16[1,2048,768]{2,1,0:T(8,128)(2,1)} %param.21) | copy-start | bytes 9437188
  33.4 2.3 copy-start.15
  35.8 5.9 %copy-start.26 = (f32[1,6,2048]{2,0,1:T(1,128)S(1)}, f32[1,6,2048]{2,0,1:T(1,128)}, u32[]{:S(2)}) copy-start(f32[1,6,2048]{2,0,1:T(1,128)} %param.24) | copy-start | bytes 147460
  35.8 7.5 %copy-start.37 = (u32[256]{0:T(256)S(1)}, u32[256]{0:T(256)}, u32[]{:S(2)}) copy-start(u32[256]{0:T(256)} %constant.74) | copy-start | bytes 3076
  35.8 8.1 %copy-start.19 = (f32[1,16,768]{2,1,0:T(8,128)S(1)}, f32[1,16,768]{2,1,0:T(8,128)}, u32[]{:S(2)}) copy-start(f32[1,16,768]{2,1,0:T(8,128)} %param.20) | copy-start | bytes 147460
  43.9 6.7 %copy-start.4 = (bf16[1,768,2048]{2,1,0:T(8,128)(2,1)S(1)}, bf16[1,768,2048]{2,1,0:T(8,128)(2,1)}, u32[]{:S(2)}) copy-start(bf16[1,768,2048]{2,1,0:T(8,128)(2,1)} %param.23) | copy-start | bytes 9437188
  50.6 2.5 copy-start.3
  55.5 9.7 %copy-start.17 = (bf16[1,16,2048]{2,1,0:T(8,128)(2,1)S(1)}, bf16[1,16,2048]{2,1,0:T(8,128)(2,1)}, u32[]{:S(2)}) copy-start(bf16[1,16,2048]{2,1,0:T(8,128)(2,1)} %param.27) | copy-start | bytes 196612
  58.0 24.1 %all-to-all-start.2 = ((bf16[16,16,2048]{2,1,0:T(8,128)(2,1)}), bf16[16,16,2048]{2,1,0:T(8,128)(2,1)S(1)}, u32[]{:S(2)}, u32[]{:S(2)}) async-start(bf16[16,16,2048]{2,1,0:T(8,128)(2,1)} %fusion.11), calls=%async_computation.2 | async-start | bytes 2097152 | tf_op jit(solution)/shard_map/all_to_all | solution.py:205
  65.6 3.5 %copy-start.12 = (bf16[16,128,768]{2,1,0:T(8,128)(2,1)S(1)}, bf16[16,128,768]{2,1,0:T(8,128)(2,1)}, u32[]{:S(2)}) copy-start(bf16[16,128,768]{2,1,0:T(8,128)(2,1)} %multiply_convert_fusion.2) | copy-start | bytes 9437188
  70.9 14.5 %copy-start.16 = (bf16[1,16,2048]{2,1,0:T(8,128)(2,1)S(1)}, bf16[1,16,2048]{2,1,0:T(8,128)(2,1)}, u32[]{:S(2)}) copy-start(bf16[1,16,2048]{2,1,0:T(8,128)(2,1)} %param.30) | copy-start | bytes 196612
  82.1 3.7 %copy-start.8 = (bf16[16,16,2048]{2,1,0:T(8,128)(2,1)}, bf16[16,16,2048]{2,1,0:T(8,128)(2,1)S(1)}, u32[]{:S(2)}) copy-start(bf16[16,16,2048]{2,1,0:T(8,128)(2,1)S(1)} %all-to-all-done.2) | copy-start | bytes 3145732
  82.1 3.7 %copy-start.24 = (bf16[1,16,768]{2,1,0:T(8,128)(2,1)S(1)}, bf16[1,16,768]{2,1,0:T(8,128)(2,1)}, u32[]{:S(2)}) copy-start(bf16[1,16,768]{2,1,0:T(8,128)(2,1)} %param.28) | copy-start | bytes 73732
  82.1 4.0 %copy-start.13 = (f32[256,768]{1,0:T(8,128)S(1)}, f32[256,768]{1,0:T(8,128)}, u32[]{:S(2)}) copy-start(f32[256,768]{1,0:T(8,128)} %fusion.51) | copy-start | bytes 2359300
  82.1 4.1 %copy-start.23 = (bf16[1,16,768]{2,1,0:T(8,128)(2,1)S(1)}, bf16[1,16,768]{2,1,0:T(8,128)(2,1)}, u32[]{:S(2)}) copy-start(bf16[1,16,768]{2,1,0:T(8,128)(2,1)} %param.26) | copy-start | bytes 73732
  85.4 1.0 copy-start.27
  87.1 2.9 copy-start.9
  87.1 3.2 %copy-start.10 = (bf16[256,768]{1,0:T(8,128)(2,1)}, bf16[256,768]{1,0:T(8,128)(2,1)S(1)}, u32[]{:S(2)}) copy-start(bf16[256,768]{1,0:T(8,128)(2,1)S(1)} %get-tuple-element.15) | copy-start | bytes 1179652
  87.1 4.2 %copy-start.11 = (bf16[256,768]{1,0:T(8,128)(2,1)}, bf16[256,768]{1,0:T(8,128)(2,1)S(1)}, u32[]{:S(2)}) copy-start(bf16[256,768]{1,0:T(8,128)(2,1)S(1)} %get-tuple-element.14) | copy-start | bytes 1179652
  87.1 3.2 %copy-start.6 = (bf16[2048,768]{1,0:T(8,128)(2,1)S(1)}, bf16[2048,768]{1,0:T(8,128)(2,1)}, u32[]{:S(2)}) copy-start(bf16[2048,768]{1,0:T(8,128)(2,1)} %fusion.1) | copy-start | bytes 9437188
  89.9 2.0 copy-start.5
  92.9 9.6 %copy-start.25 = (bf16[256,16]{0,1:T(8,128)(2,1)S(1)}, bf16[256,16]{0,1:T(8,128)(2,1)}, u32[]{:S(2)}) copy-start(bf16[256,16]{0,1:T(8,128)(2,1)} %convolution_convert_fusion.5) | copy-start | bytes 24580
  94.3 10.3 %copy-start.7 = (bf16[768,2048]{1,0:T(8,128)(2,1)S(1)}, bf16[768,2048]{1,0:T(8,128)(2,1)}, u32[]{:S(2)}) copy-start(bf16[768,2048]{1,0:T(8,128)(2,1)} %fusion.2) | copy-start | bytes 9437188
  94.3 20.4 %all-to-all-start.3 = ((bf16[16,16,2048]{2,1,0:T(8,128)(2,1)}), bf16[16,16,2048]{2,1,0:T(8,128)(2,1)}, u32[]{:S(2)}, u32[]{:S(2)}) async-start(bf16[16,16,2048]{2,1,0:T(8,128)(2,1)} %bitcast.177), calls=%async_computation.3 | async-start | bytes 2097152 | tf_op jit(solution)/shard_map/all_to_all | solution.py:211
  106.7 11.8 %copy-start.20 = (f32[1,16,768]{2,1,0:T(8,128)S(1)}, f32[1,16,768]{2,1,0:T(8,128)}, u32[]{:S(2)}) copy-start(f32[1,16,768]{2,1,0:T(8,128)} %fusion.15) | copy-start | bytes 147460
  106.7 11.8 %copy-start.21 = (f32[1,16,768]{2,1,0:T(8,128)S(1)}, f32[1,16,768]{2,1,0:T(8,128)}, u32[]{:S(2)}) copy-start(f32[1,16,768]{2,1,0:T(8,128)} %fusion.16) | copy-start | bytes 147460
  106.7 11.8 %copy-start.22 = (f32[1,16,768]{2,1,0:T(8,128)S(1)}, f32[1,16,768]{2,1,0:T(8,128)}, u32[]{:S(2)}) copy-start(f32[1,16,768]{2,1,0:T(8,128)} %fusion.17) | copy-start | bytes 147460
  106.7 12.8 %copy-start.14 = (f32[1,16,2048]{2,1,0:T(8,128)S(1)}, f32[1,16,2048]{2,1,0:T(8,128)}, u32[]{:S(2)}) copy-start(f32[1,16,2048]{2,1,0:T(8,128)} %fusion.8) | copy-start | bytes 393220
  114.8 129.7 %all-to-all-start.1 = ((bf16[16,16,2048]{2,1,0:T(8,128)(2,1)}), bf16[16,16,2048]{2,1,0:T(8,128)(2,1)S(1)}, u32[]{:S(2)}, u32[]{:S(2)}) async-start(bf16[16,16,2048]{2,1,0:T(8,128)(2,1)} %bitcast.21), calls=%async_computation.1 | async-start | bytes 2097152 | tf_op jit(solution)/shard_map/all_to_all | solution.py:202
  118.4 106.1 %all-reduce.7.cloned.1.call-start = ((), (), s32[]{:S(2)}) async-start(), calls=%async_computation.6 | async-start | bytes 294912
  119.2 162.3 %reduce-scatter.3.cloned.1.call-start = ((), (), s32[]{:S(2)}) async-start(), calls=%async_computation.5 | async-start | bytes 417792 | tf_op jit(solution)/shard_map/reduce_scatter | solution.py:217
  254.4 2.0 copy-start.29
  254.4 2.0 copy-start.30
  254.4 2.0 copy-start.31
  254.4 2.0 copy-start.32
  254.4 2.1 copy-start.33
  254.4 2.1 copy-start.34
  254.4 2.1 copy-start.35
  254.4 2.1 copy-start.36
  254.4 27.1 %copy-start.1 = (bf16[1,16,2048]{2,1,0:T(8,128)(2,1)S(1)}, bf16[1,16,2048]{2,1,0:T(8,128)(2,1)}, u32[]{:S(2)}) copy-start(bf16[1,16,2048]{2,1,0:T(8,128)(2,1)} %param.25) | copy-start | bytes 196612
Sparse Core Ops, SparseCore 0:
  122.2 102.2 all-reduce.6
  227.7 53.7 reduce-scatter.2
where the time goes:
time: 293 us; the launch traced here: 288 us
  waiting for transfers between devices  144 us (49%)
  local copies, waits for them, and re-layouts  45.8 us (16%)
  other arithmetic  35 us (12%)
  matrix products  26.2 us (9%)
  starting transfers between devices  22.8 us (8%)
  between operations  14.7 us (5%)
    unnamed x3, waiting for transfers between devices  104 us
    reduce_scatter x1, waiting for transfers between devices, shards(): lax.psum_scatter(grad_wide, 'dp', scatter_dimension=2, tiled=True)  21.9 us
    convert_element_type x6, other arithmetic, dequantize(): (levels.astype(jnp.float32) * jnp.repeat(scales, GROUP, axis=0)).astype(j...  18.3 us
    gather x8, local copies, waits for them, and re-layouts, shards(): input_grad = input_grad + back_pad[column_slot].astype(jnp.float32)  13.3 us
    gather x8, local copies, waits for them, and re-layouts, shards(): output_pad[column_slot].astype(jnp.float32)  11.8 us
    dot_general x9, matrix products, product_result(): jnp.dot(left_operand, right_operand, preferred_element_type=jnp.float32)  11.4 us
    all_to_all x1, waiting for transfers between devices, shards(): lax.all_to_all(send_grad, 'expert', split_axis=0, concat_axis=0, tiled=True)  11.2 us
    dot_general x9, matrix products, matrix_product(): lax.dot_general(left_operand, right_operand, (((1,), (1,)), ((), ())), pr...  7.66 us
  transfers between devices with their start and end apart: 6, of which 4 were waited for; matrix products, arithmetic and copies ran while one was open for 28% of the time, Pallas kernels for 0%

commit v1 on v0

v1 whole, which is shorter than its diff:
```python
import jax
import jax.numpy as jnp
from jax import lax
from jax.experimental import pallas as pl
from jax.experimental.pallas import tpu as pltpu
from jax.sharding import PartitionSpec as P

GROUP = 128
CAP = 16
SCALING = 0.5
BF = jnp.bfloat16
F32 = jnp.float32
VMEM = pl.BlockSpec(memory_space=pltpu.VMEM)
SMEM = pl.BlockSpec(memory_space=pltpu.SMEM)
LIMIT = 48 * 1024 * 1024


def nn(a, b):
    return lax.dot_general(a, b, (((1,), (0,)), ((), ())), preferred_element_type=F32)


def nt(a, b):
    return lax.dot_general(a, b, (((1,), (1,)), ((), ())), preferred_element_type=F32)


def tn(a, b):
    return lax.dot_general(a, b, (((0,), (0,)), ((), ())), preferred_element_type=F32)


def params(cost=None):
    return pltpu.CompilerParams(vmem_limit_bytes=LIMIT)


def cost(flops, bytes_accessed):
    return pl.CostEstimate(flops=flops, bytes_accessed=bytes_accessed, transcendentals=0)


def slot_tables(routes, gates, experts):
    tokens, top = routes.shape
    routes_t = routes.astype(F32).T
    gates_t = gates.T
    column = lax.broadcasted_iota(jnp.int32, (experts, tokens), 0).astype(F32)
    named = jnp.zeros((experts, tokens), F32)
    weight = jnp.zeros((experts, tokens), F32)
    for k in range(top):
        hit = routes_t[k : k + 1, :] == column
        named = named + jnp.where(hit, 1.0, 0.0)
        weight = weight + jnp.where(hit, gates_t[k : k + 1, :], 0.0)
    earlier = lax.broadcasted_iota(jnp.int32, (tokens, tokens), 0)
    later = lax.broadcasted_iota(jnp.int32, (tokens, tokens), 1)
    before = jnp.where(earlier < later, 1.0, 0.0).astype(BF)
    place = nn(named.astype(BF), before)
    place = jnp.where(named > 0.0, place, -1.0)
    slot = lax.broadcasted_iota(jnp.int32, (experts, CAP, tokens), 1).astype(F32)
    taken = place[:, None, :] == slot
    one = jnp.where(taken, 1.0, 0.0).reshape(experts * CAP, tokens)
    gate = jnp.where(taken, weight[:, None, :], 0.0).reshape(experts * CAP, tokens)
    return one, gate


def dispatch_kernel(routes_ref, gates_ref, act_ref, up_ref, send_ref):
    experts = send_ref.shape[0]
    width = act_ref.shape[1]
    one, gate = slot_tables(routes_ref[...], gates_ref[...], experts)
    one = one.astype(BF)
    weight = jnp.sum(gate, axis=1, keepdims=True)
    step = 512
    for lo in range(0, width, step):
        cols = slice(lo, lo + step)
        send_ref[:, :CAP, cols] = nn(one, act_ref[:, cols]).astype(BF).reshape(experts, CAP, step)
        picked = weight * nn(one, up_ref[:, cols])
        send_ref[:, CAP:, cols] = picked.astype(BF).reshape(experts, CAP, step)


def dispatch(routes, gates, activations, upstream, experts):
    width = activations.shape[1]
    return pl.pallas_call(
        dispatch_kernel,
        out_shape=jax.ShapeDtypeStruct((experts, 2 * CAP, width), BF),
        in_specs=[VMEM] * 4,
        out_specs=VMEM,
        compiler_params=params(),
        name="dispatch",
    )(routes, gates, activations, upstream)


def tables_kernel(routes_ref, gates_ref, one_ref, high_ref, low_ref):
    experts = one_ref.shape[0] // CAP
    one, gate = slot_tables(routes_ref[...], gates_ref[...], experts)
    high = gate.astype(BF)
    one_ref[...] = one.astype(BF)
    high_ref[...] = high
    low_ref[...] = (gate - high.astype(F32)).astype(BF)


def tables(routes, gates, experts):
    shape = jax.ShapeDtypeStruct((experts * CAP, routes.shape[0]), BF)
    return pl.pallas_call(
        tables_kernel,
        out_shape=(shape, shape, shape),
        in_specs=[VMEM] * 2,
        out_specs=(VMEM,) * 3,
        compiler_params=params(),
        name="tables",
    )(routes, gates)


def combine_kernel(got_ref, one_ref, high_ref, low_ref, mixed_ref, grad_ref):
    experts = got_ref.shape[0]
    width = got_ref.shape[2]
    one = one_ref[...]
    high = high_ref[...]
    low = low_ref[...]
    step = 512
    for lo in range(0, width, step):
        cols = slice(lo, lo + step)
        out = got_ref[:, :CAP, cols].reshape(experts * CAP, step)
        back = got_ref[:, CAP:, cols].reshape(experts * CAP, step)
        mixed_ref[:, cols] = (tn(high, out) + tn(low, out)).astype(BF)
        grad_ref[:, cols] = tn(one, back).astype(BF)


def combine(got, one, high, low):
    shape = jax.ShapeDtypeStruct((one.shape[1], got.shape[2]), BF)
    return pl.pallas_call(
        combine_kernel,
        out_shape=(shape, shape),
        in_specs=[VMEM] * 4,
        out_specs=(VMEM,) * 2,
        compiler_params=params(),
        name="combine",
    )(got, one, high, low)


def dequantize_kernel(levels_ref, scales_ref, frozen_ref):
    group = pl.program_id(0)
    per_step = levels_ref.shape[0] // GROUP
    for i in range(per_step):
        rows = slice(i * GROUP, (i + 1) * GROUP)
        scale = scales_ref[pl.ds(group * per_step + i, 1), :]
        frozen_ref[rows, :] = (levels_ref[rows, :].astype(F32) * scale).astype(BF)


def dequantize(levels, scales, per_step):
    rows, columns = levels.shape
    block = pl.BlockSpec((per_step * GROUP, columns), lambda i: (i, 0))
    return pl.pallas_call(
        dequantize_kernel,
        grid=(rows // (per_step * GROUP),),
        out_shape=jax.ShapeDtypeStruct(levels.shape, BF),
        in_specs=[block, pl.BlockSpec(scales.shape, lambda i: (0, 0))],
        out_specs=block,
        compiler_params=params(),
        cost_estimate=cost(levels.size, levels.size * 4),
        name="dequantize",
    )(levels, scales)


def expert_kernel(
    got_ref, gate_ref, up_ref, down_ref, first_ref, gate_second_ref, up_second_ref, down_first_ref,
    down_second_ref, send_ref, hidden_ref, d_gate_ref, d_up_ref, low_ref,
):
    experts, _, width = got_ref.shape
    rows = experts * CAP
    inner = gate_ref.shape[1]
    step = 256
    x = got_ref[:, :CAP, :].reshape(rows, width)
    g = got_ref[:, CAP:, :].reshape(rows, width)
    first_low = nt(x, first_ref[...]).astype(BF)
    rank = first_low.shape[1] // 2
    gate_low, up_low = first_low[:, :rank], first_low[:, rank:]
    back_down = nt(g, down_second_ref[...]).astype(BF)
    half = jnp.asarray(SCALING, BF)
    down_low = jnp.zeros((rows, rank), F32)
    back_gate = jnp.zeros((rows, rank), F32)
    back_up = jnp.zeros((rows, rank), F32)
    for lo in range(0, inner, step):
        cols = slice(lo, lo + step)
        gate_pre = nn(x, gate_ref[:, cols]) + nn(gate_low * half, gate_second_ref[:, cols])
        up_pre = nn(x, up_ref[:, cols]) + nn(up_low * half, up_second_ref[:, cols])
        d_hidden = nt(g, down_ref[cols, :]) + nn(back_down * half, down_first_ref[:, cols])
        logistic = jax.nn.sigmoid(gate_pre)
        activated = gate_pre * logistic
        hidden = (activated * up_pre).astype(BF)
        d_gate = (d_hidden * up_pre * logistic * (1.0 + gate_pre * (1.0 - logistic))).astype(BF)
        d_up = (d_hidden * activated).astype(BF)
        hidden_ref[:, cols] = hidden
        d_gate_ref[:, cols] = d_gate
        d_up_ref[:, cols] = d_up
        down_low += nt(hidden, down_first_ref[:, cols])
        back_gate += nt(d_gate, gate_second_ref[:, cols])
        back_up += nt(d_up, up_second_ref[:, cols])
    down_low = down_low.astype(BF)
    back_both = jnp.concatenate([back_gate, back_up], axis=1).astype(BF)
    low_ref[...] = jnp.concatenate([first_low, back_down, down_low, back_both], axis=1)
    hidden = hidden_ref[...]
    d_gate = d_gate_ref[...]
    d_up = d_up_ref[...]
    for lo in range(0, width, step):
        cols = slice(lo, lo + step)
        out = nn(hidden, down_ref[:, cols]) + nn(down_low * half, down_second_ref[:, cols])
        send_ref[:, :CAP, cols] = out.astype(BF).reshape(experts, CAP, step)
        back = nt(d_gate, gate_ref[cols, :]) + nt(d_up, up_ref[cols, :])
        back = back + nn(back_both * half, first_ref[:, cols])
        send_ref[:, CAP:, cols] = back.astype(BF).reshape(experts, CAP, step)


def expert(got, gate, up, down, first, gate_second, up_second, down_first, down_second):
    rows = got.shape[0] * CAP
    inner = gate.shape[1]
    wide = jax.ShapeDtypeStruct((rows, inner), BF)
    return pl.pallas_call(
        expert_kernel,
        out_shape=(
            jax.ShapeDtypeStruct(got.shape, BF), wide, wide, wide,
            jax.ShapeDtypeStruct((rows, 6 * gate_second.shape[0]), BF),
        ),
        in_specs=[VMEM] * 9,
        out_specs=(VMEM,) * 5,
        compiler_params=params(),
        name="expert",
    )(got, gate, up, down, first, gate_second, up_second, down_first, down_second)


def grads_kernel(group_ref, got_ref, hidden_ref, d_gate_ref, d_up_ref, low_ref, keep_ref, send_ref, piece_ref):
    experts, _, width = got_ref.shape
    rows = experts * CAP
    groups = piece_ref.shape[0]
    inner = hidden_ref.shape[1]
    rank = low_ref.shape[1] // 6
    low = low_ref[...]
    gate_low, up_low, back_down, down_low = (low[:, i * rank : (i + 1) * rank] for i in range(4))
    back_both = low[:, 4 * rank :]
    column = width // groups
    step = 512
    for lo in range(0, width, step):
        cols = slice(lo, lo + step)
        x = got_ref[:, :CAP, cols].reshape(rows, step)
        g = got_ref[:, CAP:, cols].reshape(rows, step)
        both = SCALING * tn(back_both, x)
        down = SCALING * tn(down_low, g)
        for i in range(step // column):
            piece = lo // column + i
            part = slice(i * column, (i + 1) * column)
            piece_ref[piece, : 2 * rank, :] = both[:, part]
            piece_ref[piece, 2 * rank : 3 * rank, :] = down[:, part]
    source = lax.broadcasted_iota(jnp.int32, (rank, 8 * rank), 0)
    target = lax.broadcasted_iota(jnp.int32, (rank, 8 * rank), 1)
    narrow = jnp.zeros((8 * rank, inner), F32)
    for i, (left, right) in enumerate(((gate_low, d_gate_ref), (up_low, d_up_ref), (back_down, hidden_ref))):
        spread = jnp.where(target == 8 * source + i, 1.0, 0.0).astype(BF)
        narrow += tn(nn(left, spread).astype(BF), right[...])
    narrow = SCALING * narrow
    for piece in range(groups):
        for i in range(inner // column):
            at = 3 * rank + 8 * i
            piece_ref[piece, at : at + 8, :] = narrow[8 * piece : 8 * piece + 8, i * column : (i + 1) * column]
    group = group_ref[0]
    side = group % 2
    plane = group // 2
    for place in range(groups // 2):
        turned = (place & 1) * 4 + (place & 2) + (place >> 2)
        other = lax.bitwise_xor(plane, jnp.int32(turned))
        keep_ref[place] = piece_ref[2 * other + side]
        send_ref[place] = piece_ref[2 * other + 1 - side]


def adapter_grads(group, got, hidden, d_gate, d_up, low, groups):
    width = got.shape[2]
    inner = hidden.shape[1]
    rank = low.shape[1] // 6
    column = width // groups
    height = 3 * rank + 8 * (inner // column)
    shape = jax.ShapeDtypeStruct((groups // 2, height, column), F32)
    return pl.pallas_call(
        grads_kernel,
        out_shape=(shape, shape),
        in_specs=[SMEM] + [VMEM] * 5,
        out_specs=(VMEM,) * 2,
        scratch_shapes=[pltpu.VMEM((groups, height, column), F32)],
        compiler_params=params(),
        name="adapter_grads",
    )(group, got, hidden, d_gate, d_up, low)


def shards(
    activations, routes, gates, gate_levels, gate_scales, up_levels, up_scales, down_levels, down_scales,
    gate_adapter_first, gate_adapter_second, up_adapter_first, up_adapter_second,
    down_adapter_first, down_adapter_second, upstream,
):
    experts = lax.axis_size("expert")
    groups = lax.axis_size("dp")
    width = activations.shape[1]
    inner = gate_levels.shape[2]
    rank = gate_adapter_first.shape[1]

    send = dispatch(routes, gates, activations, upstream, experts)
    got = lax.all_to_all(send, "expert", split_axis=0, concat_axis=0, tiled=True)

    gate = dequantize(gate_levels[0], gate_scales[0], 4)
    up = dequantize(up_levels[0], up_scales[0], 4)
    down = dequantize(down_levels[0], down_scales[0], 2)
    first = jnp.concatenate([gate_adapter_first[0], up_adapter_first[0]], axis=0)
    one, high, low_part = tables(routes, gates, experts)

    send, hidden, d_gate, d_up, low = expert(
        got, gate, up, down, first, gate_adapter_second[0], up_adapter_second[0],
        down_adapter_first[0], down_adapter_second[0],
    )
    back = lax.all_to_all(send, "expert", split_axis=0, concat_axis=0, tiled=True)

    group = lax.axis_index("dp").astype(jnp.int32).reshape(1)
    keep, other = adapter_grads(group, got, hidden, d_gate, d_up, low, groups)
    total = keep + lax.ppermute(other, "dp", [(i, i ^ 1) for i in range(groups)])
    mask = 2
    while total.shape[0] > 1:
        half = total.shape[0] // 2
        total = total[:half] + lax.ppermute(total[half:], "dp", [(i, i ^ mask) for i in range(groups)])
        mask *= 2
    column = width // groups
    grad_wide = total[0, : 3 * rank].reshape(1, 3, rank, column)
    narrow = total[0, 3 * rank :].reshape(inner // column, 8, column)[:, :3]
    grad_narrow = narrow.transpose(1, 0, 2).reshape(1, 3, 1, inner)

    mixed, input_grad = combine(back, one, high, low_part)
    return mixed, input_grad, grad_wide, grad_narrow


def solution(mesh):
    rows = P(("dp", "expert"), None)
    weight = P("expert", None, None)
    return jax.shard_map(
        shards,
        mesh=mesh,
        in_specs=(rows,) * 3 + (weight,) * 12 + (rows,),
        out_specs=(rows, rows, P("expert", None, None, "dp"), P("expert", None, "dp", None)),
        check_vma=False,
    )
```

time: 293 us -> 99.2 us (0.34); the launches traced: 288 us -> 98.3 us
  waiting for transfers between devices: 144 us -> 35.8 us
  other arithmetic: 35 us -> 0.09 us
  local copies, waits for them, and re-layouts: 45.8 us -> 16.2 us
  matrix products: 26.2 us -> 0 us
  Pallas kernels: 0 us -> 25.1 us
  between operations: 14.7 us -> 0.84 us
    unnamed x3 -> x0, waiting for transfers between devices: 104 us -> none
    gather x18 -> x0, local copies, waits for them, and re-layouts: 28.7 us -> none  [the longest x8 13.3 us: shards(): input_grad = input_grad + back_pad[column_slot].astype(jnp.float32)]
    dot_general x24 -> x0, matrix products: 26.2 us -> none  [the longest x9 11.4 us: product_result(): jnp.dot(left_operand, right_operand, preferred_element_type=jnp.float32)]
    convert_element_type x10 -> x0, other arithmetic: 26 us -> none  [the longest x6 18.3 us: dequantize(): (levels.astype(jnp.float32) * jnp.repeat(scales, GROUP, axis=0)).astype(j...]
    pallas_call x0 -> x8, Pallas kernels: none -> 25.1 us  [the longest x1 11.1 us: expert(): pl.pallas_call(expert_kernel, out_shape=(jax.ShapeDtypeStruct(got.shape,...]
    reduce_scatter x1 -> x0, waiting for transfers between devices: 21.9 us -> none  [shards(): lax.psum_scatter(grad_wide, 'dp', scatter_dimension=2, tiled=True)]
    ppermute x0 -> x4, waiting for transfers between devices: none -> 15.1 us  [the longest x3 13.4 us: shards(): lax.ppermute(total[half:], 'dp', [(i, i ^ mask) for i in range(groups)])]
    unnamed x80 -> x39, local copies, waits for them, and re-layouts: 2.32 us -> 15 us
  transfers between devices with their start and end apart: 6 -> 6, of which waited for: 4 -> 6; matrix products, arithmetic and copies ran while one was open for 28% -> 1% of each run, Pallas kernels for 0% -> 10%
where the time goes in v1:
time: 99.2 us; the launch traced here: 98.3 us
  waiting for transfers between devices  35.8 us (36%)
  Pallas kernels  25.1 us (25%)
  starting transfers between devices  20.2 us (20%)
  local copies, waits for them, and re-layouts  16.2 us (16%)
    all_to_all x2, waiting for transfers between devices, shards(): lax.all_to_all(send, 'expert', split_axis=0, concat_axis=0, tiled=True)  20.7 us
    unnamed x39, local copies, waits for them, and re-layouts  15 us
    ppermute x3, waiting for transfers between devices, shards(): lax.ppermute(total[half:], 'dp', [(i, i ^ mask) for i in range(groups)])  13.4 us
    all_to_all x2, starting transfers between devices, shards(): lax.all_to_all(send, 'expert', split_axis=0, concat_axis=0, tiled=True)  11.6 us
    pallas_call x1, Pallas kernels, expert(): pl.pallas_call(expert_kernel, out_shape=(jax.ShapeDtypeStruct(got.shape,...  11.1 us
    pallas_call x3, Pallas kernels, dequantize(): pl.pallas_call(dequantize_kernel, grid=(rows // (per_step * GROUP),), out...  8.62 us
    ppermute x3, starting transfers between devices, shards(): lax.ppermute(total[half:], 'dp', [(i, i ^ mask) for i in range(groups)])  8.52 us
    pallas_call x1, Pallas kernels, combine(): pl.pallas_call(combine_kernel, out_shape=(shape, shape), in_specs=[VMEM]...  3.13 us
  transfers between devices with their start and end apart: 6, of which 6 were waited for; matrix products, arithmetic and copies ran while one was open for 1% of the time, Pallas kernels for 10%

profile of v1, /device:TPU:32, one launch (start us, length us, event | category | flops | bytes accessed | tf_op | source)
XLA Modules:
  0.0 98.3 jit_solution(7859735350292303618)
XLA Ops:
  0.6 0.8 copy.20.routes_ref
  1.4 0.8 copy.21.gates_ref
  2.2 0.0 copy-start.5
  2.2 1.0 %copy-done.5 = bf16[128,2048]{1,0:T(8,128)(2,1)S(1)} copy-done((bf16[128,2048]{1,0:T(8,128)(2,1)S(1)}, bf16[128,2048]{1,0:T(8,128)(2,1)}, u32[]{:S(2)}) %copy-start.5) | copy-done | bytes 524312
  3.2 0.0 copy-start.6
  3.2 1.0 %copy-done.6 = bf16[128,2048]{1,0:T(8,128)(2,1)S(1)} copy-done((bf16[128,2048]{1,0:T(8,128)(2,1)S(1)}, bf16[128,2048]{1,0:T(8,128)(2,1)}, u32[]{:S(2)}) %copy-start.6) | copy-done | bytes 524312
  4.3 0.0 copy-start.17
  4.3 0.9 dispatch.1
  5.2 0.0 copy-start.3
  5.2 1.3 %copy-done.3 = bf16[16,32,2048]{2,1,0:T(8,128)(2,1)} copy-done((bf16[16,32,2048]{2,1,0:T(8,128)(2,1)}, bf16[16,32,2048]{2,1,0:T(8,128)(2,1)S(1)}, u32[]{:S(2)}) %copy-start.3) | copy-done | bytes 2097176
  6.5 7.0 %all-to-all-start = ((bf16[16,32,2048]{2,1,0:T(8,128)(2,1)}), bf16[16,32,2048]{2,1,0:T(8,128)(2,1)S(1)}, u32[]{:S(2)}, u32[]{:S(2)}) async-start(bf16[16,32,2048]{2,1,0:T(8,128)(2,1)} %copy-done.3), calls=%async_computation | async-start | bytes 4194304 | tf_op jit(solution)/shard_map/all_to_all | solution.py:298
  13.6 0.0 copy-done.17
  13.6 0.0 copy-start.10
  13.6 2.9 %dequantize.5.down_ref = bf16[768,2048]{1,0:T(8,128)(2,1)S(1)} custom-call(bf16[768,2048]{1,0:T(8,128)(2,1)} %bitcast.27, f32[6,2048]{1,0:T(8,128)S(1)} %bitcast.20), custom_call_target="tpu_custom_call" | custom-call | flops 1572864 | bytes 6291456 | tf_op jit(solution)/shard_map/dequantize/pallas_call | solution.py:147
  16.5 0.0 copy-start
  16.5 1.7 %copy-done = bf16[768,2048]{1,0:T(8,128)(2,1)} copy-done((bf16[768,2048]{1,0:T(8,128)(2,1)}, bf16[768,2048]{1,0:T(8,128)(2,1)S(1)}, u32[]{:S(2)}) %copy-start) | copy-done | bytes 3145752
  18.2 0.0 copy-done.10
  18.2 0.0 copy-start.11
  18.2 2.9 %dequantize.3.gate_ref = bf16[2048,768]{1,0:T(8,128)(2,1)S(1)} custom-call(bf16[2048,768]{1,0:T(8,128)(2,1)} %bitcast.28, f32[16,768]{1,0:T(8,128)S(1)} %bitcast.22), custom_call_target="tpu_custom_call" | custom-call | flops 1572864 | bytes 6291456 | tf_op jit(solution)/shard_map/dequantize/pallas_call | solution.py:147
  21.1 0.0 copy-start.1
  21.1 1.6 %copy-done.1 = bf16[2048,768]{1,0:T(8,128)(2,1)} copy-done((bf16[2048,768]{1,0:T(8,128)(2,1)}, bf16[2048,768]{1,0:T(8,128)(2,1)S(1)}, u32[]{:S(2)}) %copy-start.1) | copy-done | bytes 3145752
  22.7 0.0 copy-done.11
  22.7 0.0 copy-start.15
  22.7 0.0 copy-start.16
  22.7 2.9 %dequantize.4.up_ref = bf16[2048,768]{1,0:T(8,128)(2,1)S(1)} custom-call(bf16[2048,768]{1,0:T(8,128)(2,1)} %bitcast.29, f32[16,768]{1,0:T(8,128)S(1)} %bitcast.23), custom_call_target="tpu_custom_call" | custom-call | flops 1572864 | bytes 6291456 | tf_op jit(solution)/shard_map/dequantize/pallas_call | solution.py:147
  25.6 0.0 copy-start.2
  25.6 1.7 %copy-done.2 = bf16[2048,768]{1,0:T(8,128)(2,1)} copy-done((bf16[2048,768]{1,0:T(8,128)(2,1)}, bf16[2048,768]{1,0:T(8,128)(2,1)S(1)}, u32[]{:S(2)}) %copy-start.2) | copy-done | bytes 3145752
  27.3 0.0 copy-done.15
  27.3 0.0 copy-done.16
  27.3 17.9 %all-to-all-done.got_ref = bf16[16,32,2048]{2,1,0:T(8,128)(2,1)S(1)} async-done(((bf16[16,32,2048]{2,1,0:T(8,128)(2,1)}), bf16[16,32,2048]{2,1,0:T(8,128)(2,1)S(1)}, u32[]{:S(2)}, u32[]{:S(2)}) %all-to-all-start) | async-done | bytes 2097184 | tf_op jit(solution)/shard_map/all_to_all | solution.py:298
  45.2 0.0 copy-start.7
  45.2 0.8 copy-done.7
  46.0 0.0 copy-start.12
  46.0 0.7 copy-done.12
  46.8 0.0 copy-start.13
  46.8 0.7 copy-done.13
  47.5 0.0 copy-start.14
  47.5 0.7 copy-done.14
  48.3 11.1 %expert.1 = (bf16[16,32,2048]{2,1,0:T(8,128)(2,1)S(1)}, bf16[256,768]{1,0:T(8,128)(2,1)S(1)}, bf16[256,768]{1,0:T(8,128)(2,1)S(1)}, bf16[256,768]{1,0:T(8,128)(2,1)S(1)}, bf16[256,96]{1,0:T(8,128)(2,1)S(1)}) custom-call(bf16[16,32,2048]{2,1,0:T(8,128)(2,1)S(1)} %all-to-all-done.got_ref, bf16[2048,768]{1,0:T(8,128)(2,1)} %copy-done.1, ...), custom_call_target="tpu_custom_call" | custom-call | tf_op jit(solution)/shard_map/expert/pallas_call | solution.py:212
  59.3 0.0 copy-start.4
  59.3 1.3 %copy-done.4 = bf16[16,32,2048]{2,1,0:T(8,128)(2,1)} copy-done((bf16[16,32,2048]{2,1,0:T(8,128)(2,1)}, bf16[16,32,2048]{2,1,0:T(8,128)(2,1)S(1)}, u32[]{:S(2)}) %copy-start.4) | copy-done | bytes 2097176
  60.6 0.0 copy-start.8
  60.6 0.6 copy-done.8
  61.3 0.0 copy-start.9
  61.3 4.6 %all-to-all-start.1 = ((bf16[16,32,2048]{2,1,0:T(8,128)(2,1)}), bf16[16,32,2048]{2,1,0:T(8,128)(2,1)}, u32[]{:S(2)}, u32[]{:S(2)}) async-start(bf16[16,32,2048]{2,1,0:T(8,128)(2,1)} %copy-done.4), calls=%async_computation.1 | async-start | bytes 4194304 | tf_op jit(solution)/shard_map/all_to_all | solution.py:310
  65.8 0.0 copy-done.9
  65.9 1.2 %adapter_grads.1 = (f32[8,96,128]{2,1,0:T(8,128)S(1)}, f32[8,96,128]{2,1,0:T(8,128)S(1)}) custom-call(s32[1]{0:T(128)} %bitcast.11.group_ref, bf16[16,32,2048]{2,1,0:T(8,128)(2,1)S(1)} %all-to-all-done.got_ref, bf16[256,768]{1,0:T(8,128)(2,1)S(1)} %get-tuple-element.22.hidden_ref, bf16[256,768]{1,0:T(8,128)(2,1)S(1)} %get-tuple-element.23.d_gate_ref, ...), custom_call_target="tpu_custom_call" | custom-call | tf_op jit(solution)/shard_map/adapter_grads/pallas_call | solution.py:275
  67.1 0.1 collective-permute-start
  67.2 1.7 %collective-permute-done = f32[8,96,128]{2,1,0:T(8,128)S(1)} collective-permute-done((f32[8,96,128]{2,1,0:T(8,128)S(1)}, f32[8,96,128]{2,1,0:T(8,128)S(1)}, u32[]{:S(2)}, u32[]{:S(2)}) %collective-permute-start) | collective-permute-done | bytes 393248 | tf_op jit(solution)/shard_map/ppermute | solution.py:314
  68.9 0.2 collective-permute-start.1
  69.1 6.8 %collective-permute-done.1 = f32[4,96,128]{2,1,0:T(8,128)S(1)} collective-permute-done((f32[4,96,128]{2,1,0:T(8,128)S(1)}, f32[4,96,128]{2,1,0:T(8,128)S(1)}, u32[]{:S(2)}, u32[]{:S(2)}) %collective-permute-start.1) | collective-permute-done | bytes 196640 | tf_op jit(solution)/shard_map/ppermute | solution.py:318
  76.0 3.4 %collective-permute-start.2 = (f32[2,96,128]{2,1,0:T(8,128)S(1)}, f32[2,96,128]{2,1,0:T(8,128)S(1)}, u32[]{:S(2)}, u32[]{:S(2)}) collective-permute-start(f32[2,96,128]{2,1,0:T(8,128)S(1)} %slice.39), channel_id=1, source_target_pairs={{0,64},{16,80},{32,96},{48,112},{64,0},{80,16},{96,32},{112,48},{1... | collective-permute-start | bytes 294920 | tf_op jit(solution)/shard_map/ppermute | solution.py:318
  79.4 3.7 %collective-permute-done.2 = f32[2,96,128]{2,1,0:T(8,128)S(1)} collective-permute-done((f32[2,96,128]{2,1,0:T(8,128)S(1)}, f32[2,96,128]{2,1,0:T(8,128)S(1)}, u32[]{:S(2)}, u32[]{:S(2)}) %collective-permute-start.2) | collective-permute-done | bytes 98336 | tf_op jit(solution)/shard_map/ppermute | solution.py:318
  83.1 5.0 %collective-permute-start.3 = (f32[1,96,128]{2,1,0:T(8,128)S(1)}, f32[1,96,128]{2,1,0:T(8,128)S(1)}, u32[]{:S(2)}, u32[]{:S(2)}) collective-permute-start(f32[1,96,128]{2,1,0:T(8,128)S(1)} %slice.41), channel_id=1, source_target_pairs={{0,128},{16,144},{32,160},{48,176},{64,192},{80,208},{96,224},{112... | collective-permute-start | bytes 147464 | tf_op jit(solution)/shard_map/ppermute | solution.py:318
  88.0 0.2 tables.1
  88.3 2.9 %collective-permute-done.3 = f32[1,96,128]{2,1,0:T(8,128)S(1)} collective-permute-done((f32[1,96,128]{2,1,0:T(8,128)S(1)}, f32[1,96,128]{2,1,0:T(8,128)S(1)}, u32[]{:S(2)}, u32[]{:S(2)}) %collective-permute-start.3) | collective-permute-done | bytes 49184 | tf_op jit(solution)/shard_map/ppermute | solution.py:318
  91.2 0.6 slice_bitcast_fusion
  91.8 0.6 reshape.15
  92.4 2.8 %all-to-all-done.1.got_ref = bf16[16,32,2048]{2,1,0:T(8,128)(2,1)} async-done(((bf16[16,32,2048]{2,1,0:T(8,128)(2,1)}), bf16[16,32,2048]{2,1,0:T(8,128)(2,1)}, u32[]{:S(2)}, u32[]{:S(2)}) %all-to-all-start.1) | async-done | bytes 2097184 | tf_op jit(solution)/shard_map/all_to_all | solution.py:310
  95.2 3.1 %combine.1 = (bf16[128,2048]{1,0:T(8,128)(2,1)}, bf16[128,2048]{1,0:T(8,128)(2,1)}) custom-call(bf16[16,32,2048]{2,1,0:T(8,128)(2,1)} %all-to-all-done.1.got_ref, bf16[256,128]{1,0:T(8,128)(2,1)S(1)} %get-tuple-element.17.one_ref, bf16[256,128]{1,0:T(8,128)(2,1)S(1)} %get-tuple-element.18.high_ref, bf16[256,128]{1,0:T(8,128)(2,1)S(1)} %get-tuple-element.19.low_ref), custom_call_target="tpu_custom_call" | custom-call | tf_op jit(solution)/shard_map/combine/pallas_call | solution.py:125
  (11 shorter events, 0.2 us)
Async XLA Ops:
  2.2 1.0 %copy-start.5 = (bf16[128,2048]{1,0:T(8,128)(2,1)S(1)}, bf16[128,2048]{1,0:T(8,128)(2,1)}, u32[]{:S(2)}) copy-start(bf16[128,2048]{1,0:T(8,128)(2,1)} %act_ref.1) | copy-start | bytes 1572868
  3.2 1.0 %copy-start.6 = (bf16[128,2048]{1,0:T(8,128)(2,1)S(1)}, bf16[128,2048]{1,0:T(8,128)(2,1)}, u32[]{:S(2)}) copy-start(bf16[128,2048]{1,0:T(8,128)(2,1)} %up_ref.1) | copy-start | bytes 1572868
  4.3 9.3 %copy-start.17 = (f32[1,6,2048]{2,0,1:T(1,128)S(1)}, f32[1,6,2048]{2,0,1:T(1,128)}, u32[]{:S(2)}) copy-start(f32[1,6,2048]{2,0,1:T(1,128)} %param.24) | copy-start | bytes 147460
  5.2 1.3 %copy-start.3 = (bf16[16,32,2048]{2,1,0:T(8,128)(2,1)}, bf16[16,32,2048]{2,1,0:T(8,128)(2,1)S(1)}, u32[]{:S(2)}) copy-start(bf16[16,32,2048]{2,1,0:T(8,128)(2,1)S(1)} %dispatch.1) | copy-start | bytes 6291460
  6.5 38.7 %all-to-all-start = ((bf16[16,32,2048]{2,1,0:T(8,128)(2,1)}), bf16[16,32,2048]{2,1,0:T(8,128)(2,1)S(1)}, u32[]{:S(2)}, u32[]{:S(2)}) async-start(bf16[16,32,2048]{2,1,0:T(8,128)(2,1)} %copy-done.3), calls=%async_computation | async-start | bytes 4194304 | tf_op jit(solution)/shard_map/all_to_all | solution.py:298
  13.6 4.6 %copy-start.10 = (f32[1,16,768]{2,1,0:T(8,128)S(1)}, f32[1,16,768]{2,1,0:T(8,128)}, u32[]{:S(2)}) copy-start(f32[1,16,768]{2,1,0:T(8,128)} %param.20) | copy-start | bytes 147460
  16.5 1.7 %copy-start = (bf16[768,2048]{1,0:T(8,128)(2,1)}, bf16[768,2048]{1,0:T(8,128)(2,1)S(1)}, u32[]{:S(2)}) copy-start(bf16[768,2048]{1,0:T(8,128)(2,1)S(1)} %dequantize.5.down_ref) | copy-start | bytes 9437188
  18.2 4.5 %copy-start.11 = (f32[1,16,768]{2,1,0:T(8,128)S(1)}, f32[1,16,768]{2,1,0:T(8,128)}, u32[]{:S(2)}) copy-start(f32[1,16,768]{2,1,0:T(8,128)} %param.22) | copy-start | bytes 147460
  21.1 1.6 %copy-start.1 = (bf16[2048,768]{1,0:T(8,128)(2,1)}, bf16[2048,768]{1,0:T(8,128)(2,1)S(1)}, u32[]{:S(2)}) copy-start(bf16[2048,768]{1,0:T(8,128)(2,1)S(1)} %dequantize.3.gate_ref) | copy-start | bytes 9437188
  22.7 4.6 %copy-start.15 = (bf16[1,16,2048]{2,1,0:T(8,128)(2,1)S(1)}, bf16[1,16,2048]{2,1,0:T(8,128)(2,1)}, u32[]{:S(2)}) copy-start(bf16[1,16,2048]{2,1,0:T(8,128)(2,1)} %param.27) | copy-start | bytes 196612
  22.7 4.6 %copy-start.16 = (bf16[1,16,2048]{2,1,0:T(8,128)(2,1)S(1)}, bf16[1,16,2048]{2,1,0:T(8,128)(2,1)}, u32[]{:S(2)}) copy-start(bf16[1,16,2048]{2,1,0:T(8,128)(2,1)} %param.25) | copy-start | bytes 196612
  25.6 1.7 %copy-start.2 = (bf16[2048,768]{1,0:T(8,128)(2,1)}, bf16[2048,768]{1,0:T(8,128)(2,1)S(1)}, u32[]{:S(2)}) copy-start(bf16[2048,768]{1,0:T(8,128)(2,1)S(1)} %dequantize.4.up_ref) | copy-start | bytes 9437188
  45.2 0.8 copy-start.7
  46.0 0.7 copy-start.12
  46.8 0.7 copy-start.13
  47.5 0.7 copy-start.14
  59.3 1.3 %copy-start.4 = (bf16[16,32,2048]{2,1,0:T(8,128)(2,1)}, bf16[16,32,2048]{2,1,0:T(8,128)(2,1)S(1)}, u32[]{:S(2)}) copy-start(bf16[16,32,2048]{2,1,0:T(8,128)(2,1)S(1)} %get-tuple-element.16) | copy-start | bytes 6291460
  60.6 0.6 copy-start.8
  61.3 4.6 %copy-start.9 = (bf16[256,96]{1,0:T(8,128)(2,1)S(1)}, bf16[256,96]{1,0:T(8,128)(2,1)}, u32[]{:S(2)}) copy-start(bf16[256,96]{1,0:T(8,128)(2,1)} %copy-done.8) | copy-start | bytes 147460
  61.3 34.0 %all-to-all-start.1 = ((bf16[16,32,2048]{2,1,0:T(8,128)(2,1)}), bf16[16,32,2048]{2,1,0:T(8,128)(2,1)}, u32[]{:S(2)}, u32[]{:S(2)}) async-start(bf16[16,32,2048]{2,1,0:T(8,128)(2,1)} %copy-done.4), calls=%async_computation.1 | async-start | bytes 4194304 | tf_op jit(solution)/shard_map/all_to_all | solution.py:310
  67.1 1.8 %collective-permute-start = (f32[8,96,128]{2,1,0:T(8,128)S(1)}, f32[8,96,128]{2,1,0:T(8,128)S(1)}, u32[]{:S(2)}, u32[]{:S(2)}) collective-permute-start(f32[8,96,128]{2,1,0:T(8,128)S(1)} %get-tuple-element.27), channel_id=1, source_target_pairs={{0,16},{16,0},{32,48},{48,32},{64,80},{80,64},{96,112},{112,96},{1... | collective-permute-start | bytes 1179656 | tf_op jit(solution)/shard_map/ppermute | solution.py:314
  68.9 7.0 %collective-permute-start.1 = (f32[4,96,128]{2,1,0:T(8,128)S(1)}, f32[4,96,128]{2,1,0:T(8,128)S(1)}, u32[]{:S(2)}, u32[]{:S(2)}) collective-permute-start(f32[4,96,128]{2,1,0:T(8,128)S(1)} %slice.37), channel_id=1, source_target_pairs={{0,32},{16,48},{32,0},{48,16},{64,96},{80,112},{96,64},{112,80},{1... | collective-permute-start | bytes 589832 | tf_op jit(solution)/shard_map/ppermute | solution.py:318
  76.0 7.0 %collective-permute-start.2 = (f32[2,96,128]{2,1,0:T(8,128)S(1)}, f32[2,96,128]{2,1,0:T(8,128)S(1)}, u32[]{:S(2)}, u32[]{:S(2)}) collective-permute-start(f32[2,96,128]{2,1,0:T(8,128)S(1)} %slice.39), channel_id=1, source_target_pairs={{0,64},{16,80},{32,96},{48,112},{64,0},{80,16},{96,32},{112,48},{1... | collective-permute-start | bytes 294920 | tf_op jit(solution)/shard_map/ppermute | solution.py:318
  83.1 8.1 %collective-permute-start.3 = (f32[1,96,128]{2,1,0:T(8,128)S(1)}, f32[1,96,128]{2,1,0:T(8,128)S(1)}, u32[]{:S(2)}, u32[]{:S(2)}) collective-permute-start(f32[1,96,128]{2,1,0:T(8,128)S(1)} %slice.41), channel_id=1, source_target_pairs={{0,128},{16,144},{32,160},{48,176},{64,192},{80,208},{96,224},{112... | collective-permute-start | bytes 147464 | tf_op jit(solution)/shard_map/ppermute | solution.py:318

commit v2 on v1

v2 whole, which is shorter than its diff:
```python
import jax
import jax.numpy as jnp
from jax import lax
from jax.experimental import pallas as pl
from jax.experimental.pallas import tpu as pltpu
from jax.sharding import PartitionSpec as P

GROUP = 128
CAP = 16
SCALING = 0.5
BF = jnp.bfloat16
F32 = jnp.float32
VMEM = pl.BlockSpec(memory_space=pltpu.VMEM)
SMEM = pl.BlockSpec(memory_space=pltpu.SMEM)
HBM = pl.BlockSpec(memory_space=pltpu.HBM)
DMA = pltpu.SemaphoreType.DMA
SPLITS = {1280: 1280, 2048: 768}


def nn(a, b):
    return lax.dot_general(a, b, (((1,), (0,)), ((), ())), preferred_element_type=F32)


def nt(a, b):
    return lax.dot_general(a, b, (((1,), (1,)), ((), ())), preferred_element_type=F32)


def tn(a, b):
    return lax.dot_general(a, b, (((0,), (0,)), ((), ())), preferred_element_type=F32)


def params(mebibytes):
    return pltpu.CompilerParams(vmem_limit_bytes=mebibytes * 1024 * 1024)


def cost(flops, bytes_accessed):
    return pl.CostEstimate(flops=flops, bytes_accessed=bytes_accessed, transcendentals=0)


def in_vmem(array):
    return pltpu.with_memory_space_constraint(array, pltpu.VMEM)


def in_hbm(array):
    return pltpu.with_memory_space_constraint(array, pltpu.HBM)


def slot_tables(routes, gates_t, experts):
    top, tokens = routes.shape
    routes_t = routes.astype(F32)
    column = lax.broadcasted_iota(jnp.int32, (experts, tokens), 0).astype(F32)
    named = jnp.zeros((experts, tokens), F32)
    weight = jnp.zeros((experts, tokens), F32)
    for k in range(top):
        hit = routes_t[k : k + 1, :] == column
        named = named + jnp.where(hit, 1.0, 0.0)
        weight = weight + jnp.where(hit, gates_t[k : k + 1, :], 0.0)
    earlier = lax.broadcasted_iota(jnp.int32, (tokens, tokens), 0)
    later = lax.broadcasted_iota(jnp.int32, (tokens, tokens), 1)
    before = jnp.where(earlier < later, 1.0, 0.0).astype(BF)
    place = nn(named.astype(BF), before)
    place = jnp.where(named > 0.0, place, -1.0)
    slot = lax.broadcasted_iota(jnp.int32, (experts, CAP, tokens), 1).astype(F32)
    taken = place[:, None, :] == slot
    one = jnp.where(taken, 1.0, 0.0).reshape(experts * CAP, tokens)
    gate = jnp.where(taken, weight[:, None, :], 0.0).reshape(experts * CAP, tokens)
    return one, gate


def dispatch_kernel(
    routes_hbm, gates_hbm, act_hbm, up_hbm, send_hbm, routes_ref, gates_ref, act_ref, up_ref, send_ref, in_sem, out_sem
):
    experts = send_ref.shape[0]
    width = act_ref.shape[1]
    pairs = ((routes_hbm, routes_ref), (gates_hbm, gates_ref), (act_hbm, act_ref), (up_hbm, up_ref))
    loads = [pltpu.make_async_copy(source, target, in_sem.at[i]) for i, (source, target) in enumerate(pairs)]
    for load in loads:
        load.start()
    loads[0].wait()
    loads[1].wait()
    one, gate = slot_tables(routes_ref[...], gates_ref[...], experts)
    one = one.astype(BF)
    weight = jnp.sum(gate, axis=1, keepdims=True)
    loads[2].wait()
    loads[3].wait()
    step = 512
    stores = []
    for i, lo in enumerate(range(0, width, step)):
        cols = slice(lo, lo + step)
        send_ref[:, :CAP, cols] = nn(one, act_ref[:, cols]).astype(BF).reshape(experts, CAP, step)
        picked = weight * nn(one, up_ref[:, cols])
        send_ref[:, CAP:, cols] = picked.astype(BF).reshape(experts, CAP, step)
        store = pltpu.make_async_copy(send_ref.at[:, :, cols], send_hbm.at[:, :, cols], out_sem.at[i])
        store.start()
        stores.append(store)
    for store in stores:
        store.wait()


def dispatch(routes, gates, activations, upstream, experts):
    width = activations.shape[1]
    shape = (experts, 2 * CAP, width)
    return pl.pallas_call(
        dispatch_kernel,
        out_shape=pltpu.HBM(shape, BF),
        in_specs=[HBM] * 4,
        out_specs=HBM,
        scratch_shapes=[
            pltpu.VMEM(routes.shape, jnp.int32), pltpu.VMEM(gates.shape, F32), pltpu.VMEM(activations.shape, BF),
            pltpu.VMEM(upstream.shape, BF), pltpu.VMEM(shape, BF), DMA((4,)), DMA((4,)),
        ],
        compiler_params=params(12),
        name="dispatch",
    )(*(in_hbm(array) for array in (routes, gates, activations, upstream)))


def tables_kernel(routes_ref, gates_ref, table_ref):
    slots = table_ref.shape[2]
    one, gate = slot_tables(routes_ref[...], gates_ref[...], slots // CAP)
    one, gate = one.T, gate.T
    high = gate.astype(BF)
    table_ref[0] = one.astype(BF)
    table_ref[1] = high
    table_ref[2] = (gate - high.astype(F32)).astype(BF)


def tables(routes, gates, experts):
    return pl.pallas_call(
        tables_kernel,
        out_shape=jax.ShapeDtypeStruct((3, routes.shape[1], experts * CAP), BF),
        in_specs=[VMEM] * 2,
        out_specs=VMEM,
        compiler_params=params(4),
        name="tables",
    )(routes, gates)


def combine_kernel(got_ref, table_hbm, mixed_hbm, grad_hbm, table_ref, mixed_ref, grad_ref, in_sem, out_sem):
    load = pltpu.make_async_copy(table_hbm, table_ref, in_sem)
    load.start()
    experts = got_ref.shape[0]
    width = got_ref.shape[2]
    load.wait()
    one, high, low = table_ref[0], table_ref[1], table_ref[2]
    step = 512
    stores = []
    for i, lo in enumerate(range(0, width, step)):
        cols = slice(lo, lo + step)
        out = got_ref[:, :CAP, cols].reshape(experts * CAP, step)
        back = got_ref[:, CAP:, cols].reshape(experts * CAP, step)
        mixed_ref[:, cols] = (nn(high, out) + nn(low, out)).astype(BF)
        stores.append(pltpu.make_async_copy(mixed_ref.at[:, cols], mixed_hbm.at[:, cols], out_sem.at[0, i]))
        stores[-1].start()
        grad_ref[:, cols] = nn(one, back).astype(BF)
        stores.append(pltpu.make_async_copy(grad_ref.at[:, cols], grad_hbm.at[:, cols], out_sem.at[1, i]))
        stores[-1].start()
    for store in stores:
        store.wait()


def combine(got, table):
    shape = (table.shape[1], got.shape[2])
    return pl.pallas_call(
        combine_kernel,
        out_shape=(pltpu.HBM(shape, BF),) * 2,
        in_specs=[VMEM, HBM],
        out_specs=(HBM,) * 2,
        scratch_shapes=[pltpu.VMEM(table.shape, BF), pltpu.VMEM(shape, BF), pltpu.VMEM(shape, BF), DMA, DMA((2, 4))],
        compiler_params=params(8),
        name="combine",
    )(in_vmem(got), in_hbm(table))


def expert_kernel(
    group_ref, got_ref, gate_hbm, up_hbm, down_hbm, gate_scale_hbm, up_scale_hbm, down_scale_hbm, gate_first_hbm, up_first_hbm,
    down_second_hbm, gate_second_hbm, up_second_hbm, down_first_hbm, send_hbm, keep_hbm, other_hbm,
    gate_ref, up_ref, down_ref, gate_scale_ref, up_scale_ref, down_scale_ref, wide_ref, narrow_ref, send_ref,
    inside_ref, piece_ref, level_sem, small_sem, out_sem, piece_sem,
):
    experts, _, width = got_ref.shape
    rows = experts * CAP
    inner = gate_ref.shape[1]
    rank = gate_first_hbm.shape[0]
    step = 256

    pairs = [(source, wide_ref.at[i * rank : (i + 1) * rank, :])
             for i, source in enumerate((gate_first_hbm, up_first_hbm, down_second_hbm))]
    pairs += [(source, narrow_ref.at[i * rank : (i + 1) * rank, :])
              for i, source in enumerate((gate_second_hbm, up_second_hbm, down_first_hbm))]
    pairs += [(gate_scale_hbm, gate_scale_ref), (up_scale_hbm, up_scale_ref), (down_scale_hbm, down_scale_ref)]
    small = [pltpu.make_async_copy(source, target, small_sem.at[i]) for i, (source, target) in enumerate(pairs)]
    for copy in small:
        copy.start()
    weights = ((gate_hbm, gate_ref), (up_hbm, up_ref), (down_hbm, down_ref))
    pieces = [(part, kind) for part in range(inner // step) for kind in range(3)]
    levels = []
    for part, kind in pieces:
        cols = slice(part * step, (part + 1) * step)
        place = (cols, slice(0, width)) if kind == 2 else (slice(0, width), cols)
        source, target = weights[kind]
        levels.append(pltpu.make_async_copy(source.at[place], target.at[place], level_sem.at[part, kind]))
    for copy in levels[:3]:
        copy.start()
    def land(index):
        part, kind = pieces[index]
        if kind == 2:
            for i in range(part * step // GROUP, (part + 1) * step // GROUP):
                group = slice(i * GROUP, (i + 1) * GROUP)
                down_ref[group, :] = (down_ref[group, :].astype(F32) * down_scale_ref[i]).astype(BF)
        else:
            cols = slice(part * step, (part + 1) * step)
            target, scale_ref = ((gate_ref, gate_scale_ref), (up_ref, up_scale_ref))[kind]
            for i in range(width // GROUP):
                group = slice(i * GROUP, (i + 1) * GROUP)
                target[group, cols] = (target[group, cols].astype(F32) * scale_ref[i : i + 1, cols]).astype(BF)

    x = got_ref[:, :CAP, :].reshape(rows, width)
    g = got_ref[:, CAP:, :].reshape(rows, width)
    first_ref = wide_ref.at[: 2 * rank, :]
    down_second_ref = wide_ref.at[2 * rank :, :]
    gate_second_ref = narrow_ref.at[:rank, :]
    up_second_ref = narrow_ref.at[rank : 2 * rank, :]
    down_first_ref = narrow_ref.at[2 * rank :, :]
    for copy in small:
        copy.wait()
    for copy in levels[3:]:
        copy.start()
    first_low = nt(x, first_ref[...]).astype(BF)
    gate_low, up_low = first_low[:, :rank], first_low[:, rank:]
    back_down = nt(g, down_second_ref[...]).astype(BF)
    half = jnp.asarray(SCALING, BF)
    down_low = jnp.zeros((rows, rank), F32)
    back_gate = jnp.zeros((rows, rank), F32)
    back_up = jnp.zeros((rows, rank), F32)
    for index, (part, kind) in enumerate(pieces):
        if kind == 0:
            for copy in levels[index : index + 3]:
                copy.wait()
        land(index)
        cols = slice(part * step, (part + 1) * step)
        if kind == 0:
            gate_pre = nn(x, gate_ref[:, cols]) + nn(gate_low * half, gate_second_ref[:, cols])
            logistic = jax.nn.sigmoid(gate_pre)
            activated = gate_pre * logistic
            slope = logistic * (1.0 + gate_pre * (1.0 - logistic))
        elif kind == 1:
            up_pre = nn(x, up_ref[:, cols]) + nn(up_low * half, up_second_ref[:, cols])
            hidden = (activated * up_pre).astype(BF)
            inside_ref[0, :, cols] = hidden
            down_low += nt(hidden, down_first_ref[:, cols])
        else:
            d_hidden = nt(g, down_ref[cols, :]) + nn(back_down * half, down_first_ref[:, cols])
            d_gate = (d_hidden * up_pre * slope).astype(BF)
            d_up = (d_hidden * activated).astype(BF)
            inside_ref[1, :, cols] = d_gate
            inside_ref[2, :, cols] = d_up
            back_gate += nt(d_gate, gate_second_ref[:, cols])
            back_up += nt(d_up, up_second_ref[:, cols])
    down_low = down_low.astype(BF)
    back_both = jnp.concatenate([back_gate, back_up], axis=1).astype(BF)
    hidden, d_gate, d_up = inside_ref[0], inside_ref[1], inside_ref[2]
    stores = []
    for i, lo in enumerate(range(0, width, step)):
        cols = slice(lo, lo + step)
        out = nn(hidden, down_ref[:, cols]) + nn(down_low * half, down_second_ref[:, cols])
        send_ref[:, :CAP, cols] = out.astype(BF).reshape(experts, CAP, step)
        back = nt(d_gate, gate_ref[cols, :]) + nt(d_up, up_ref[cols, :])
        back = back + nn(back_both * half, first_ref[:, cols])
        send_ref[:, CAP:, cols] = back.astype(BF).reshape(experts, CAP, step)
        if lo + step in SPLITS:
            cols = slice(lo + step - SPLITS[lo + step], lo + step)
            stores.append(pltpu.make_async_copy(send_ref.at[:, :, cols], send_hbm.at[:, :, cols], out_sem.at[i]))
            stores[-1].start()
    groups = piece_ref.shape[0]
    column = width // groups
    for lo in range(0, width, 512):
        cols = slice(lo, lo + 512)
        both = SCALING * tn(back_both, got_ref[:, :CAP, cols].reshape(rows, 512))
        down = SCALING * tn(down_low, got_ref[:, CAP:, cols].reshape(rows, 512))
        for i in range(512 // column):
            part = slice(i * column, (i + 1) * column)
            piece_ref[lo // column + i, : 2 * rank, :] = both[:, part]
            piece_ref[lo // column + i, 2 * rank : 3 * rank, :] = down[:, part]
    source = lax.broadcasted_iota(jnp.int32, (rank, 8 * rank), 0)
    target = lax.broadcasted_iota(jnp.int32, (rank, 8 * rank), 1)
    narrow = jnp.zeros((8 * rank, inner), F32)
    for i, (left, right) in enumerate(((gate_low, d_gate), (up_low, d_up), (back_down, hidden))):
        spread = jnp.where(target == 8 * source + i, SCALING, 0.0).astype(BF)
        narrow += tn(nn(left, spread).astype(BF), right)
    for piece in range(groups):
        for i in range(inner // column):
            at = 3 * rank + 8 * i
            piece_ref[piece, at : at + 8, :] = narrow[8 * piece : 8 * piece + 8, i * column : (i + 1) * column]
    group = group_ref[0]
    side = group % 2
    plane = group // 2
    for place in range(groups // 2):
        turned = (place & 1) * 4 + (place & 2) + (place >> 2)
        other = lax.bitwise_xor(plane, jnp.int32(turned))
        for mine, out in ((side, keep_hbm), (1 - side, other_hbm)):
            stores.append(pltpu.make_async_copy(piece_ref.at[2 * other + mine], out.at[place], piece_sem.at[place, 0 if out is keep_hbm else 1]))
            stores[-1].start()
    for store in stores:
        store.wait()


def expert(group, groups, got, levels, scales, wide, narrow):
    rows = got.shape[0] * CAP
    width = got.shape[2]
    inner = levels[0].shape[1]
    rank = wide[0].shape[0]
    column = width // groups
    height = 3 * rank + 8 * (inner // column)
    part = (groups // 2, height, column)
    return pl.pallas_call(
        expert_kernel,
        out_shape=(pltpu.HBM(got.shape, BF), pltpu.HBM(part, F32), pltpu.HBM(part, F32)),
        in_specs=[SMEM, VMEM] + [HBM] * 12,
        out_specs=(HBM,) * 3,
        scratch_shapes=[
            *(pltpu.VMEM(level.shape, BF) for level in levels),
            *(pltpu.VMEM(scale.shape, F32) for scale in scales),
            pltpu.VMEM((3 * rank, width), BF), pltpu.VMEM((3 * rank, inner), BF),
            pltpu.VMEM(got.shape, BF), pltpu.VMEM((3, rows, inner), BF), pltpu.VMEM((groups, height, column), F32),
            DMA((inner // 256, 3)), DMA((9,)), DMA((width // 256,)), DMA((groups // 2, 2)),
        ],
        compiler_params=params(32),
        name="expert",
    )(group, in_vmem(got), *(in_hbm(array) for array in (*levels, *scales, *wide, *narrow)))


def shards(
    activations, routes, gates, gate_levels, gate_scales, up_levels, up_scales, down_levels, down_scales,
    gate_adapter_first, gate_adapter_second, up_adapter_first, up_adapter_second,
    down_adapter_first, down_adapter_second, upstream,
):
    experts = lax.axis_size("expert")
    groups = lax.axis_size("dp")
    width = activations.shape[1]
    inner = gate_levels.shape[2]
    rank = gate_adapter_first.shape[1]

    routes, gates = routes.T, gates.T
    group = lax.axis_index("dp").astype(jnp.int32).reshape(1)
    send, group = lax.optimization_barrier((dispatch(routes, gates, activations, upstream, experts), group))
    got = lax.all_to_all(send, "expert", split_axis=0, concat_axis=0, tiled=True)

    send, keep, other = expert(
        group,
        groups,
        got,
        (gate_levels[0], up_levels[0], down_levels[0]),
        (gate_scales[0], up_scales[0], down_scales.transpose(1, 0, 2)),
        (gate_adapter_first[0], up_adapter_first[0], down_adapter_second[0]),
        (gate_adapter_second[0], up_adapter_second[0], down_adapter_first[0]),
    )
    routes, gates, keep = lax.optimization_barrier((routes, gates, keep))
    table = tables(routes, gates, experts)
    back = lax.all_to_all(send, "expert", split_axis=0, concat_axis=0, tiled=True)

    def swap(part, mask):
        return lax.ppermute(part, "dp", [(i, i ^ mask) for i in range(groups)])

    total = keep + swap(other, 1)
    half = groups // 4
    total = total[:half] + swap(total[half:], 2)
    total = total[0] + (swap(total[1], 8) + swap(total[2], 4) + swap(total[3], 12))
    column = width // groups
    grad_wide = total[: 3 * rank].reshape(1, 3, rank, column)
    narrow = total[3 * rank :].reshape(inner // column, 8, column)[:, :3]
    grad_narrow = narrow.transpose(1, 0, 2).reshape(1, 3, 1, inner)

    mixed, input_grad = combine(back, table)
    return mixed, input_grad, grad_wide, grad_narrow


def solution(mesh):
    rows = P(("dp", "expert"), None)
    weight = P("expert", None, None)
    return jax.shard_map(
        shards,
        mesh=mesh,
        in_specs=(rows,) * 3 + (weight,) * 12 + (rows,),
        out_specs=(rows, rows, P("expert", None, None, "dp"), P("expert", None, "dp", None)),
        check_vma=False,
    )
```

time: 99.2 us -> 87.2 us (0.88)
  blocking collectives: 0 us -> 35.4 us
  waiting for transfers between devices: 35.8 us -> 19 us
  local copies, waits for them, and re-layouts: 16.2 us -> 1.94 us
  starting transfers between devices: 20.2 us -> 12 us
  Pallas kernels: 25.1 us -> 17.7 us
    all_to_all x0 -> x1, blocking collectives: none -> 35.4 us  [shards(): lax.all_to_all(send, 'expert', split_axis=0, concat_axis=0, tiled=True)]
    all_to_all x2 -> x1, waiting for transfers between devices: 20.7 us -> 5.23 us  [shards(): lax.all_to_all(send, 'expert', split_axis=0, concat_axis=0, tiled=True)]
    unnamed x39 -> x10, local copies, waits for them, and re-layouts: 15 us -> 0.68 us
    all_to_all x2 -> x1, starting transfers between devices: 11.6 us -> 3.86 us  [shards(): lax.all_to_all(send, 'expert', split_axis=0, concat_axis=0, tiled=True)]
    pallas_call x8 -> x4, Pallas kernels: 25.1 us -> 17.7 us  [the longest x1 12.3 us: expert(): pl.pallas_call(expert_kernel, out_shape=(pltpu.HBM(got.shape, BF), pltpu....]
    ppermute x4 -> x5, waiting for transfers between devices: 15.1 us -> 13.8 us  [swap(): return lax.ppermute(part, 'dp', [(i, i ^ mask) for i in range(groups)])]
    ppermute x4 -> x5, starting transfers between devices: 8.61 us -> 8.14 us  [swap(): return lax.ppermute(part, 'dp', [(i, i ^ mask) for i in range(groups)])]
  transfers between devices with their start and end apart: 6 -> 6, of which waited for: 6 -> 6; matrix products, arithmetic and copies ran while one was open for 1% -> 2% of each run, Pallas kernels for 10% -> 0%
where the time goes in v2:
time: 87.2 us; the launch traced here: 87 us
  blocking collectives  35.4 us (41%)
  waiting for transfers between devices  19 us (22%)
  Pallas kernels  17.7 us (20%)
  starting transfers between devices  12 us (14%)
  local copies, waits for them, and re-layouts  1.94 us (2%)
    all_to_all x1, blocking collectives, shards(): lax.all_to_all(send, 'expert', split_axis=0, concat_axis=0, tiled=True)  35.4 us
    ppermute x5, waiting for transfers between devices, swap(): return lax.ppermute(part, 'dp', [(i, i ^ mask) for i in range(groups)])  13.8 us
    pallas_call x1, Pallas kernels, expert(): pl.pallas_call(expert_kernel, out_shape=(pltpu.HBM(got.shape, BF), pltpu....  12.3 us
    ppermute x5, starting transfers between devices, swap(): return lax.ppermute(part, 'dp', [(i, i ^ mask) for i in range(groups)])  8.14 us
    all_to_all x1, waiting for transfers between devices, shards(): lax.all_to_all(send, 'expert', split_axis=0, concat_axis=0, tiled=True)  5.23 us
    all_to_all x1, starting transfers between devices, shards(): lax.all_to_all(send, 'expert', split_axis=0, concat_axis=0, tiled=True)  3.86 us
    pallas_call x1, Pallas kernels, dispatch(): pl.pallas_call(dispatch_kernel, out_shape=pltpu.HBM(shape, BF), in_specs=...  2.92 us
    pallas_call x1, Pallas kernels, combine(): pl.pallas_call(combine_kernel, out_shape=(pltpu.HBM(shape, BF),) * 2, in_...  2.26 us
  transfers between devices with their start and end apart: 6, of which 6 were waited for; matrix products, arithmetic and copies ran while one was open for 2% of the time, Pallas kernels for 0%

profile of v2, /device:TPU:32, one launch (start us, length us, event | category | flops | bytes accessed | tf_op | source)
XLA Modules:
  0.0 87.0 jit_solution(542046397965267897)
XLA Ops:
  0.6 2.9 %dispatch.1 = bf16[16,32,2048]{2,1,0:T(8,128)(2,1)} custom-call(s32[8,128]{1,0:T(8,128)} %bitcast.30, f32[8,128]{1,0:T(8,128)} %bitcast.32, bf16[128,2048]{1,0:T(8,128)(2,1)} %act_hbm.1, bf16[128,2048]{1,0:T(8,128)(2,1)} %up_hbm.1), custom_call_target="tpu_custom_call" | custom-call | tf_op jit(solution)/shard_map/dispatch/pallas_call | solution.py:103
  3.6 35.4 %all_to_all.10.got_ref = bf16[16,32,2048]{2,1,0:T(8,128)(2,1)S(1)} all-to-all(bf16[16,32,2048]{2,1,0:T(8,128)(2,1)} %dispatch.1), channel_id=1, replica_groups=mesh['dp'=16,'expert'=16] {'expert'}, dimensions={0} | all-to-all | bytes 4194304 | tf_op jit(solution)/shard_map/all_to_all | solution.py:346
  39.0 12.3 %expert.1 = (bf16[16,32,2048]{2,1,0:T(8,128)(2,1)}, f32[8,96,128]{2,1,0:T(8,128)}, f32[8,96,128]{2,1,0:T(8,128)}) custom-call(s32[1]{0:T(128)} %bitcast.2.group_ref, bf16[16,32,2048]{2,1,0:T(8,128)(2,1)S(1)} %all_to_all.10.got_ref, bf16[2048,768]{1,0:T(8,128)(2,1)} %bitcast.34, bf16[2048,768]{1,0:T(8,128)(2,1)} %bitcast.35, bf16[768,2048]{1,0:T(8,128)(2,1)} %bitcast.36, ...), custom_call_target="tpu_custom_call" | custom-call | tf_op jit(solution)/shard_map/expert/pallas_call | solution.py:315
  51.3 0.0 copy-start.4
  51.3 0.0 copy-start.3
  51.3 3.9 %all-to-all-start.1 = ((bf16[16,32,2048]{2,1,0:T(8,128)(2,1)}), bf16[16,32,2048]{2,1,0:T(8,128)(2,1)S(1)}, u32[]{:S(2)}, u32[]{:S(2)}) async-start(bf16[16,32,2048]{2,1,0:T(8,128)(2,1)} %get-tuple-element.16), calls=%async_computation.1 | async-start | bytes 4194304 | tf_op jit(solution)/shard_map/all_to_all | solution.py:359
  55.2 0.0 copy-start.1
  55.2 0.0 copy-start.2
  55.2 0.0 copy-done.4
  55.2 0.1 collective-permute-start
  55.3 1.7 %collective-permute-done = f32[8,96,128]{2,1,0:T(8,128)S(1)} collective-permute-done((f32[8,96,128]{2,1,0:T(8,128)S(1)}, f32[8,96,128]{2,1,0:T(8,128)S(1)}, u32[]{:S(2)}, u32[]{:S(2)}) %collective-permute-start) | collective-permute-done | bytes 393248 | tf_op jit(solution)/shard_map/ppermute | solution.py:362
  57.0 0.0 copy-done.3
  57.0 0.1 add.15
  57.1 0.2 collective-permute-start.1
  57.3 6.8 %collective-permute-done.1 = f32[4,96,128]{2,1,0:T(8,128)S(1)} collective-permute-done((f32[4,96,128]{2,1,0:T(8,128)S(1)}, f32[4,96,128]{2,1,0:T(8,128)S(1)}, u32[]{:S(2)}, u32[]{:S(2)}) %collective-permute-start.1) | collective-permute-done | bytes 196640 | tf_op jit(solution)/shard_map/ppermute | solution.py:362
  64.2 6.4 %collective-permute-start.2 = (f32[96,128]{1,0:T(8,128)S(1)}, f32[96,128]{1,0:T(8,128)S(1)}, u32[]{:S(2)}, u32[]{:S(2)}) collective-permute-start(f32[96,128]{1,0:T(8,128)S(1)} %get-tuple-element.26), channel_id=1, source_target_pairs={{0,128},{16,144},{32,160},{48,176},{64,192},{80,208},{96,224},{112... | collective-permute-start | bytes 147464 | tf_op jit(solution)/shard_map/ppermute | solution.py:362
  70.6 1.5 %collective-permute-start.3 = (f32[96,128]{1,0:T(8,128)S(1)}, f32[96,128]{1,0:T(8,128)S(1)}, u32[]{:S(2)}, u32[]{:S(2)}) collective-permute-start(f32[96,128]{1,0:T(8,128)S(1)} %get-tuple-element.24), channel_id=1, source_target_pairs={{0,64},{16,80},{32,96},{48,112},{64,0},{80,16},{96,32},{112,48},{1... | collective-permute-start | bytes 147464 | tf_op jit(solution)/shard_map/ppermute | solution.py:362
  72.0 0.0 collective-permute-start.4
  72.1 0.0 copy-done.1
  72.1 0.0 copy-done.2
  72.1 0.3 tables.1.table_hbm
  72.3 0.0 copy-start
  72.3 0.7 copy-done
  73.0 0.7 collective-permute-done.2
  73.7 1.9 %collective-permute-done.3 = f32[96,128]{1,0:T(8,128)S(1)} collective-permute-done((f32[96,128]{1,0:T(8,128)S(1)}, f32[96,128]{1,0:T(8,128)S(1)}, u32[]{:S(2)}, u32[]{:S(2)}) %collective-permute-start.3) | collective-permute-done | bytes 49184 | tf_op jit(solution)/shard_map/ppermute | solution.py:362
  75.6 2.6 %collective-permute-done.4 = f32[96,128]{1,0:T(8,128)S(1)} collective-permute-done((f32[96,128]{1,0:T(8,128)S(1)}, f32[96,128]{1,0:T(8,128)S(1)}, u32[]{:S(2)}, u32[]{:S(2)}) %collective-permute-start.4) | collective-permute-done | bytes 49184 | tf_op jit(solution)/shard_map/ppermute | solution.py:362
  78.3 0.6 slice_bitcast_fusion.4
  78.9 0.6 reshape.23
  79.5 5.2 %all-to-all-done.1.got_ref = bf16[16,32,2048]{2,1,0:T(8,128)(2,1)S(1)} async-done(((bf16[16,32,2048]{2,1,0:T(8,128)(2,1)}), bf16[16,32,2048]{2,1,0:T(8,128)(2,1)S(1)}, u32[]{:S(2)}, u32[]{:S(2)}) %all-to-all-start.1) | async-done | bytes 2097184 | tf_op jit(solution)/shard_map/all_to_all | solution.py:359
  84.7 2.3 %combine.1 = (bf16[128,2048]{1,0:T(8,128)(2,1)}, bf16[128,2048]{1,0:T(8,128)(2,1)}) custom-call(bf16[16,32,2048]{2,1,0:T(8,128)(2,1)S(1)} %all-to-all-done.1.got_ref, bf16[3,128,256]{2,1,0:T(8,128)(2,1)} %copy-done), custom_call_target="tpu_custom_call" | custom-call | tf_op jit(solution)/shard_map/combine/pallas_call | solution.py:163
  (6 shorter events, 0.1 us)
Async XLA Ops:
  51.3 3.9 %copy-start.4 = (f32[8,96,128]{2,1,0:T(8,128)S(1)}, f32[8,96,128]{2,1,0:T(8,128)}, u32[]{:S(2)}) copy-start(f32[8,96,128]{2,1,0:T(8,128)} %get-tuple-element.23) | copy-start | bytes 1179652
  51.3 5.7 %copy-start.3 = (f32[8,96,128]{2,1,0:T(8,128)S(1)}, f32[8,96,128]{2,1,0:T(8,128)}, u32[]{:S(2)}) copy-start(f32[8,96,128]{2,1,0:T(8,128)} %get-tuple-element.22) | copy-start | bytes 1179652
  51.3 33.4 %all-to-all-start.1 = ((bf16[16,32,2048]{2,1,0:T(8,128)(2,1)}), bf16[16,32,2048]{2,1,0:T(8,128)(2,1)S(1)}, u32[]{:S(2)}, u32[]{:S(2)}) async-start(bf16[16,32,2048]{2,1,0:T(8,128)(2,1)} %get-tuple-element.16), calls=%async_computation.1 | async-start | bytes 4194304 | tf_op jit(solution)/shard_map/all_to_all | solution.py:359
  55.2 16.9 %copy-start.1 = (s32[128,8]{0,1:T(8,128)S(1)}, s32[128,8]{0,1:T(8,128)}, u32[]{:S(2)}) copy-start(s32[128,8]{0,1:T(8,128)} %param.17) | copy-start | bytes 12292
  55.2 16.9 %copy-start.2 = (f32[128,8]{0,1:T(8,128)S(1)}, f32[128,8]{0,1:T(8,128)}, u32[]{:S(2)}) copy-start(f32[128,8]{0,1:T(8,128)} %param.18) | copy-start | bytes 12292
  55.2 1.8 %collective-permute-start = (f32[8,96,128]{2,1,0:T(8,128)S(1)}, f32[8,96,128]{2,1,0:T(8,128)S(1)}, u32[]{:S(2)}, u32[]{:S(2)}) collective-permute-start(f32[8,96,128]{2,1,0:T(8,128)S(1)} %copy-done.4), channel_id=1, source_target_pairs={{0,16},{16,0},{32,48},{48,32},{64,80},{80,64},{96,112},{112,96},{1... | collective-permute-start | bytes 1179656 | tf_op jit(solution)/shard_map/ppermute | solution.py:362
  57.1 7.0 %collective-permute-start.1 = (f32[4,96,128]{2,1,0:T(8,128)S(1)}, f32[4,96,128]{2,1,0:T(8,128)S(1)}, u32[]{:S(2)}, u32[]{:S(2)}) collective-permute-start(f32[4,96,128]{2,1,0:T(8,128)S(1)} %slice.37), channel_id=1, source_target_pairs={{0,32},{16,48},{32,0},{48,16},{64,96},{80,112},{96,64},{112,80},{1... | collective-permute-start | bytes 589832 | tf_op jit(solution)/shard_map/ppermute | solution.py:362
  64.2 9.5 %collective-permute-start.2 = (f32[96,128]{1,0:T(8,128)S(1)}, f32[96,128]{1,0:T(8,128)S(1)}, u32[]{:S(2)}, u32[]{:S(2)}) collective-permute-start(f32[96,128]{1,0:T(8,128)S(1)} %get-tuple-element.26), channel_id=1, source_target_pairs={{0,128},{16,144},{32,160},{48,176},{64,192},{80,208},{96,224},{112... | collective-permute-start | bytes 147464 | tf_op jit(solution)/shard_map/ppermute | solution.py:362
  70.6 5.1 %collective-permute-start.3 = (f32[96,128]{1,0:T(8,128)S(1)}, f32[96,128]{1,0:T(8,128)S(1)}, u32[]{:S(2)}, u32[]{:S(2)}) collective-permute-start(f32[96,128]{1,0:T(8,128)S(1)} %get-tuple-element.24), channel_id=1, source_target_pairs={{0,64},{16,80},{32,96},{48,112},{64,0},{80,16},{96,32},{112,48},{1... | collective-permute-start | bytes 147464 | tf_op jit(solution)/shard_map/ppermute | solution.py:362
  72.0 6.2 %collective-permute-start.4 = (f32[96,128]{1,0:T(8,128)S(1)}, f32[96,128]{1,0:T(8,128)S(1)}, u32[]{:S(2)}, u32[]{:S(2)}) collective-permute-start(f32[96,128]{1,0:T(8,128)S(1)} %get-tuple-element.25), channel_id=1, source_target_pairs={{0,192},{16,208},{32,224},{48,240},{64,128},{80,144},{96,160},{112... | collective-permute-start | bytes 147464 | tf_op jit(solution)/shard_map/ppermute | solution.py:362
  72.3 0.7 copy-start

commit v3 on v2

--- a/solution.py
+++ b/solution.py
@@ -6,6 +6,7 @@
 from jax.sharding import PartitionSpec as P
 
 GROUP = 128
+FIRST_TO_FREEZE = 0
 CAP = 16
 SCALING = 0.5
 BF = jnp.bfloat16
@@ -171,11 +172,54 @@
     )(in_vmem(got), in_hbm(table))
 
 
+def freeze_kernel(group_ref, *refs):
+    levels, scales, frozen = refs[:3], refs[3:6], refs[-11:-8]
+    level_refs, scale_refs = refs[-8:-5], refs[-5:-2]
+    in_sem, out_sem = refs[-2:]
+
+    @pl.when(group_ref[0] % 2 == FIRST_TO_FREEZE)
+    def _():
+        loads = [pltpu.make_async_copy(*pair, in_sem.at[i])
+                 for i, pair in enumerate((*zip(scales, scale_refs), *zip(levels, level_refs)))]
+        for load in loads:
+            load.start()
+        for load in loads[:3]:
+            load.wait()
+        stores = []
+        for i, (level_ref, scale_ref) in enumerate(zip(level_refs, scale_refs)):
+            loads[3 + i].wait()
+            for j in range(scale_ref.shape[0]):
+                rows = slice(j * GROUP, (j + 1) * GROUP)
+                scale = scale_ref[j] if len(scale_ref.shape) == 3 else scale_ref[j : j + 1, :]
+                level_ref[rows, :] = (level_ref[rows, :].astype(F32) * scale).astype(BF)
+            stores.append(pltpu.make_async_copy(level_ref, frozen[i], out_sem.at[i]))
+            stores[-1].start()
+        for store in stores:
+            store.wait()
+
+
+def freeze(group, levels, scales):
+    return pl.pallas_call(
+        freeze_kernel,
+        out_shape=tuple(pltpu.HBM(level.shape, BF) for level in levels),
+        in_specs=[SMEM] + [HBM] * 6,
+        out_specs=(HBM,) * 3,
+        scratch_shapes=[
+            *(pltpu.VMEM(level.shape, BF) for level in levels), *(pltpu.VMEM(scale.shape, F32) for scale in scales),
+            DMA((6,)), DMA((3,)),
+        ],
+        compiler_params=params(16),
+        cost_estimate=cost(1 << 24, 1 << 24),
+        name="freeze",
+    )(group, *(in_hbm(array) for array in (*levels, *scales)))
+
+
 def expert_kernel(
-    group_ref, got_ref, gate_hbm, up_hbm, down_hbm, gate_scale_hbm, up_scale_hbm, down_scale_hbm, gate_first_hbm, up_first_hbm,
-    down_second_hbm, gate_second_hbm, up_second_hbm, down_first_hbm, send_hbm, keep_hbm, other_hbm,
+    group_ref, got_ref, gate_hbm, up_hbm, down_hbm, gate_frozen_hbm, up_frozen_hbm, down_frozen_hbm,
+    gate_scale_hbm, up_scale_hbm, down_scale_hbm, gate_first_hbm, up_first_hbm, down_second_hbm,
+    gate_second_hbm, up_second_hbm, down_first_hbm, send_hbm, keep_hbm, other_hbm,
     gate_ref, up_ref, down_ref, gate_scale_ref, up_scale_ref, down_scale_ref, wide_ref, narrow_ref, send_ref,
-    inside_ref, piece_ref, level_sem, small_sem, out_sem, piece_sem,
+    inside_ref, piece_ref, rounded_ref, level_sem, small_sem, scale_sem, out_sem, piece_sem,
 ):
     experts, _, width = got_ref.shape
     rows = experts * CAP
@@ -187,32 +231,59 @@
              for i, source in enumerate((gate_first_hbm, up_first_hbm, down_second_hbm))]
     pairs += [(source, narrow_ref.at[i * rank : (i + 1) * rank, :])
               for i, source in enumerate((gate_second_hbm, up_second_hbm, down_first_hbm))]
-    pairs += [(gate_scale_hbm, gate_scale_ref), (up_scale_hbm, up_scale_ref), (down_scale_hbm, down_scale_ref)]
     small = [pltpu.make_async_copy(source, target, small_sem.at[i]) for i, (source, target) in enumerate(pairs)]
     for copy in small:
         copy.start()
-    weights = ((gate_hbm, gate_ref), (up_hbm, up_ref), (down_hbm, down_ref))
+    ready = group_ref[0] % 2 == FIRST_TO_FREEZE
+    raw = ((gate_hbm, gate_ref), (up_hbm, up_ref), (down_hbm, down_ref))
+    frozen = ((gate_frozen_hbm, gate_ref), (up_frozen_hbm, up_ref), (down_frozen_hbm, down_ref))
     pieces = [(part, kind) for part in range(inner // step) for kind in range(3)]
-    levels = []
-    for part, kind in pieces:
+
+    def loads(weights, some):
+        copies = []
+        for part, kind in some:
+            cols = slice(part * step, (part + 1) * step)
+            place = (cols, slice(0, width)) if kind == 2 else (slice(0, width), cols)
+            source, target = weights[kind]
+            copies.append(pltpu.make_async_copy(source.at[place], target.at[place], level_sem.at[part, kind]))
+        return copies
+
+    scales = (gate_scale_ref, up_scale_ref, down_scale_ref)
+    scale_loads = [pltpu.make_async_copy(source, target, scale_sem.at[i]) for i, (source, target) in enumerate(
+        zip((gate_scale_hbm, up_scale_hbm, down_scale_hbm), scales))]
+
+    @pl.when(ready)
+    def _():
+        for scale_ref in scales:
+            scale_ref[...] = jnp.ones_like(scale_ref)
+
+    @pl.when(jnp.logical_not(ready))
+    def _():
+        for copy in scale_loads:
+            copy.start()
+
+    def start(some):
+        for condition, weights in ((ready, frozen), (jnp.logical_not(ready), raw)):
+
+            @pl.when(condition)
+            def _(weights=weights):
+                for copy in loads(weights, some):
+                    copy.start()
+
+    start(pieces[:3])
+
+    def land(part):
+        for copy in loads(raw, pieces[3 * part : 3 * part + 3]):
+            copy.wait()
+
         cols = slice(part * step, (part + 1) * step)
-        place = (cols, slice(0, width)) if kind == 2 else (slice(0, width), cols)
-        source, target = weights[kind]
-        levels.append(pltpu.make_async_copy(source.at[place], target.at[place], level_sem.at[part, kind]))
-    for copy in levels[:3]:
-        copy.start()
-    def land(index):
-        part, kind = pieces[index]
-        if kind == 2:
-            for i in range(part * step // GROUP, (part + 1) * step // GROUP):
-                group = slice(i * GROUP, (i + 1) * GROUP)
-                down_ref[group, :] = (down_ref[group, :].astype(F32) * down_scale_ref[i]).astype(BF)
-        else:
-            cols = slice(part * step, (part + 1) * step)
-            target, scale_ref = ((gate_ref, gate_scale_ref), (up_ref, up_scale_ref))[kind]
+        for target, scale_ref in ((gate_ref, gate_scale_ref), (up_ref, up_scale_ref)):
             for i in range(width // GROUP):
                 group = slice(i * GROUP, (i + 1) * GROUP)
                 target[group, cols] = (target[group, cols].astype(F32) * scale_ref[i : i + 1, cols]).astype(BF)
+        for i in range(part * step // GROUP, (part + 1) * step // GROUP):
+            group = slice(i * GROUP, (i + 1) * GROUP)
+            down_ref[group, :] = (down_ref[group, :].astype(F32) * down_scale_ref[i]).astype(BF)
 
     x = got_ref[:, :CAP, :].reshape(rows, width)
     g = got_ref[:, CAP:, :].reshape(rows, width)
@@ -223,8 +294,13 @@
     down_first_ref = narrow_ref.at[2 * rank :, :]
     for copy in small:
         copy.wait()
-    for copy in levels[3:]:
-        copy.start()
+    start(pieces[3:])
+
+    @pl.when(jnp.logical_not(ready))
+    def _():
+        for copy in scale_loads:
+            copy.wait()
+
     first_low = nt(x, first_ref[...]).astype(BF)
     gate_low, up_low = first_low[:, :rank], first_low[:, rank:]
     back_down = nt(g, down_second_ref[...]).astype(BF)
@@ -234,9 +310,7 @@
     back_up = jnp.zeros((rows, rank), F32)
     for index, (part, kind) in enumerate(pieces):
         if kind == 0:
-            for copy in levels[index : index + 3]:
-                copy.wait()
-        land(index)
+            land(part)
         cols = slice(part * step, (part + 1) * step)
         if kind == 0:
             gate_pre = nn(x, gate_ref[:, cols]) + nn(gate_low * half, gate_second_ref[:, cols])
@@ -294,39 +368,46 @@
     group = group_ref[0]
     side = group % 2
     plane = group // 2
+    rounded_ref[...] = piece_ref[...].astype(BF)
+    half = groups // 4
     for place in range(groups // 2):
         turned = (place & 1) * 4 + (place & 2) + (place >> 2)
         other = lax.bitwise_xor(plane, jnp.int32(turned))
-        for mine, out in ((side, keep_hbm), (1 - side, other_hbm)):
-            stores.append(pltpu.make_async_copy(piece_ref.at[2 * other + mine], out.at[place], piece_sem.at[place, 0 if out is keep_hbm else 1]))
-            stores[-1].start()
+        source, target = (piece_ref, keep_hbm) if place < half else (rounded_ref, other_hbm)
+        for i, core in enumerate((side, 1 - side)):
+            copy = pltpu.make_async_copy(
+                source.at[2 * other + core], target.at[place % half, i], piece_sem.at[place, i]
+            )
+            stores.append(copy)
+            copy.start()
     for store in stores:
         store.wait()
 
 
-def expert(group, groups, got, levels, scales, wide, narrow):
+def expert(group, groups, got, levels, frozen, scales, wide, narrow):
     rows = got.shape[0] * CAP
     width = got.shape[2]
     inner = levels[0].shape[1]
     rank = wide[0].shape[0]
     column = width // groups
     height = 3 * rank + 8 * (inner // column)
-    part = (groups // 2, height, column)
+    part = (groups // 4, 2, height, column)
     return pl.pallas_call(
         expert_kernel,
-        out_shape=(pltpu.HBM(got.shape, BF), pltpu.HBM(part, F32), pltpu.HBM(part, F32)),
-        in_specs=[SMEM, VMEM] + [HBM] * 12,
+        out_shape=(pltpu.HBM(got.shape, BF), pltpu.HBM(part, F32), pltpu.HBM(part, BF)),
+        in_specs=[SMEM, VMEM] + [HBM] * 15,
         out_specs=(HBM,) * 3,
         scratch_shapes=[
             *(pltpu.VMEM(level.shape, BF) for level in levels),
             *(pltpu.VMEM(scale.shape, F32) for scale in scales),
             pltpu.VMEM((3 * rank, width), BF), pltpu.VMEM((3 * rank, inner), BF),
             pltpu.VMEM(got.shape, BF), pltpu.VMEM((3, rows, inner), BF), pltpu.VMEM((groups, height, column), F32),
-            DMA((inner // 256, 3)), DMA((9,)), DMA((width // 256,)), DMA((groups // 2, 2)),
+            pltpu.VMEM((groups, height, column), BF),
+            DMA((inner // 256, 3)), DMA((6,)), DMA((3,)), DMA((width // 256,)), DMA((groups // 2, 2)),
         ],
         compiler_params=params(32),
         name="expert",
-    )(group, in_vmem(got), *(in_hbm(array) for array in (*levels, *scales, *wide, *narrow)))
+    )(group, in_vmem(got), *(in_hbm(array) for array in (*levels, *frozen, *scales, *wide, *narrow)))
 
 
 def shards(
@@ -342,15 +423,21 @@
 
     routes, gates = routes.T, gates.T
     group = lax.axis_index("dp").astype(jnp.int32).reshape(1)
-    send, group = lax.optimization_barrier((dispatch(routes, gates, activations, upstream, experts), group))
+    levels = (gate_levels[0], up_levels[0], down_levels[0])
+    scales = (gate_scales[0], up_scales[0], down_scales.transpose(1, 0, 2))
+    frozen = freeze(group, levels, scales)
+    routes, gates, frozen = lax.optimization_barrier((routes, gates, frozen))
+    send = dispatch(routes, gates, activations, upstream, experts)
+    send, group, frozen = lax.optimization_barrier((send, group, frozen))
     got = lax.all_to_all(send, "expert", split_axis=0, concat_axis=0, tiled=True)
 
     send, keep, other = expert(
         group,
         groups,
         got,
-        (gate_levels[0], up_levels[0], down_levels[0]),
-        (gate_scales[0], up_scales[0], down_scales.transpose(1, 0, 2)),
+        levels,
+        frozen,
+        scales,
         (gate_adapter_first[0], up_adapter_first[0], down_adapter_second[0]),
         (gate_adapter_second[0], up_adapter_second[0], down_adapter_first[0]),
     )
@@ -361,10 +448,10 @@
     def swap(part, mask):
         return lax.ppermute(part, "dp", [(i, i ^ mask) for i in range(groups)])
 
-    total = keep + swap(other, 1)
-    half = groups // 4
-    total = total[:half] + swap(total[half:], 2)
-    total = total[0] + (swap(total[1], 8) + swap(total[2], 4) + swap(total[3], 12))
+    total = keep + swap(other, 2).astype(F32)
+    sent = total.astype(BF)
+    total = total[0] + (swap(sent[1], 8).astype(F32) + swap(sent[2], 4).astype(F32) + swap(sent[3], 12).astype(F32))
+    total = total[0] + swap(total[1], 1)
     column = width // groups
     grad_wide = total[: 3 * rank].reshape(1, 3, rank, column)
     narrow = total[3 * rank :].reshape(inner // column, 8, column)[:, :3]

time: 87.2 us -> 82.4 us (0.945)
  Pallas kernels: 17.7 us -> 24.5 us
  blocking collectives: 35.4 us -> 29 us
  waiting for transfers between devices: 19 us -> 13.5 us
    pallas_call x0 -> x1, Pallas kernels: none -> 6.88 us  [freeze(): pl.pallas_call(freeze_kernel, out_shape=tuple((pltpu.HBM(level.shape, BF)...]
    all_to_all x1, blocking collectives: 35.4 us -> 29 us  [shards(): lax.all_to_all(send, 'expert', split_axis=0, concat_axis=0, tiled=True)]
    all_to_all x1, waiting for transfers between devices: 5.23 us -> 0.72 us  [shards(): lax.all_to_all(send, 'expert', split_axis=0, concat_axis=0, tiled=True)]
    ppermute x5, waiting for transfers between devices: 13.8 us -> 12.8 us  [swap(): return lax.ppermute(part, 'dp', [(i, i ^ mask) for i in range(groups)])]
where the time goes in v3:
time: 82.4 us; the launch traced here: 81.4 us
  blocking collectives  29 us (35%)
  Pallas kernels  24.5 us (30%)
  waiting for transfers between devices  13.5 us (16%)
  starting transfers between devices  11.4 us (14%)
  local copies, waits for them, and re-layouts  1.94 us (2%)
  between operations  0.94 us (1%)
    all_to_all x1, blocking collectives, shards(): lax.all_to_all(send, 'expert', split_axis=0, concat_axis=0, tiled=True)  29 us
    ppermute x5, waiting for transfers between devices, swap(): return lax.ppermute(part, 'dp', [(i, i ^ mask) for i in range(groups)])  12.8 us
    pallas_call x1, Pallas kernels, expert(): pl.pallas_call(expert_kernel, out_shape=(pltpu.HBM(got.shape, BF), pltpu....  12.2 us
    ppermute x5, starting transfers between devices, swap(): return lax.ppermute(part, 'dp', [(i, i ^ mask) for i in range(groups)])  7.51 us
    pallas_call x1, Pallas kernels, freeze(): pl.pallas_call(freeze_kernel, out_shape=tuple((pltpu.HBM(level.shape, BF)...  6.88 us
    all_to_all x1, starting transfers between devices, shards(): lax.all_to_all(send, 'expert', split_axis=0, concat_axis=0, tiled=True)  3.86 us
    pallas_call x1, Pallas kernels, dispatch(): pl.pallas_call(dispatch_kernel, out_shape=pltpu.HBM(shape, BF), in_specs=...  2.94 us
    pallas_call x1, Pallas kernels, combine(): pl.pallas_call(combine_kernel, out_shape=(pltpu.HBM(shape, BF),) * 2, in_...  2.26 us
  transfers between devices with their start and end apart: 6, of which 6 were waited for; matrix products, arithmetic and copies ran while one was open for 2% of the time, Pallas kernels for 0%

profile of v3, /device:TPU:32, one launch (start us, length us, event | category | flops | bytes accessed | tf_op | source)
XLA Modules:
  0.0 81.4 jit_solution(8297144703735065946)
XLA Ops:
  0.6 6.9 %freeze.1 = (bf16[2048,768]{1,0:T(8,128)(2,1)}, bf16[2048,768]{1,0:T(8,128)(2,1)}, bf16[768,2048]{1,0:T(8,128)(2,1)}) custom-call(s32[1]{0:T(128)} %bitcast.2.group_ref, bf16[2048,768]{1,0:T(8,128)(2,1)} %bitcast.40, bf16[2048,768]{1,0:T(8,128)(2,1)} %bitcast.42, bf16[768,2048]{1,0:T(8,128)(2,1)} %bitcast.44, f32[16,768]{1,0:T(8,128)} %bitcast.46, ...), custom_call_target="tpu_custom_call" | custom-call | flops 16777216 | bytes 16777216 | tf_op jit(solution)/shard_map/freeze/pallas_call | solution.py:202
  7.5 2.9 %dispatch.1 = bf16[16,32,2048]{2,1,0:T(8,128)(2,1)} custom-call(s32[8,128]{1,0:T(8,128)} %bitcast.36, f32[8,128]{1,0:T(8,128)} %bitcast.38, bf16[128,2048]{1,0:T(8,128)(2,1)} %act_hbm.1, bf16[128,2048]{1,0:T(8,128)(2,1)} %up_hbm.1), custom_call_target="tpu_custom_call" | custom-call | tf_op jit(solution)/shard_map/dispatch/pallas_call | solution.py:104
  10.5 29.0 %all_to_all.10.got_ref = bf16[16,32,2048]{2,1,0:T(8,128)(2,1)S(1)} all-to-all(bf16[16,32,2048]{2,1,0:T(8,128)(2,1)} %dispatch.1), channel_id=1, replica_groups=mesh['dp'=16,'expert'=16] {'expert'}, dimensions={0} | all-to-all | bytes 4194304 | tf_op jit(solution)/shard_map/all_to_all | solution.py:432
  39.5 12.2 %expert.1 = (bf16[16,32,2048]{2,1,0:T(8,128)(2,1)}, f32[4,2,96,128]{3,2,1,0:T(8,128)}, bf16[4,2,96,128]{3,2,1,0:T(8,128)(2,1)}) custom-call(s32[1]{0:T(128)} %bitcast.2.group_ref, bf16[16,32,2048]{2,1,0:T(8,128)(2,1)S(1)} %all_to_all.10.got_ref, bf16[2048,768]{1,0:T(8,128)(2,1)} %bitcast.41, bf16[2048,768]{1,0:T(8,128)(2,1)} %bitcast.43, ...), custom_call_target="tpu_custom_call" | custom-call | tf_op jit(solution)/shard_map/expert/pallas_call | solution.py:395
  51.7 0.0 copy-start.4
  51.7 0.0 copy-start.3
  51.7 0.0 copy-start.1
  51.7 0.0 copy-start.2
  51.7 3.9 %all-to-all-start.1 = ((bf16[16,32,2048]{2,1,0:T(8,128)(2,1)}), bf16[16,32,2048]{2,1,0:T(8,128)(2,1)S(1)}, u32[]{:S(2)}, u32[]{:S(2)}) async-start(bf16[16,32,2048]{2,1,0:T(8,128)(2,1)} %get-tuple-element.38), calls=%async_computation.1 | async-start | bytes 4194304 | tf_op jit(solution)/shard_map/all_to_all | solution.py:446
  55.6 0.0 copy-done.4
  55.6 0.2 collective-permute-start
  55.8 7.1 %collective-permute-done = bf16[4,2,96,128]{3,2,1,0:T(8,128)(2,1)S(1)} collective-permute-done((bf16[4,2,96,128]{3,2,1,0:T(8,128)(2,1)S(1)}, bf16[4,2,96,128]{3,2,1,0:T(8,128)(2,1)S(1)}, u32[]{:S(2)}, u32[]{:S(2)}) %collective-permute-start) | collective-permute-done | bytes 196640 | tf_op jit(solution)/shard_map/ppermute | solution.py:449
  62.9 0.0 copy-done.3
  62.9 0.1 fusion.2
  63.0 5.6 %collective-permute-start.1 = (bf16[2,96,128]{2,1,0:T(8,128)(2,1)S(1)}, bf16[2,96,128]{2,1,0:T(8,128)(2,1)S(1)}, u32[]{:S(2)}, u32[]{:S(2)}) collective-permute-start(bf16[2,96,128]{2,1,0:T(8,128)(2,1)S(1)} %get-tuple-element.48), channel_id=1, source_target_pairs={{0,128},{16,144},{32,160},{48,176},{64,192},{80,208},{96,224},{112... | collective-permute-start | bytes 147464 | tf_op jit(solution)/shard_map/ppermute | solution.py:449
  68.6 1.5 %collective-permute-start.3 = (bf16[2,96,128]{2,1,0:T(8,128)(2,1)S(1)}, bf16[2,96,128]{2,1,0:T(8,128)(2,1)S(1)}, u32[]{:S(2)}, u32[]{:S(2)}) collective-permute-start(bf16[2,96,128]{2,1,0:T(8,128)(2,1)S(1)} %get-tuple-element.49), channel_id=1, source_target_pairs={{0,192},{16,208},{32,224},{48,240},{64,128},{80,144},{96,160},{112... | collective-permute-start | bytes 147464 | tf_op jit(solution)/shard_map/ppermute | solution.py:449
  70.1 0.1 collective-permute-start.2
  70.2 1.0 %collective-permute-done.1 = bf16[2,96,128]{2,1,0:T(8,128)(2,1)S(1)} collective-permute-done((bf16[2,96,128]{2,1,0:T(8,128)(2,1)S(1)}, bf16[2,96,128]{2,1,0:T(8,128)(2,1)S(1)}, u32[]{:S(2)}, u32[]{:S(2)}) %collective-permute-start.1) | collective-permute-done | bytes 49184 | tf_op jit(solution)/shard_map/ppermute | solution.py:449
  71.3 3.5 %collective-permute-done.3 = bf16[2,96,128]{2,1,0:T(8,128)(2,1)S(1)} collective-permute-done((bf16[2,96,128]{2,1,0:T(8,128)(2,1)S(1)}, bf16[2,96,128]{2,1,0:T(8,128)(2,1)S(1)}, u32[]{:S(2)}, u32[]{:S(2)}) %collective-permute-start.3) | collective-permute-done | bytes 49184 | tf_op jit(solution)/shard_map/ppermute | solution.py:449
  74.8 0.8 %collective-permute-done.2 = bf16[2,96,128]{2,1,0:T(8,128)(2,1)S(1)} collective-permute-done((bf16[2,96,128]{2,1,0:T(8,128)(2,1)S(1)}, bf16[2,96,128]{2,1,0:T(8,128)(2,1)S(1)}, u32[]{:S(2)}, u32[]{:S(2)}) %collective-permute-start.2) | collective-permute-done | bytes 49184 | tf_op jit(solution)/shard_map/ppermute | solution.py:449
  75.7 0.1 collective-permute-start.4
  75.8 0.0 copy-done.1
  75.8 0.0 copy-done.2
  75.8 0.3 tables.1.table_hbm
  76.1 0.0 copy-start
  76.1 0.7 copy-done
  76.7 0.2 collective-permute-done.4
  77.0 0.6 slice_bitcast_fusion.6
  77.6 0.6 reshape.23
  78.2 0.7 all-to-all-done.1.got_ref
  78.9 2.3 %combine.1 = (bf16[128,2048]{1,0:T(8,128)(2,1)}, bf16[128,2048]{1,0:T(8,128)(2,1)}) custom-call(bf16[16,32,2048]{2,1,0:T(8,128)(2,1)S(1)} %all-to-all-done.1.got_ref, bf16[3,128,256]{2,1,0:T(8,128)(2,1)} %copy-done), custom_call_target="tpu_custom_call" | custom-call | tf_op jit(solution)/shard_map/combine/pallas_call | solution.py:164
  (6 shorter events, 0.1 us)
Async XLA Ops:
  51.7 3.9 %copy-start.4 = (bf16[4,2,96,128]{3,2,1,0:T(8,128)(2,1)S(1)}, bf16[4,2,96,128]{3,2,1,0:T(8,128)(2,1)}, u32[]{:S(2)}) copy-start(bf16[4,2,96,128]{3,2,1,0:T(8,128)(2,1)} %get-tuple-element.45) | copy-start | bytes 589828
  51.7 11.3 %copy-start.3 = (f32[4,2,96,128]{3,2,1,0:T(8,128)S(1)}, f32[4,2,96,128]{3,2,1,0:T(8,128)}, u32[]{:S(2)}) copy-start(f32[4,2,96,128]{3,2,1,0:T(8,128)} %get-tuple-element.44) | copy-start | bytes 1179652
  51.7 24.1 %copy-start.1 = (s32[128,8]{0,1:T(8,128)S(1)}, s32[128,8]{0,1:T(8,128)}, u32[]{:S(2)}) copy-start(s32[128,8]{0,1:T(8,128)} %param.17) | copy-start | bytes 12292
  51.7 24.1 %copy-start.2 = (f32[128,8]{0,1:T(8,128)S(1)}, f32[128,8]{0,1:T(8,128)}, u32[]{:S(2)}) copy-start(f32[128,8]{0,1:T(8,128)} %param.18) | copy-start | bytes 12292
  51.7 27.2 %all-to-all-start.1 = ((bf16[16,32,2048]{2,1,0:T(8,128)(2,1)}), bf16[16,32,2048]{2,1,0:T(8,128)(2,1)S(1)}, u32[]{:S(2)}, u32[]{:S(2)}) async-start(bf16[16,32,2048]{2,1,0:T(8,128)(2,1)} %get-tuple-element.38), calls=%async_computation.1 | async-start | bytes 4194304 | tf_op jit(solution)/shard_map/all_to_all | solution.py:446
  55.6 7.3 %collective-permute-start = (bf16[4,2,96,128]{3,2,1,0:T(8,128)(2,1)S(1)}, bf16[4,2,96,128]{3,2,1,0:T(8,128)(2,1)S(1)}, u32[]{:S(2)}, u32[]{:S(2)}) collective-permute-start(bf16[4,2,96,128]{3,2,1,0:T(8,128)(2,1)S(1)} %copy-done.4), channel_id=1, source_target_pairs={{0,32},{16,48},{32,0},{48,16},{64,96},{80,112},{96,64},{112,80},{1... | collective-permute-start | bytes 589832 | tf_op jit(solution)/shard_map/ppermute | solution.py:449
  63.0 8.3 %collective-permute-start.1 = (bf16[2,96,128]{2,1,0:T(8,128)(2,1)S(1)}, bf16[2,96,128]{2,1,0:T(8,128)(2,1)S(1)}, u32[]{:S(2)}, u32[]{:S(2)}) collective-permute-start(bf16[2,96,128]{2,1,0:T(8,128)(2,1)S(1)} %get-tuple-element.48), channel_id=1, source_target_pairs={{0,128},{16,144},{32,160},{48,176},{64,192},{80,208},{96,224},{112... | collective-permute-start | bytes 147464 | tf_op jit(solution)/shard_map/ppermute | solution.py:449
  68.6 6.2 %collective-permute-start.3 = (bf16[2,96,128]{2,1,0:T(8,128)(2,1)S(1)}, bf16[2,96,128]{2,1,0:T(8,128)(2,1)S(1)}, u32[]{:S(2)}, u32[]{:S(2)}) collective-permute-start(bf16[2,96,128]{2,1,0:T(8,128)(2,1)S(1)} %get-tuple-element.49), channel_id=1, source_target_pairs={{0,192},{16,208},{32,224},{48,240},{64,128},{80,144},{96,160},{112... | collective-permute-start | bytes 147464 | tf_op jit(solution)/shard_map/ppermute | solution.py:449
  70.1 5.5 %collective-permute-start.2 = (bf16[2,96,128]{2,1,0:T(8,128)(2,1)S(1)}, bf16[2,96,128]{2,1,0:T(8,128)(2,1)S(1)}, u32[]{:S(2)}, u32[]{:S(2)}) collective-permute-start(bf16[2,96,128]{2,1,0:T(8,128)(2,1)S(1)} %get-tuple-element.50), channel_id=1, source_target_pairs={{0,64},{16,80},{32,96},{48,112},{64,0},{80,16},{96,32},{112,48},{1... | collective-permute-start | bytes 147464 | tf_op jit(solution)/shard_map/ppermute | solution.py:449
  75.7 1.3 %collective-permute-start.4 = (f32[96,128]{1,0:T(8,128)S(1)}, f32[96,128]{1,0:T(8,128)S(1)}, u32[]{:S(2)}, u32[]{:S(2)}) collective-permute-start(f32[96,128]{1,0:T(8,128)S(1)} %slice_bitcast_fusion.1), channel_id=1, source_target_pairs={{0,16},{16,0},{32,48},{48,32},{64,80},{80,64},{96,112},{112,96},{1... | collective-permute-start | bytes 147464 | tf_op jit(solution)/shard_map/ppermute | solution.py:449
  76.1 0.7 copy-start

commit v4 on v3

--- a/solution.py
+++ b/solution.py
@@ -7,6 +7,7 @@
 
 GROUP = 128
 FIRST_TO_FREEZE = 0
+SPLIT = (0,)
 CAP = 16
 SCALING = 0.5
 BF = jnp.bfloat16
@@ -136,15 +137,30 @@
     )(routes, gates)
 
 
-def combine_kernel(got_ref, table_hbm, mixed_hbm, grad_hbm, table_ref, mixed_ref, grad_ref, in_sem, out_sem):
+def combine_kernel(
+    got_ref, table_hbm, mine_ref, theirs_ref, mixed_hbm, grad_hbm, wide_hbm, narrow_hbm, table_ref, wide_ref, narrow_ref,
+    mixed_ref, grad_ref, in_sem, out_sem, wide_sem,
+):
     load = pltpu.make_async_copy(table_hbm, table_ref, in_sem)
     load.start()
+    total = mine_ref[...] + theirs_ref[...]
+    tall, column = wide_ref.shape
+    wide_ref[...] = total[:tall]
+    for i in range(narrow_ref.shape[2] // column):
+        for j in range(narrow_ref.shape[0]):
+            at = tall + 8 * i + j
+            narrow_ref[j, :, i * column : (i + 1) * column] = total[at : at + 1]
+    stores = [
+        pltpu.make_async_copy(wide_ref, wide_hbm, wide_sem.at[0]),
+        pltpu.make_async_copy(narrow_ref, narrow_hbm, wide_sem.at[1]),
+    ]
+    for store in stores:
+        store.start()
     experts = got_ref.shape[0]
     width = got_ref.shape[2]
     load.wait()
     one, high, low = table_ref[0], table_ref[1], table_ref[2]
     step = 512
-    stores = []
     for i, lo in enumerate(range(0, width, step)):
         cols = slice(lo, lo + step)
         out = got_ref[:, :CAP, cols].reshape(experts * CAP, step)
@@ -159,17 +175,21 @@
         store.wait()
 
 
-def combine(got, table):
+def combine(got, table, mine, theirs, tall, inner):
     shape = (table.shape[1], got.shape[2])
+    wide, narrow = (tall, mine.shape[1]), (3, 1, inner)
     return pl.pallas_call(
         combine_kernel,
-        out_shape=(pltpu.HBM(shape, BF),) * 2,
-        in_specs=[VMEM, HBM],
-        out_specs=(HBM,) * 2,
-        scratch_shapes=[pltpu.VMEM(table.shape, BF), pltpu.VMEM(shape, BF), pltpu.VMEM(shape, BF), DMA, DMA((2, 4))],
+        out_shape=(pltpu.HBM(shape, BF), pltpu.HBM(shape, BF), pltpu.HBM(wide, F32), pltpu.HBM(narrow, F32)),
+        in_specs=[VMEM, HBM, VMEM, VMEM],
+        out_specs=(HBM,) * 4,
+        scratch_shapes=[
+            pltpu.VMEM(table.shape, BF), pltpu.VMEM(wide, F32), pltpu.VMEM(narrow, F32), pltpu.VMEM(shape, BF),
+            pltpu.VMEM(shape, BF), DMA, DMA((2, 4)), DMA((2,)),
+        ],
         compiler_params=params(8),
         name="combine",
-    )(in_vmem(got), in_hbm(table))
+    )(in_vmem(got), in_hbm(table), mine, theirs)
 
 
 def freeze_kernel(group_ref, *refs):
@@ -229,6 +249,7 @@
 
     pairs = [(source, wide_ref.at[i * rank : (i + 1) * rank, :])
              for i, source in enumerate((gate_first_hbm, up_first_hbm, down_second_hbm))]
+    pairs += [(down_second_hbm, down_ref.at[inner : inner + rank, :])]
     pairs += [(source, narrow_ref.at[i * rank : (i + 1) * rank, :])
               for i, source in enumerate((gate_second_hbm, up_second_hbm, down_first_hbm))]
     small = [pltpu.make_async_copy(source, target, small_sem.at[i]) for i, (source, target) in enumerate(pairs)]
@@ -270,18 +291,19 @@
                 for copy in loads(weights, some):
                     copy.start()
 
-    start(pieces[:3])
-
-    def land(part):
-        for copy in loads(raw, pieces[3 * part : 3 * part + 3]):
+    start(pieces[:2])
+    down_ref[inner + rank :, :] = jnp.zeros((GROUP - rank, width), BF)
+
+    def land(part, kinds=(0, 1, 2)):
+        for copy in loads(raw, [(part, kind) for kind in kinds]):
             copy.wait()
 
         cols = slice(part * step, (part + 1) * step)
-        for target, scale_ref in ((gate_ref, gate_scale_ref), (up_ref, up_scale_ref)):
+        for target, scale_ref in ((gate_ref, gate_scale_ref), (up_ref, up_scale_ref)) if 0 in kinds else ():
             for i in range(width // GROUP):
                 group = slice(i * GROUP, (i + 1) * GROUP)
                 target[group, cols] = (target[group, cols].astype(F32) * scale_ref[i : i + 1, cols]).astype(BF)
-        for i in range(part * step // GROUP, (part + 1) * step // GROUP):
+        for i in range(part * step // GROUP, (part + 1) * step // GROUP) if 2 in kinds else ():
             group = slice(i * GROUP, (i + 1) * GROUP)
             down_ref[group, :] = (down_ref[group, :].astype(F32) * down_scale_ref[i]).astype(BF)
 
@@ -294,7 +316,7 @@
     down_first_ref = narrow_ref.at[2 * rank :, :]
     for copy in small:
         copy.wait()
-    start(pieces[3:])
+    start(pieces[2:])
 
     @pl.when(jnp.logical_not(ready))
     def _():
@@ -310,7 +332,9 @@
     back_up = jnp.zeros((rows, rank), F32)
     for index, (part, kind) in enumerate(pieces):
         if kind == 0:
-            land(part)
+            land(part, (0, 1) if part in SPLIT else (0, 1, 2))
+        if kind == 2 and part in SPLIT:
+            land(part, (2,))
         cols = slice(part * step, (part + 1) * step)
         if kind == 0:
             gate_pre = nn(x, gate_ref[:, cols]) + nn(gate_low * half, gate_second_ref[:, cols])
@@ -333,10 +357,11 @@
     down_low = down_low.astype(BF)
     back_both = jnp.concatenate([back_gate, back_up], axis=1).astype(BF)
     hidden, d_gate, d_up = inside_ref[0], inside_ref[1], inside_ref[2]
+    hidden_low = jnp.concatenate([hidden, down_low * half, jnp.zeros((rows, GROUP - rank), BF)], axis=1)
     stores = []
     for i, lo in enumerate(range(0, width, step)):
         cols = slice(lo, lo + step)
-        out = nn(hidden, down_ref[:, cols]) + nn(down_low * half, down_second_ref[:, cols])
+        out = nn(hidden_low, down_ref[:, cols])
         send_ref[:, :CAP, cols] = out.astype(BF).reshape(experts, CAP, step)
         back = nt(d_gate, gate_ref[cols, :]) + nt(d_up, up_ref[cols, :])
         back = back + nn(back_both * half, first_ref[:, cols])
@@ -398,12 +423,12 @@
         in_specs=[SMEM, VMEM] + [HBM] * 15,
         out_specs=(HBM,) * 3,
         scratch_shapes=[
-            *(pltpu.VMEM(level.shape, BF) for level in levels),
+            pltpu.VMEM(levels[0].shape, BF), pltpu.VMEM(levels[1].shape, BF), pltpu.VMEM((inner + GROUP, width), BF),
             *(pltpu.VMEM(scale.shape, F32) for scale in scales),
             pltpu.VMEM((3 * rank, width), BF), pltpu.VMEM((3 * rank, inner), BF),
             pltpu.VMEM(got.shape, BF), pltpu.VMEM((3, rows, inner), BF), pltpu.VMEM((groups, height, column), F32),
             pltpu.VMEM((groups, height, column), BF),
-            DMA((inner // 256, 3)), DMA((6,)), DMA((3,)), DMA((width // 256,)), DMA((groups // 2, 2)),
+            DMA((inner // 256, 3)), DMA((7,)), DMA((3,)), DMA((width // 256,)), DMA((groups // 2, 2)),
         ],
         compiler_params=params(32),
         name="expert",
@@ -451,13 +476,9 @@
     total = keep + swap(other, 2).astype(F32)
     sent = total.astype(BF)
     total = total[0] + (swap(sent[1], 8).astype(F32) + swap(sent[2], 4).astype(F32) + swap(sent[3], 12).astype(F32))
-    total = total[0] + swap(total[1], 1)
-    column = width // groups
-    grad_wide = total[: 3 * rank].reshape(1, 3, rank, column)
-    narrow = total[3 * rank :].reshape(inner // column, 8, column)[:, :3]
-    grad_narrow = narrow.transpose(1, 0, 2).reshape(1, 3, 1, inner)
-
-    mixed, input_grad = combine(back, table)
+    mixed, input_grad, grad_wide, grad_narrow = combine(back, table, total[0], swap(total[1], 1), 3 * rank, inner)
+    grad_wide = grad_wide.reshape(1, 3, rank, width // groups)
+    grad_narrow = grad_narrow.reshape(1, 3, 1, inner)
     return mixed, input_grad, grad_wide, grad_narrow
 
 

time: 82.4 us -> 81.5 us (0.989)
  local copies, waits for them, and re-layouts: 1.94 us -> 0.71 us
  waiting for transfers between devices: 13.5 us -> 14.7 us
    all_to_all x1, waiting for transfers between devices: 0.72 us -> 1.96 us  [shards(): lax.all_to_all(send, 'expert', split_axis=0, concat_axis=0, tiled=True)]
    reshape x2 -> x0, local copies, waits for them, and re-layouts: 1.23 us -> none  [the longest x1 0.61 us: shards(): grad_narrow = narrow.transpose(1, 0, 2).reshape(1, 3, 1, inner)]
  transfers between devices with their start and end apart: 6 -> 6, of which waited for: 6 -> 6; matrix products, arithmetic and copies ran while one was open for 2% -> 0% of each run, Pallas kernels for 0% -> 0%
where the time goes in v4:
time: 81.5 us; the launch traced here: 81.3 us
  blocking collectives  29 us (36%)
  Pallas kernels  24.4 us (30%)
  waiting for transfers between devices  14.7 us (18%)
  starting transfers between devices  11.4 us (14%)
  between operations  0.94 us (1%)
    all_to_all x1, blocking collectives, shards(): lax.all_to_all(send, 'expert', split_axis=0, concat_axis=0, tiled=True)  29 us
    ppermute x5, waiting for transfers between devices, swap(): return lax.ppermute(part, 'dp', [(i, i ^ mask) for i in range(groups)])  12.8 us
    pallas_call x1, Pallas kernels, expert(): pl.pallas_call(expert_kernel, out_shape=(pltpu.HBM(got.shape, BF), pltpu....  12 us
    ppermute x5, starting transfers between devices, swap(): return lax.ppermute(part, 'dp', [(i, i ^ mask) for i in range(groups)])  7.51 us
    pallas_call x1, Pallas kernels, freeze(): pl.pallas_call(freeze_kernel, out_shape=tuple((pltpu.HBM(level.shape, BF)...  6.88 us
    all_to_all x1, starting transfers between devices, shards(): lax.all_to_all(send, 'expert', split_axis=0, concat_axis=0, tiled=True)  3.86 us
    pallas_call x1, Pallas kernels, dispatch(): pl.pallas_call(dispatch_kernel, out_shape=pltpu.HBM(shape, BF), in_specs=...  2.94 us
    pallas_call x1, Pallas kernels, combine(): pl.pallas_call(combine_kernel, out_shape=(pltpu.HBM(shape, BF), pltpu.HBM...  2.29 us
  transfers between devices with their start and end apart: 6, of which 6 were waited for; matrix products, arithmetic and copies ran while one was open for 0% of the time, Pallas kernels for 0%

profile of v4, /device:TPU:32, one launch (start us, length us, event | category | flops | bytes accessed | tf_op | source)
XLA Modules:
  0.0 81.3 jit_solution(3589243891190752729)
XLA Ops:
  0.6 6.9 %freeze.1 = (bf16[2048,768]{1,0:T(8,128)(2,1)}, bf16[2048,768]{1,0:T(8,128)(2,1)}, bf16[768,2048]{1,0:T(8,128)(2,1)}) custom-call(s32[1]{0:T(128)} %bitcast.2.group_ref, bf16[2048,768]{1,0:T(8,128)(2,1)} %bitcast.35, bf16[2048,768]{1,0:T(8,128)(2,1)} %bitcast.37, bf16[768,2048]{1,0:T(8,128)(2,1)} %bitcast.39, f32[16,768]{1,0:T(8,128)} %bitcast.41, ...), custom_call_target="tpu_custom_call" | custom-call | flops 16777216 | bytes 16777216 | tf_op jit(solution)/shard_map/freeze/pallas_call | solution.py:222
  7.5 2.9 %dispatch.1 = bf16[16,32,2048]{2,1,0:T(8,128)(2,1)} custom-call(s32[8,128]{1,0:T(8,128)} %bitcast.31, f32[8,128]{1,0:T(8,128)} %bitcast.33, bf16[128,2048]{1,0:T(8,128)(2,1)} %act_hbm.1, bf16[128,2048]{1,0:T(8,128)(2,1)} %up_hbm.1), custom_call_target="tpu_custom_call" | custom-call | tf_op jit(solution)/shard_map/dispatch/pallas_call | solution.py:105
  10.5 29.0 %all_to_all.10.got_ref = bf16[16,32,2048]{2,1,0:T(8,128)(2,1)S(1)} all-to-all(bf16[16,32,2048]{2,1,0:T(8,128)(2,1)} %dispatch.1), channel_id=1, replica_groups=mesh['dp'=16,'expert'=16] {'expert'}, dimensions={0} | all-to-all | bytes 4194304 | tf_op jit(solution)/shard_map/all_to_all | solution.py:457
  39.5 12.0 %expert.1 = (bf16[16,32,2048]{2,1,0:T(8,128)(2,1)}, f32[4,2,96,128]{3,2,1,0:T(8,128)}, bf16[4,2,96,128]{3,2,1,0:T(8,128)(2,1)}) custom-call(s32[1]{0:T(128)} %bitcast.2.group_ref, bf16[16,32,2048]{2,1,0:T(8,128)(2,1)S(1)} %all_to_all.10.got_ref, bf16[2048,768]{1,0:T(8,128)(2,1)} %bitcast.36, bf16[2048,768]{1,0:T(8,128)(2,1)} %bitcast.38, ...), custom_call_target="tpu_custom_call" | custom-call | tf_op jit(solution)/shard_map/expert/pallas_call | solution.py:420
  51.5 0.0 copy-start.4
  51.5 0.0 copy-start.3
  51.5 0.0 copy-start.1
  51.6 0.0 copy-start.2
  51.6 3.9 %all-to-all-start.1 = ((bf16[16,32,2048]{2,1,0:T(8,128)(2,1)}), bf16[16,32,2048]{2,1,0:T(8,128)(2,1)S(1)}, u32[]{:S(2)}, u32[]{:S(2)}) async-start(bf16[16,32,2048]{2,1,0:T(8,128)(2,1)} %get-tuple-element.40), calls=%async_computation.1 | async-start | bytes 4194304 | tf_op jit(solution)/shard_map/all_to_all | solution.py:471
  55.4 0.0 copy-done.4
  55.4 0.2 collective-permute-start
  55.7 7.1 %collective-permute-done = bf16[4,2,96,128]{3,2,1,0:T(8,128)(2,1)S(1)} collective-permute-done((bf16[4,2,96,128]{3,2,1,0:T(8,128)(2,1)S(1)}, bf16[4,2,96,128]{3,2,1,0:T(8,128)(2,1)S(1)}, u32[]{:S(2)}, u32[]{:S(2)}) %collective-permute-start) | collective-permute-done | bytes 196640 | tf_op jit(solution)/shard_map/ppermute | solution.py:474
  62.8 0.0 copy-done.3
  62.8 0.1 fusion.1
  62.9 5.6 %collective-permute-start.1 = (bf16[2,96,128]{2,1,0:T(8,128)(2,1)S(1)}, bf16[2,96,128]{2,1,0:T(8,128)(2,1)S(1)}, u32[]{:S(2)}, u32[]{:S(2)}) collective-permute-start(bf16[2,96,128]{2,1,0:T(8,128)(2,1)S(1)} %get-tuple-element.52), channel_id=1, source_target_pairs={{0,128},{16,144},{32,160},{48,176},{64,192},{80,208},{96,224},{112... | collective-permute-start | bytes 147464 | tf_op jit(solution)/shard_map/ppermute | solution.py:474
  68.4 1.5 %collective-permute-start.3 = (bf16[2,96,128]{2,1,0:T(8,128)(2,1)S(1)}, bf16[2,96,128]{2,1,0:T(8,128)(2,1)S(1)}, u32[]{:S(2)}, u32[]{:S(2)}) collective-permute-start(bf16[2,96,128]{2,1,0:T(8,128)(2,1)S(1)} %get-tuple-element.53), channel_id=1, source_target_pairs={{0,192},{16,208},{32,224},{48,240},{64,128},{80,144},{96,160},{112... | collective-permute-start | bytes 147464 | tf_op jit(solution)/shard_map/ppermute | solution.py:474
  70.0 0.1 collective-permute-start.2
  70.1 1.1 %collective-permute-done.1 = bf16[2,96,128]{2,1,0:T(8,128)(2,1)S(1)} collective-permute-done((bf16[2,96,128]{2,1,0:T(8,128)(2,1)S(1)}, bf16[2,96,128]{2,1,0:T(8,128)(2,1)S(1)}, u32[]{:S(2)}, u32[]{:S(2)}) %collective-permute-start.1) | collective-permute-done | bytes 49184 | tf_op jit(solution)/shard_map/ppermute | solution.py:474
  71.1 3.5 %collective-permute-done.3 = bf16[2,96,128]{2,1,0:T(8,128)(2,1)S(1)} collective-permute-done((bf16[2,96,128]{2,1,0:T(8,128)(2,1)S(1)}, bf16[2,96,128]{2,1,0:T(8,128)(2,1)S(1)}, u32[]{:S(2)}, u32[]{:S(2)}) %collective-permute-start.3) | collective-permute-done | bytes 49184 | tf_op jit(solution)/shard_map/ppermute | solution.py:474
  74.6 0.8 %collective-permute-done.2 = bf16[2,96,128]{2,1,0:T(8,128)(2,1)S(1)} collective-permute-done((bf16[2,96,128]{2,1,0:T(8,128)(2,1)S(1)}, bf16[2,96,128]{2,1,0:T(8,128)(2,1)S(1)}, u32[]{:S(2)}, u32[]{:S(2)}) %collective-permute-start.2) | collective-permute-done | bytes 49184 | tf_op jit(solution)/shard_map/ppermute | solution.py:474
  75.5 0.1 collective-permute-start.4
  75.6 0.0 copy-done.1
  75.6 0.0 copy-done.2
  75.7 0.3 tables.1.table_hbm
  75.9 0.0 copy-start
  75.9 0.7 copy-done
  76.6 0.2 collective-permute-done.4.theirs_ref
  76.8 2.0 %all-to-all-done.1.got_ref = bf16[16,32,2048]{2,1,0:T(8,128)(2,1)S(1)} async-done(((bf16[16,32,2048]{2,1,0:T(8,128)(2,1)}), bf16[16,32,2048]{2,1,0:T(8,128)(2,1)S(1)}, u32[]{:S(2)}, u32[]{:S(2)}) %all-to-all-start.1) | async-done | bytes 2097184 | tf_op jit(solution)/shard_map/all_to_all | solution.py:471
  78.8 2.3 %combine.1 = (bf16[128,2048]{1,0:T(8,128)(2,1)}, bf16[128,2048]{1,0:T(8,128)(2,1)}, f32[48,128]{1,0:T(8,128)}, f32[3,1,768]{2,1,0:T(1,128)}) custom-call(bf16[16,32,2048]{2,1,0:T(8,128)(2,1)S(1)} %all-to-all-done.1.got_ref, bf16[3,128,256]{2,1,0:T(8,128)(2,1)} %copy-done, f32[96,128]{1,0:T(8,128)S(1)} %get-tuple-element.56.mine_ref, ...), custom_call_target="tpu_custom_call" | custom-call | tf_op jit(solution)/shard_map/combine/pallas_call | solution.py:181
  (3 shorter events, 0.0 us)
Async XLA Ops:
  51.5 3.9 %copy-start.4 = (bf16[4,2,96,128]{3,2,1,0:T(8,128)(2,1)S(1)}, bf16[4,2,96,128]{3,2,1,0:T(8,128)(2,1)}, u32[]{:S(2)}) copy-start(bf16[4,2,96,128]{3,2,1,0:T(8,128)(2,1)} %get-tuple-element.45) | copy-start | bytes 589828
  51.5 11.3 %copy-start.3 = (f32[4,2,96,128]{3,2,1,0:T(8,128)S(1)}, f32[4,2,96,128]{3,2,1,0:T(8,128)}, u32[]{:S(2)}) copy-start(f32[4,2,96,128]{3,2,1,0:T(8,128)} %get-tuple-element.44) | copy-start | bytes 1179652
  51.5 24.1 %copy-start.1 = (s32[128,8]{0,1:T(8,128)S(1)}, s32[128,8]{0,1:T(8,128)}, u32[]{:S(2)}) copy-start(s32[128,8]{0,1:T(8,128)} %param.17) | copy-start | bytes 12292
  51.6 24.1 %copy-start.2 = (f32[128,8]{0,1:T(8,128)S(1)}, f32[128,8]{0,1:T(8,128)}, u32[]{:S(2)}) copy-start(f32[128,8]{0,1:T(8,128)} %param.18) | copy-start | bytes 12292
  51.6 27.2 %all-to-all-start.1 = ((bf16[16,32,2048]{2,1,0:T(8,128)(2,1)}), bf16[16,32,2048]{2,1,0:T(8,128)(2,1)S(1)}, u32[]{:S(2)}, u32[]{:S(2)}) async-start(bf16[16,32,2048]{2,1,0:T(8,128)(2,1)} %get-tuple-element.40), calls=%async_computation.1 | async-start | bytes 4194304 | tf_op jit(solution)/shard_map/all_to_all | solution.py:471
  55.4 7.3 %collective-permute-start = (bf16[4,2,96,128]{3,2,1,0:T(8,128)(2,1)S(1)}, bf16[4,2,96,128]{3,2,1,0:T(8,128)(2,1)S(1)}, u32[]{:S(2)}, u32[]{:S(2)}) collective-permute-start(bf16[4,2,96,128]{3,2,1,0:T(8,128)(2,1)S(1)} %copy-done.4), channel_id=1, source_target_pairs={{0,32},{16,48},{32,0},{48,16},{64,96},{80,112},{96,64},{112,80},{1... | collective-permute-start | bytes 589832 | tf_op jit(solution)/shard_map/ppermute | solution.py:474
  62.9 8.3 %collective-permute-start.1 = (bf16[2,96,128]{2,1,0:T(8,128)(2,1)S(1)}, bf16[2,96,128]{2,1,0:T(8,128)(2,1)S(1)}, u32[]{:S(2)}, u32[]{:S(2)}) collective-permute-start(bf16[2,96,128]{2,1,0:T(8,128)(2,1)S(1)} %get-tuple-element.52), channel_id=1, source_target_pairs={{0,128},{16,144},{32,160},{48,176},{64,192},{80,208},{96,224},{112... | collective-permute-start | bytes 147464 | tf_op jit(solution)/shard_map/ppermute | solution.py:474
  68.4 6.2 %collective-permute-start.3 = (bf16[2,96,128]{2,1,0:T(8,128)(2,1)S(1)}, bf16[2,96,128]{2,1,0:T(8,128)(2,1)S(1)}, u32[]{:S(2)}, u32[]{:S(2)}) collective-permute-start(bf16[2,96,128]{2,1,0:T(8,128)(2,1)S(1)} %get-tuple-element.53), channel_id=1, source_target_pairs={{0,192},{16,208},{32,224},{48,240},{64,128},{80,144},{96,160},{112... | collective-permute-start | bytes 147464 | tf_op jit(solution)/shard_map/ppermute | solution.py:474
  70.0 5.5 %collective-permute-start.2 = (bf16[2,96,128]{2,1,0:T(8,128)(2,1)S(1)}, bf16[2,96,128]{2,1,0:T(8,128)(2,1)S(1)}, u32[]{:S(2)}, u32[]{:S(2)}) collective-permute-start(bf16[2,96,128]{2,1,0:T(8,128)(2,1)S(1)} %get-tuple-element.54), channel_id=1, source_target_pairs={{0,64},{16,80},{32,96},{48,112},{64,0},{80,16},{96,32},{112,48},{1... | collective-permute-start | bytes 147464 | tf_op jit(solution)/shard_map/ppermute | solution.py:474
  75.5 1.3 %collective-permute-start.4 = (f32[96,128]{1,0:T(8,128)S(1)}, f32[96,128]{1,0:T(8,128)S(1)}, u32[]{:S(2)}, u32[]{:S(2)}) collective-permute-start(f32[96,128]{1,0:T(8,128)S(1)} %get-tuple-element.55), channel_id=1, source_target_pairs={{0,16},{16,0},{32,48},{48,32},{64,80},{80,64},{96,112},{112,96},{1... | collective-permute-start | bytes 147464 | tf_op jit(solution)/shard_map/ppermute | solution.py:474
  75.9 0.7 copy-start

commit v5 on v4

--- a/solution.py
+++ b/solution.py
@@ -193,45 +193,49 @@
 
 
 def freeze_kernel(group_ref, *refs):
-    levels, scales, frozen = refs[:3], refs[3:6], refs[-11:-8]
-    level_refs, scale_refs = refs[-8:-5], refs[-5:-2]
-    in_sem, out_sem = refs[-2:]
+    levels, scales, adapters, frozen = refs[:3], refs[3:6], refs[6:12], refs[12:15]
+    level_refs, scale_refs, adapter_refs = refs[15:18], refs[18:21], refs[21:27]
+    in_sem, out_sem = refs[27:]
 
     @pl.when(group_ref[0] % 2 == FIRST_TO_FREEZE)
     def _():
         loads = [pltpu.make_async_copy(*pair, in_sem.at[i])
-                 for i, pair in enumerate((*zip(scales, scale_refs), *zip(levels, level_refs)))]
+                 for i, pair in enumerate((*zip(scales, scale_refs), *zip(adapters, adapter_refs), *zip(levels, level_refs)))]
         for load in loads:
             load.start()
-        for load in loads[:3]:
+        for load in loads[:9]:
             load.wait()
+        firsts = (adapter_refs[0], adapter_refs[1], adapter_refs[5])
+        seconds = (adapter_refs[3], adapter_refs[4], adapter_refs[2])
         stores = []
         for i, (level_ref, scale_ref) in enumerate(zip(level_refs, scale_refs)):
-            loads[3 + i].wait()
+            loads[9 + i].wait()
             for j in range(scale_ref.shape[0]):
                 rows = slice(j * GROUP, (j + 1) * GROUP)
                 scale = scale_ref[j] if len(scale_ref.shape) == 3 else scale_ref[j : j + 1, :]
-                level_ref[rows, :] = (level_ref[rows, :].astype(F32) * scale).astype(BF)
+                weight = (level_ref[rows, :].astype(F32) * scale).astype(BF)
+                low = tn(firsts[i][:, rows], seconds[i][...])
+                level_ref[rows, :] = (weight.astype(F32) + SCALING * low).astype(BF)
             stores.append(pltpu.make_async_copy(level_ref, frozen[i], out_sem.at[i]))
             stores[-1].start()
         for store in stores:
             store.wait()
 
 
-def freeze(group, levels, scales):
+def freeze(group, levels, scales, adapters):
     return pl.pallas_call(
         freeze_kernel,
         out_shape=tuple(pltpu.HBM(level.shape, BF) for level in levels),
-        in_specs=[SMEM] + [HBM] * 6,
+        in_specs=[SMEM] + [HBM] * 12,
         out_specs=(HBM,) * 3,
         scratch_shapes=[
             *(pltpu.VMEM(level.shape, BF) for level in levels), *(pltpu.VMEM(scale.shape, F32) for scale in scales),
-            DMA((6,)), DMA((3,)),
+            *(pltpu.VMEM(adapter.shape, BF) for adapter in adapters), DMA((12,)), DMA((3,)),
         ],
         compiler_params=params(16),
         cost_estimate=cost(1 << 24, 1 << 24),
         name="freeze",
-    )(group, *(in_hbm(array) for array in (*levels, *scales)))
+    )(group, *(in_hbm(array) for array in (*levels, *scales, *adapters)))
 
 
 def expert_kernel(
@@ -239,7 +243,7 @@
     gate_scale_hbm, up_scale_hbm, down_scale_hbm, gate_first_hbm, up_first_hbm, down_second_hbm,
     gate_second_hbm, up_second_hbm, down_first_hbm, send_hbm, keep_hbm, other_hbm,
     gate_ref, up_ref, down_ref, gate_scale_ref, up_scale_ref, down_scale_ref, wide_ref, narrow_ref, send_ref,
-    inside_ref, piece_ref, rounded_ref, level_sem, small_sem, scale_sem, out_sem, piece_sem,
+    inside_ref, down_low_ref, back_both_ref, piece_ref, rounded_ref, level_sem, small_sem, scale_sem, out_sem, piece_sem,
 ):
     experts, _, width = got_ref.shape
     rows = experts * CAP
@@ -273,11 +277,6 @@
     scale_loads = [pltpu.make_async_copy(source, target, scale_sem.at[i]) for i, (source, target) in enumerate(
         zip((gate_scale_hbm, up_scale_hbm, down_scale_hbm), scales))]
 
-    @pl.when(ready)
-    def _():
-        for scale_ref in scales:
-            scale_ref[...] = jnp.ones_like(scale_ref)
-
     @pl.when(jnp.logical_not(ready))
     def _():
         for copy in scale_loads:
@@ -294,10 +293,11 @@
     start(pieces[:2])
     down_ref[inner + rank :, :] = jnp.zeros((GROUP - rank, width), BF)
 
-    def land(part, kinds=(0, 1, 2)):
+    def land(part, kinds, folded):
         for copy in loads(raw, [(part, kind) for kind in kinds]):
             copy.wait()
-
+        if folded:
+            return
         cols = slice(part * step, (part + 1) * step)
         for target, scale_ref in ((gate_ref, gate_scale_ref), (up_ref, up_scale_ref)) if 0 in kinds else ():
             for i in range(width // GROUP):
@@ -327,49 +327,74 @@
     gate_low, up_low = first_low[:, :rank], first_low[:, rank:]
     back_down = nt(g, down_second_ref[...]).astype(BF)
     half = jnp.asarray(SCALING, BF)
-    down_low = jnp.zeros((rows, rank), F32)
-    back_gate = jnp.zeros((rows, rank), F32)
-    back_up = jnp.zeros((rows, rank), F32)
-    for index, (part, kind) in enumerate(pieces):
-        if kind == 0:
-            land(part, (0, 1) if part in SPLIT else (0, 1, 2))
-        if kind == 2 and part in SPLIT:
-            land(part, (2,))
-        cols = slice(part * step, (part + 1) * step)
-        if kind == 0:
-            gate_pre = nn(x, gate_ref[:, cols]) + nn(gate_low * half, gate_second_ref[:, cols])
-            logistic = jax.nn.sigmoid(gate_pre)
-            activated = gate_pre * logistic
-            slope = logistic * (1.0 + gate_pre * (1.0 - logistic))
-        elif kind == 1:
-            up_pre = nn(x, up_ref[:, cols]) + nn(up_low * half, up_second_ref[:, cols])
-            hidden = (activated * up_pre).astype(BF)
-            inside_ref[0, :, cols] = hidden
-            down_low += nt(hidden, down_first_ref[:, cols])
-        else:
-            d_hidden = nt(g, down_ref[cols, :]) + nn(back_down * half, down_first_ref[:, cols])
-            d_gate = (d_hidden * up_pre * slope).astype(BF)
-            d_up = (d_hidden * activated).astype(BF)
-            inside_ref[1, :, cols] = d_gate
-            inside_ref[2, :, cols] = d_up
-            back_gate += nt(d_gate, gate_second_ref[:, cols])
-            back_up += nt(d_up, up_second_ref[:, cols])
-    down_low = down_low.astype(BF)
-    back_both = jnp.concatenate([back_gate, back_up], axis=1).astype(BF)
+    sends = {}
+    for index, hi in enumerate(SPLITS):
+        cols = slice(hi - SPLITS[hi], hi)
+        sends[hi] = pltpu.make_async_copy(send_ref.at[:, :, cols], send_hbm.at[:, :, cols], out_sem.at[index])
+
+    def both_ways(folded):
+        down_low = jnp.zeros((rows, rank), F32)
+        back_gate = jnp.zeros((rows, rank), F32)
+        back_up = jnp.zeros((rows, rank), F32)
+        for part, kind in pieces:
+            if kind == 0:
+                land(part, (0, 1) if part in SPLIT else (0, 1, 2), folded)
+            if kind == 2 and part in SPLIT:
+                land(part, (2,), folded)
+            cols = slice(part * step, (part + 1) * step)
+            if kind == 0:
+                gate_pre = nn(x, gate_ref[:, cols])
+                if not folded:
+                    gate_pre = gate_pre + nn(gate_low * half, gate_second_ref[:, cols])
+                logistic = jax.nn.sigmoid(gate_pre)
+                activated = gate_pre * logistic
+                slope = logistic * (1.0 + gate_pre * (1.0 - logistic))
+            elif kind == 1:
+                up_pre = nn(x, up_ref[:, cols])
+                if not folded:
+                    up_pre = up_pre + nn(up_low * half, up_second_ref[:, cols])
+                hidden = (activated * up_pre).astype(BF)
+                inside_ref[0, :, cols] = hidden
+                down_low += nt(hidden, down_first_ref[:, cols])
+            else:
+                d_hidden = nt(g, down_ref[cols, :])
+                if not folded:
+                    d_hidden = d_hidden + nn(back_down * half, down_first_ref[:, cols])
+                d_gate = (d_hidden * up_pre * slope).astype(BF)
+                d_up = (d_hidden * activated).astype(BF)
+                inside_ref[1, :, cols] = d_gate
+                inside_ref[2, :, cols] = d_up
+                back_gate += nt(d_gate, gate_second_ref[:, cols])
+                back_up += nt(d_up, up_second_ref[:, cols])
+        down_low = down_low.astype(BF)
+        back_both = jnp.concatenate([back_gate, back_up], axis=1).astype(BF)
+        down_low_ref[...] = down_low
+        back_both_ref[...] = back_both
+        hidden, d_gate, d_up = inside_ref[0], inside_ref[1], inside_ref[2]
+        if not folded:
+            hidden = jnp.concatenate([hidden, down_low * half, jnp.zeros((rows, GROUP - rank), BF)], axis=1)
+        for lo in range(0, width, step):
+            cols = slice(lo, lo + step)
+            out = nn(hidden, down_ref[: hidden.shape[1], cols])
+            send_ref[:, :CAP, cols] = out.astype(BF).reshape(experts, CAP, step)
+            back = nt(d_gate, gate_ref[cols, :]) + nt(d_up, up_ref[cols, :])
+            if not folded:
+                back = back + nn(back_both * half, first_ref[:, cols])
+            send_ref[:, CAP:, cols] = back.astype(BF).reshape(experts, CAP, step)
+            if lo + step in SPLITS:
+                sends[lo + step].start()
+
+    @pl.when(ready)
+    def _():
+        both_ways(True)
+
+    @pl.when(jnp.logical_not(ready))
+    def _():
+        both_ways(False)
+
+    stores = list(sends.values())
     hidden, d_gate, d_up = inside_ref[0], inside_ref[1], inside_ref[2]
-    hidden_low = jnp.concatenate([hidden, down_low * half, jnp.zeros((rows, GROUP - rank), BF)], axis=1)
-    stores = []
-    for i, lo in enumerate(range(0, width, step)):
-        cols = slice(lo, lo + step)
-        out = nn(hidden_low, down_ref[:, cols])
-        send_ref[:, :CAP, cols] = out.astype(BF).reshape(experts, CAP, step)
-        back = nt(d_gate, gate_ref[cols, :]) + nt(d_up, up_ref[cols, :])
-        back = back + nn(back_both * half, first_ref[:, cols])
-        send_ref[:, CAP:, cols] = back.astype(BF).reshape(experts, CAP, step)
-        if lo + step in SPLITS:
-            cols = slice(lo + step - SPLITS[lo + step], lo + step)
-            stores.append(pltpu.make_async_copy(send_ref.at[:, :, cols], send_hbm.at[:, :, cols], out_sem.at[i]))
-            stores[-1].start()
+    down_low, back_both = down_low_ref[...], back_both_ref[...]
     groups = piece_ref.shape[0]
     column = width // groups
     for lo in range(0, width, 512):
@@ -426,7 +451,8 @@
             pltpu.VMEM(levels[0].shape, BF), pltpu.VMEM(levels[1].shape, BF), pltpu.VMEM((inner + GROUP, width), BF),
             *(pltpu.VMEM(scale.shape, F32) for scale in scales),
             pltpu.VMEM((3 * rank, width), BF), pltpu.VMEM((3 * rank, inner), BF),
-            pltpu.VMEM(got.shape, BF), pltpu.VMEM((3, rows, inner), BF), pltpu.VMEM((groups, height, column), F32),
+            pltpu.VMEM(got.shape, BF), pltpu.VMEM((3, rows, inner), BF), pltpu.VMEM((rows, rank), BF),
+            pltpu.VMEM((rows, 2 * rank), BF), pltpu.VMEM((groups, height, column), F32),
             pltpu.VMEM((groups, height, column), BF),
             DMA((inner // 256, 3)), DMA((7,)), DMA((3,)), DMA((width // 256,)), DMA((groups // 2, 2)),
         ],
@@ -450,7 +476,9 @@
     group = lax.axis_index("dp").astype(jnp.int32).reshape(1)
     levels = (gate_levels[0], up_levels[0], down_levels[0])
     scales = (gate_scales[0], up_scales[0], down_scales.transpose(1, 0, 2))
-    frozen = freeze(group, levels, scales)
+    wide = (gate_adapter_first[0], up_adapter_first[0], down_adapter_second[0])
+    narrow = (gate_adapter_second[0], up_adapter_second[0], down_adapter_first[0])
+    frozen = freeze(group, levels, scales, wide + narrow)
     routes, gates, frozen = lax.optimization_barrier((routes, gates, frozen))
     send = dispatch(routes, gates, activations, upstream, experts)
     send, group, frozen = lax.optimization_barrier((send, group, frozen))
@@ -463,8 +491,8 @@
         levels,
         frozen,
         scales,
-        (gate_adapter_first[0], up_adapter_first[0], down_adapter_second[0]),
-        (gate_adapter_second[0], up_adapter_second[0], down_adapter_first[0]),
+        wide,
+        narrow,
     )
     routes, gates, keep = lax.optimization_barrier((routes, gates, keep))
     table = tables(routes, gates, experts)

time: 81.5 us -> 80 us (0.982)
  blocking collectives: 29 us -> 27.1 us
  Pallas kernels: 24.4 us -> 25.7 us
    all_to_all x1, blocking collectives: 29 us -> 27.1 us  [shards(): lax.all_to_all(send, 'expert', split_axis=0, concat_axis=0, tiled=True)]
    pallas_call x1, Pallas kernels: 6.88 us -> 8.72 us  [freeze(): pl.pallas_call(freeze_kernel, out_shape=tuple((pltpu.HBM(level.shape, BF)...]
    ppermute x5, waiting for transfers between devices: 12.8 us -> 11.5 us  [swap(): return lax.ppermute(part, 'dp', [(i, i ^ mask) for i in range(groups)])]
  transfers between devices with their start and end apart: 6 -> 6, of which waited for: 6 -> 5; matrix products, arithmetic and copies ran while one was open for 0% -> 0% of each run, Pallas kernels for 0% -> 0%
where the time goes in v5:
time: 80 us; the launch traced here: 79.6 us
  blocking collectives  27.1 us (34%)
  Pallas kernels  25.7 us (32%)
  waiting for transfers between devices  14 us (18%)
  starting transfers between devices  11.1 us (14%)
  between operations  0.94 us (1%)
    all_to_all x1, blocking collectives, shards(): lax.all_to_all(send, 'expert', split_axis=0, concat_axis=0, tiled=True)  27.1 us
    ppermute x5, waiting for transfers between devices, swap(): return lax.ppermute(part, 'dp', [(i, i ^ mask) for i in range(groups)])  11.5 us
    pallas_call x1, Pallas kernels, expert(): pl.pallas_call(expert_kernel, out_shape=(pltpu.HBM(got.shape, BF), pltpu....  11.5 us
    pallas_call x1, Pallas kernels, freeze(): pl.pallas_call(freeze_kernel, out_shape=tuple((pltpu.HBM(level.shape, BF)...  8.72 us
    ppermute x5, starting transfers between devices, swap(): return lax.ppermute(part, 'dp', [(i, i ^ mask) for i in range(groups)])  7.19 us
    all_to_all x1, starting transfers between devices, shards(): lax.all_to_all(send, 'expert', split_axis=0, concat_axis=0, tiled=True)  3.86 us
    pallas_call x1, Pallas kernels, dispatch(): pl.pallas_call(dispatch_kernel, out_shape=pltpu.HBM(shape, BF), in_specs=...  2.94 us
    all_to_all x1, waiting for transfers between devices, shards(): lax.all_to_all(send, 'expert', split_axis=0, concat_axis=0, tiled=True)  2.5 us
  transfers between devices with their start and end apart: 6, of which 5 were waited for; matrix products, arithmetic and copies ran while one was open for 0% of the time, Pallas kernels for 0%

profile of v5, /device:TPU:32, one launch (start us, length us, event | category | flops | bytes accessed | tf_op | source)
XLA Modules:
  0.0 79.6 jit_solution(3646399575478632004)
XLA Ops:
  0.6 8.7 %freeze.1 = (bf16[2048,768]{1,0:T(8,128)(2,1)}, bf16[2048,768]{1,0:T(8,128)(2,1)}, bf16[768,2048]{1,0:T(8,128)(2,1)}) custom-call(s32[1]{0:T(128)} %bitcast.2.group_ref, bf16[2048,768]{1,0:T(8,128)(2,1)} %bitcast.35, bf16[2048,768]{1,0:T(8,128)(2,1)} %bitcast.37, bf16[768,2048]{1,0:T(8,128)(2,1)} %bitcast.39, f32[16,768]{1,0:T(8,128)} %bitcast.47, ...), custom_call_target="tpu_custom_call" | custom-call | flops 16777216 | bytes 16777216 | tf_op jit(solution)/shard_map/freeze/pallas_call | solution.py:226
  9.4 2.9 %dispatch.1 = bf16[16,32,2048]{2,1,0:T(8,128)(2,1)} custom-call(s32[8,128]{1,0:T(8,128)} %bitcast.31, f32[8,128]{1,0:T(8,128)} %bitcast.33, bf16[128,2048]{1,0:T(8,128)(2,1)} %act_hbm.1, bf16[128,2048]{1,0:T(8,128)(2,1)} %up_hbm.1), custom_call_target="tpu_custom_call" | custom-call | tf_op jit(solution)/shard_map/dispatch/pallas_call | solution.py:105
  12.3 27.1 %all_to_all.10.got_ref = bf16[16,32,2048]{2,1,0:T(8,128)(2,1)S(1)} all-to-all(bf16[16,32,2048]{2,1,0:T(8,128)(2,1)} %dispatch.1), channel_id=1, replica_groups=mesh['dp'=16,'expert'=16] {'expert'}, dimensions={0} | all-to-all | bytes 4194304 | tf_op jit(solution)/shard_map/all_to_all | solution.py:485
  39.4 11.5 %expert.1 = (bf16[16,32,2048]{2,1,0:T(8,128)(2,1)}, f32[4,2,96,128]{3,2,1,0:T(8,128)}, bf16[4,2,96,128]{3,2,1,0:T(8,128)(2,1)}) custom-call(s32[1]{0:T(128)} %bitcast.2.group_ref, bf16[16,32,2048]{2,1,0:T(8,128)(2,1)S(1)} %all_to_all.10.got_ref, bf16[2048,768]{1,0:T(8,128)(2,1)} %bitcast.36, bf16[2048,768]{1,0:T(8,128)(2,1)} %bitcast.38, ...), custom_call_target="tpu_custom_call" | custom-call | tf_op jit(solution)/shard_map/expert/pallas_call | solution.py:445
  50.9 0.0 copy-start.4
  50.9 0.0 copy-start.3
  50.9 0.0 copy-start.1
  51.0 0.0 copy-start.2
  51.0 3.9 %all-to-all-start.1 = ((bf16[16,32,2048]{2,1,0:T(8,128)(2,1)}), bf16[16,32,2048]{2,1,0:T(8,128)(2,1)S(1)}, u32[]{:S(2)}, u32[]{:S(2)}) async-start(bf16[16,32,2048]{2,1,0:T(8,128)(2,1)} %get-tuple-element.40), calls=%async_computation.1 | async-start | bytes 4194304 | tf_op jit(solution)/shard_map/all_to_all | solution.py:499
  54.8 0.0 copy-done.4
  54.8 0.2 collective-permute-start
  55.0 7.0 %collective-permute-done = bf16[4,2,96,128]{3,2,1,0:T(8,128)(2,1)S(1)} collective-permute-done((bf16[4,2,96,128]{3,2,1,0:T(8,128)(2,1)S(1)}, bf16[4,2,96,128]{3,2,1,0:T(8,128)(2,1)S(1)}, u32[]{:S(2)}, u32[]{:S(2)}) %collective-permute-start) | collective-permute-done | bytes 196640 | tf_op jit(solution)/shard_map/ppermute | solution.py:502
  62.0 0.0 copy-done.3
  62.0 0.1 fusion.1
  62.1 5.0 %collective-permute-start.1 = (bf16[2,96,128]{2,1,0:T(8,128)(2,1)S(1)}, bf16[2,96,128]{2,1,0:T(8,128)(2,1)S(1)}, u32[]{:S(2)}, u32[]{:S(2)}) collective-permute-start(bf16[2,96,128]{2,1,0:T(8,128)(2,1)S(1)} %get-tuple-element.52), channel_id=1, source_target_pairs={{0,128},{16,144},{32,160},{48,176},{64,192},{80,208},{96,224},{112... | collective-permute-start | bytes 147464 | tf_op jit(solution)/shard_map/ppermute | solution.py:502
  67.1 0.8 %collective-permute-start.3 = (bf16[2,96,128]{2,1,0:T(8,128)(2,1)S(1)}, bf16[2,96,128]{2,1,0:T(8,128)(2,1)S(1)}, u32[]{:S(2)}, u32[]{:S(2)}) collective-permute-start(bf16[2,96,128]{2,1,0:T(8,128)(2,1)S(1)} %get-tuple-element.53), channel_id=1, source_target_pairs={{0,192},{16,208},{32,224},{48,240},{64,128},{80,144},{96,160},{112... | collective-permute-start | bytes 147464 | tf_op jit(solution)/shard_map/ppermute | solution.py:502
  67.9 1.1 %collective-permute-start.2 = (bf16[2,96,128]{2,1,0:T(8,128)(2,1)S(1)}, bf16[2,96,128]{2,1,0:T(8,128)(2,1)S(1)}, u32[]{:S(2)}, u32[]{:S(2)}) collective-permute-start(bf16[2,96,128]{2,1,0:T(8,128)(2,1)S(1)} %get-tuple-element.54), channel_id=1, source_target_pairs={{0,64},{16,80},{32,96},{48,112},{64,0},{80,16},{96,32},{112,48},{1... | collective-permute-start | bytes 147464 | tf_op jit(solution)/shard_map/ppermute | solution.py:502
  69.0 1.2 %collective-permute-done.1 = bf16[2,96,128]{2,1,0:T(8,128)(2,1)S(1)} collective-permute-done((bf16[2,96,128]{2,1,0:T(8,128)(2,1)S(1)}, bf16[2,96,128]{2,1,0:T(8,128)(2,1)S(1)}, u32[]{:S(2)}, u32[]{:S(2)}) %collective-permute-start.1) | collective-permute-done | bytes 49184 | tf_op jit(solution)/shard_map/ppermute | solution.py:502
  70.2 3.1 %collective-permute-done.3 = bf16[2,96,128]{2,1,0:T(8,128)(2,1)S(1)} collective-permute-done((bf16[2,96,128]{2,1,0:T(8,128)(2,1)S(1)}, bf16[2,96,128]{2,1,0:T(8,128)(2,1)S(1)}, u32[]{:S(2)}, u32[]{:S(2)}) %collective-permute-start.3) | collective-permute-done | bytes 49184 | tf_op jit(solution)/shard_map/ppermute | solution.py:502
  73.3 0.0 collective-permute-done.2
  73.4 0.1 collective-permute-start.4
  73.5 0.0 copy-done.1
  73.5 0.0 copy-done.2
  73.5 0.3 tables.1.table_hbm
  73.8 0.0 copy-start
  73.8 0.7 copy-done
  74.4 0.2 collective-permute-done.4.theirs_ref
  74.7 2.5 %all-to-all-done.1.got_ref = bf16[16,32,2048]{2,1,0:T(8,128)(2,1)S(1)} async-done(((bf16[16,32,2048]{2,1,0:T(8,128)(2,1)}), bf16[16,32,2048]{2,1,0:T(8,128)(2,1)S(1)}, u32[]{:S(2)}, u32[]{:S(2)}) %all-to-all-start.1) | async-done | bytes 2097184 | tf_op jit(solution)/shard_map/all_to_all | solution.py:499
  77.2 2.3 %combine.1 = (bf16[128,2048]{1,0:T(8,128)(2,1)}, bf16[128,2048]{1,0:T(8,128)(2,1)}, f32[48,128]{1,0:T(8,128)}, f32[3,1,768]{2,1,0:T(1,128)}) custom-call(bf16[16,32,2048]{2,1,0:T(8,128)(2,1)S(1)} %all-to-all-done.1.got_ref, bf16[3,128,256]{2,1,0:T(8,128)(2,1)} %copy-done, f32[96,128]{1,0:T(8,128)S(1)} %get-tuple-element.56.mine_ref, ...), custom_call_target="tpu_custom_call" | custom-call | tf_op jit(solution)/shard_map/combine/pallas_call | solution.py:181
  (3 shorter events, 0.0 us)
Async XLA Ops:
  50.9 3.9 %copy-start.4 = (bf16[4,2,96,128]{3,2,1,0:T(8,128)(2,1)S(1)}, bf16[4,2,96,128]{3,2,1,0:T(8,128)(2,1)}, u32[]{:S(2)}) copy-start(bf16[4,2,96,128]{3,2,1,0:T(8,128)(2,1)} %get-tuple-element.45) | copy-start | bytes 589828
  50.9 11.1 %copy-start.3 = (f32[4,2,96,128]{3,2,1,0:T(8,128)S(1)}, f32[4,2,96,128]{3,2,1,0:T(8,128)}, u32[]{:S(2)}) copy-start(f32[4,2,96,128]{3,2,1,0:T(8,128)} %get-tuple-element.44) | copy-start | bytes 1179652
  50.9 22.5 %copy-start.1 = (s32[128,8]{0,1:T(8,128)S(1)}, s32[128,8]{0,1:T(8,128)}, u32[]{:S(2)}) copy-start(s32[128,8]{0,1:T(8,128)} %param.17) | copy-start | bytes 12292
  51.0 22.5 %copy-start.2 = (f32[128,8]{0,1:T(8,128)S(1)}, f32[128,8]{0,1:T(8,128)}, u32[]{:S(2)}) copy-start(f32[128,8]{0,1:T(8,128)} %param.18) | copy-start | bytes 12292
  51.0 26.2 %all-to-all-start.1 = ((bf16[16,32,2048]{2,1,0:T(8,128)(2,1)}), bf16[16,32,2048]{2,1,0:T(8,128)(2,1)S(1)}, u32[]{:S(2)}, u32[]{:S(2)}) async-start(bf16[16,32,2048]{2,1,0:T(8,128)(2,1)} %get-tuple-element.40), calls=%async_computation.1 | async-start | bytes 4194304 | tf_op jit(solution)/shard_map/all_to_all | solution.py:499
  54.8 7.2 %collective-permute-start = (bf16[4,2,96,128]{3,2,1,0:T(8,128)(2,1)S(1)}, bf16[4,2,96,128]{3,2,1,0:T(8,128)(2,1)S(1)}, u32[]{:S(2)}, u32[]{:S(2)}) collective-permute-start(bf16[4,2,96,128]{3,2,1,0:T(8,128)(2,1)S(1)} %copy-done.4), channel_id=1, source_target_pairs={{0,32},{16,48},{32,0},{48,16},{64,96},{80,112},{96,64},{112,80},{1... | collective-permute-start | bytes 589832 | tf_op jit(solution)/shard_map/ppermute | solution.py:502
  62.1 8.1 %collective-permute-start.1 = (bf16[2,96,128]{2,1,0:T(8,128)(2,1)S(1)}, bf16[2,96,128]{2,1,0:T(8,128)(2,1)S(1)}, u32[]{:S(2)}, u32[]{:S(2)}) collective-permute-start(bf16[2,96,128]{2,1,0:T(8,128)(2,1)S(1)} %get-tuple-element.52), channel_id=1, source_target_pairs={{0,128},{16,144},{32,160},{48,176},{64,192},{80,208},{96,224},{112... | collective-permute-start | bytes 147464 | tf_op jit(solution)/shard_map/ppermute | solution.py:502
  67.1 6.2 %collective-permute-start.3 = (bf16[2,96,128]{2,1,0:T(8,128)(2,1)S(1)}, bf16[2,96,128]{2,1,0:T(8,128)(2,1)S(1)}, u32[]{:S(2)}, u32[]{:S(2)}) collective-permute-start(bf16[2,96,128]{2,1,0:T(8,128)(2,1)S(1)} %get-tuple-element.53), channel_id=1, source_target_pairs={{0,192},{16,208},{32,224},{48,240},{64,128},{80,144},{96,160},{112... | collective-permute-start | bytes 147464 | tf_op jit(solution)/shard_map/ppermute | solution.py:502
  67.9 5.4 %collective-permute-start.2 = (bf16[2,96,128]{2,1,0:T(8,128)(2,1)S(1)}, bf16[2,96,128]{2,1,0:T(8,128)(2,1)S(1)}, u32[]{:S(2)}, u32[]{:S(2)}) collective-permute-start(bf16[2,96,128]{2,1,0:T(8,128)(2,1)S(1)} %get-tuple-element.54), channel_id=1, source_target_pairs={{0,64},{16,80},{32,96},{48,112},{64,0},{80,16},{96,32},{112,48},{1... | collective-permute-start | bytes 147464 | tf_op jit(solution)/shard_map/ppermute | solution.py:502
  73.4 1.3 %collective-permute-start.4 = (f32[96,128]{1,0:T(8,128)S(1)}, f32[96,128]{1,0:T(8,128)S(1)}, u32[]{:S(2)}, u32[]{:S(2)}) collective-permute-start(f32[96,128]{1,0:T(8,128)S(1)} %get-tuple-element.55), channel_id=1, source_target_pairs={{0,16},{16,0},{32,48},{48,32},{64,80},{80,64},{96,112},{112,96},{1... | collective-permute-start | bytes 147464 | tf_op jit(solution)/shard_map/ppermute | solution.py:502
  73.8 0.7 copy-start

commit v6 on v5

--- a/solution.py
+++ b/solution.py
@@ -16,7 +16,7 @@
 SMEM = pl.BlockSpec(memory_space=pltpu.SMEM)
 HBM = pl.BlockSpec(memory_space=pltpu.HBM)
 DMA = pltpu.SemaphoreType.DMA
-SPLITS = {1280: 1280, 2048: 768}
+SPLITS = {1536: 1536, 2048: 512}
 
 
 def nn(a, b):
@@ -243,7 +243,7 @@
     gate_scale_hbm, up_scale_hbm, down_scale_hbm, gate_first_hbm, up_first_hbm, down_second_hbm,
     gate_second_hbm, up_second_hbm, down_first_hbm, send_hbm, keep_hbm, other_hbm,
     gate_ref, up_ref, down_ref, gate_scale_ref, up_scale_ref, down_scale_ref, wide_ref, narrow_ref, send_ref,
-    inside_ref, down_low_ref, back_both_ref, piece_ref, rounded_ref, level_sem, small_sem, scale_sem, out_sem, piece_sem,
+    inside_ref, down_low_ref, back_both_ref, piece_ref, keep_ref, other_ref, level_sem, small_sem, scale_sem, out_sem, piece_sem,
 ):
     experts, _, width = got_ref.shape
     rows = experts * CAP
@@ -418,18 +418,22 @@
     group = group_ref[0]
     side = group % 2
     plane = group // 2
-    rounded_ref[...] = piece_ref[...].astype(BF)
     half = groups // 4
     for place in range(groups // 2):
         turned = (place & 1) * 4 + (place & 2) + (place >> 2)
         other = lax.bitwise_xor(plane, jnp.int32(turned))
-        source, target = (piece_ref, keep_hbm) if place < half else (rounded_ref, other_hbm)
         for i, core in enumerate((side, 1 - side)):
-            copy = pltpu.make_async_copy(
-                source.at[2 * other + core], target.at[place % half, i], piece_sem.at[place, i]
-            )
-            stores.append(copy)
-            copy.start()
+            piece = piece_ref[2 * other + core]
+            if place < half:
+                keep_ref[place, i] = piece
+            else:
+                other_ref[place - half, i] = piece.astype(BF)
+    stores += [
+        pltpu.make_async_copy(keep_ref, keep_hbm, piece_sem.at[0]),
+        pltpu.make_async_copy(other_ref, other_hbm, piece_sem.at[1]),
+    ]
+    for store in stores[-2:]:
+        store.start()
     for store in stores:
         store.wait()
 
@@ -453,8 +457,8 @@
             pltpu.VMEM((3 * rank, width), BF), pltpu.VMEM((3 * rank, inner), BF),
             pltpu.VMEM(got.shape, BF), pltpu.VMEM((3, rows, inner), BF), pltpu.VMEM((rows, rank), BF),
             pltpu.VMEM((rows, 2 * rank), BF), pltpu.VMEM((groups, height, column), F32),
-            pltpu.VMEM((groups, height, column), BF),
-            DMA((inner // 256, 3)), DMA((7,)), DMA((3,)), DMA((width // 256,)), DMA((groups // 2, 2)),
+            pltpu.VMEM(part, F32), pltpu.VMEM(part, BF),
+            DMA((inner // 256, 3)), DMA((7,)), DMA((3,)), DMA((width // 256,)), DMA((2,)),
         ],
         compiler_params=params(32),
         name="expert",

time: 80 us -> 79.9 us (level)
  no operation moved by 1% of the time
where the time goes in v6:
time: 79.9 us; the launch traced here: 79.5 us
  blocking collectives  27.1 us (34%)
  Pallas kernels  25.6 us (32%)
  waiting for transfers between devices  14 us (18%)
  starting transfers between devices  11.1 us (14%)
  between operations  0.94 us (1%)
    all_to_all x1, blocking collectives, shards(): lax.all_to_all(send, 'expert', split_axis=0, concat_axis=0, tiled=True)  27.1 us
    ppermute x5, waiting for transfers between devices, swap(): return lax.ppermute(part, 'dp', [(i, i ^ mask) for i in range(groups)])  11.5 us
    pallas_call x1, Pallas kernels, expert(): pl.pallas_call(expert_kernel, out_shape=(pltpu.HBM(got.shape, BF), pltpu....  11.3 us
    pallas_call x1, Pallas kernels, freeze(): pl.pallas_call(freeze_kernel, out_shape=tuple((pltpu.HBM(level.shape, BF)...  8.72 us
    ppermute x5, starting transfers between devices, swap(): return lax.ppermute(part, 'dp', [(i, i ^ mask) for i in range(groups)])  7.19 us
    all_to_all x1, starting transfers between devices, shards(): lax.all_to_all(send, 'expert', split_axis=0, concat_axis=0, tiled=True)  3.86 us
    pallas_call x1, Pallas kernels, dispatch(): pl.pallas_call(dispatch_kernel, out_shape=pltpu.HBM(shape, BF), in_specs=...  2.94 us
    all_to_all x1, waiting for transfers between devices, shards(): lax.all_to_all(send, 'expert', split_axis=0, concat_axis=0, tiled=True)  2.5 us
  transfers between devices with their start and end apart: 6, of which 5 were waited for; matrix products, arithmetic and copies ran while one was open for 0% of the time, Pallas kernels for 0%

profile of v6, /device:TPU:32, one launch (start us, length us, event | category | flops | bytes accessed | tf_op | source)
XLA Modules:
  0.0 79.5 jit_solution(8673216593452034680)
XLA Ops:
  0.6 8.7 %freeze.1 = (bf16[2048,768]{1,0:T(8,128)(2,1)}, bf16[2048,768]{1,0:T(8,128)(2,1)}, bf16[768,2048]{1,0:T(8,128)(2,1)}) custom-call(s32[1]{0:T(128)} %bitcast.2.group_ref, bf16[2048,768]{1,0:T(8,128)(2,1)} %bitcast.35, bf16[2048,768]{1,0:T(8,128)(2,1)} %bitcast.37, bf16[768,2048]{1,0:T(8,128)(2,1)} %bitcast.39, f32[16,768]{1,0:T(8,128)} %bitcast.47, ...), custom_call_target="tpu_custom_call" | custom-call | flops 16777216 | bytes 16777216 | tf_op jit(solution)/shard_map/freeze/pallas_call | solution.py:226
  9.4 2.9 %dispatch.1 = bf16[16,32,2048]{2,1,0:T(8,128)(2,1)} custom-call(s32[8,128]{1,0:T(8,128)} %bitcast.31, f32[8,128]{1,0:T(8,128)} %bitcast.33, bf16[128,2048]{1,0:T(8,128)(2,1)} %act_hbm.1, bf16[128,2048]{1,0:T(8,128)(2,1)} %up_hbm.1), custom_call_target="tpu_custom_call" | custom-call | tf_op jit(solution)/shard_map/dispatch/pallas_call | solution.py:105
  12.3 27.1 %all_to_all.10.got_ref = bf16[16,32,2048]{2,1,0:T(8,128)(2,1)S(1)} all-to-all(bf16[16,32,2048]{2,1,0:T(8,128)(2,1)} %dispatch.1), channel_id=1, replica_groups=mesh['dp'=16,'expert'=16] {'expert'}, dimensions={0} | all-to-all | bytes 4194304 | tf_op jit(solution)/shard_map/all_to_all | solution.py:489
  39.4 11.3 %expert.1 = (bf16[16,32,2048]{2,1,0:T(8,128)(2,1)}, f32[4,2,96,128]{3,2,1,0:T(8,128)}, bf16[4,2,96,128]{3,2,1,0:T(8,128)(2,1)}) custom-call(s32[1]{0:T(128)} %bitcast.2.group_ref, bf16[16,32,2048]{2,1,0:T(8,128)(2,1)S(1)} %all_to_all.10.got_ref, bf16[2048,768]{1,0:T(8,128)(2,1)} %bitcast.36, bf16[2048,768]{1,0:T(8,128)(2,1)} %bitcast.38, ...), custom_call_target="tpu_custom_call" | custom-call | tf_op jit(solution)/shard_map/expert/pallas_call | solution.py:449
  50.8 0.0 copy-start.4
  50.8 0.0 copy-start.3
  50.8 0.0 copy-start.1
  50.8 0.0 copy-start.2
  50.8 3.9 %all-to-all-start.1 = ((bf16[16,32,2048]{2,1,0:T(8,128)(2,1)}), bf16[16,32,2048]{2,1,0:T(8,128)(2,1)S(1)}, u32[]{:S(2)}, u32[]{:S(2)}) async-start(bf16[16,32,2048]{2,1,0:T(8,128)(2,1)} %get-tuple-element.40), calls=%async_computation.1 | async-start | bytes 4194304 | tf_op jit(solution)/shard_map/all_to_all | solution.py:503
  54.7 0.0 copy-done.4
  54.7 0.2 collective-permute-start
  54.9 7.0 %collective-permute-done = bf16[4,2,96,128]{3,2,1,0:T(8,128)(2,1)S(1)} collective-permute-done((bf16[4,2,96,128]{3,2,1,0:T(8,128)(2,1)S(1)}, bf16[4,2,96,128]{3,2,1,0:T(8,128)(2,1)S(1)}, u32[]{:S(2)}, u32[]{:S(2)}) %collective-permute-start) | collective-permute-done | bytes 196640 | tf_op jit(solution)/shard_map/ppermute | solution.py:506
  61.9 0.0 copy-done.3
  61.9 0.1 fusion.1
  62.0 5.0 %collective-permute-start.1 = (bf16[2,96,128]{2,1,0:T(8,128)(2,1)S(1)}, bf16[2,96,128]{2,1,0:T(8,128)(2,1)S(1)}, u32[]{:S(2)}, u32[]{:S(2)}) collective-permute-start(bf16[2,96,128]{2,1,0:T(8,128)(2,1)S(1)} %get-tuple-element.52), channel_id=1, source_target_pairs={{0,128},{16,144},{32,160},{48,176},{64,192},{80,208},{96,224},{112... | collective-permute-start | bytes 147464 | tf_op jit(solution)/shard_map/ppermute | solution.py:506
  67.0 0.8 %collective-permute-start.3 = (bf16[2,96,128]{2,1,0:T(8,128)(2,1)S(1)}, bf16[2,96,128]{2,1,0:T(8,128)(2,1)S(1)}, u32[]{:S(2)}, u32[]{:S(2)}) collective-permute-start(bf16[2,96,128]{2,1,0:T(8,128)(2,1)S(1)} %get-tuple-element.53), channel_id=1, source_target_pairs={{0,192},{16,208},{32,224},{48,240},{64,128},{80,144},{96,160},{112... | collective-permute-start | bytes 147464 | tf_op jit(solution)/shard_map/ppermute | solution.py:506
  67.8 1.1 %collective-permute-start.2 = (bf16[2,96,128]{2,1,0:T(8,128)(2,1)S(1)}, bf16[2,96,128]{2,1,0:T(8,128)(2,1)S(1)}, u32[]{:S(2)}, u32[]{:S(2)}) collective-permute-start(bf16[2,96,128]{2,1,0:T(8,128)(2,1)S(1)} %get-tuple-element.54), channel_id=1, source_target_pairs={{0,64},{16,80},{32,96},{48,112},{64,0},{80,16},{96,32},{112,48},{1... | collective-permute-start | bytes 147464 | tf_op jit(solution)/shard_map/ppermute | solution.py:506
  68.9 1.2 %collective-permute-done.1 = bf16[2,96,128]{2,1,0:T(8,128)(2,1)S(1)} collective-permute-done((bf16[2,96,128]{2,1,0:T(8,128)(2,1)S(1)}, bf16[2,96,128]{2,1,0:T(8,128)(2,1)S(1)}, u32[]{:S(2)}, u32[]{:S(2)}) %collective-permute-start.1) | collective-permute-done | bytes 49184 | tf_op jit(solution)/shard_map/ppermute | solution.py:506
  70.1 3.1 %collective-permute-done.3 = bf16[2,96,128]{2,1,0:T(8,128)(2,1)S(1)} collective-permute-done((bf16[2,96,128]{2,1,0:T(8,128)(2,1)S(1)}, bf16[2,96,128]{2,1,0:T(8,128)(2,1)S(1)}, u32[]{:S(2)}, u32[]{:S(2)}) %collective-permute-start.3) | collective-permute-done | bytes 49184 | tf_op jit(solution)/shard_map/ppermute | solution.py:506
  73.2 0.0 collective-permute-done.2
  73.2 0.1 collective-permute-start.4
  73.3 0.0 copy-done.1
  73.3 0.0 copy-done.2
  73.3 0.3 tables.1.table_hbm
  73.6 0.0 copy-start
  73.6 0.7 copy-done
  74.3 0.2 collective-permute-done.4.theirs_ref
  74.5 2.5 %all-to-all-done.1.got_ref = bf16[16,32,2048]{2,1,0:T(8,128)(2,1)S(1)} async-done(((bf16[16,32,2048]{2,1,0:T(8,128)(2,1)}), bf16[16,32,2048]{2,1,0:T(8,128)(2,1)S(1)}, u32[]{:S(2)}, u32[]{:S(2)}) %all-to-all-start.1) | async-done | bytes 2097184 | tf_op jit(solution)/shard_map/all_to_all | solution.py:503
  77.0 2.3 %combine.1 = (bf16[128,2048]{1,0:T(8,128)(2,1)}, bf16[128,2048]{1,0:T(8,128)(2,1)}, f32[48,128]{1,0:T(8,128)}, f32[3,1,768]{2,1,0:T(1,128)}) custom-call(bf16[16,32,2048]{2,1,0:T(8,128)(2,1)S(1)} %all-to-all-done.1.got_ref, bf16[3,128,256]{2,1,0:T(8,128)(2,1)} %copy-done, f32[96,128]{1,0:T(8,128)S(1)} %get-tuple-element.56.mine_ref, ...), custom_call_target="tpu_custom_call" | custom-call | tf_op jit(solution)/shard_map/combine/pallas_call | solution.py:181
  (3 shorter events, 0.0 us)
Async XLA Ops:
  50.8 3.9 %copy-start.4 = (bf16[4,2,96,128]{3,2,1,0:T(8,128)(2,1)S(1)}, bf16[4,2,96,128]{3,2,1,0:T(8,128)(2,1)}, u32[]{:S(2)}) copy-start(bf16[4,2,96,128]{3,2,1,0:T(8,128)(2,1)} %get-tuple-element.45) | copy-start | bytes 589828
  50.8 11.1 %copy-start.3 = (f32[4,2,96,128]{3,2,1,0:T(8,128)S(1)}, f32[4,2,96,128]{3,2,1,0:T(8,128)}, u32[]{:S(2)}) copy-start(f32[4,2,96,128]{3,2,1,0:T(8,128)} %get-tuple-element.44) | copy-start | bytes 1179652
  50.8 22.5 %copy-start.1 = (s32[128,8]{0,1:T(8,128)S(1)}, s32[128,8]{0,1:T(8,128)}, u32[]{:S(2)}) copy-start(s32[128,8]{0,1:T(8,128)} %param.17) | copy-start | bytes 12292
  50.8 22.5 %copy-start.2 = (f32[128,8]{0,1:T(8,128)S(1)}, f32[128,8]{0,1:T(8,128)}, u32[]{:S(2)}) copy-start(f32[128,8]{0,1:T(8,128)} %param.18) | copy-start | bytes 12292
  50.8 26.2 %all-to-all-start.1 = ((bf16[16,32,2048]{2,1,0:T(8,128)(2,1)}), bf16[16,32,2048]{2,1,0:T(8,128)(2,1)S(1)}, u32[]{:S(2)}, u32[]{:S(2)}) async-start(bf16[16,32,2048]{2,1,0:T(8,128)(2,1)} %get-tuple-element.40), calls=%async_computation.1 | async-start | bytes 4194304 | tf_op jit(solution)/shard_map/all_to_all | solution.py:503
  54.7 7.2 %collective-permute-start = (bf16[4,2,96,128]{3,2,1,0:T(8,128)(2,1)S(1)}, bf16[4,2,96,128]{3,2,1,0:T(8,128)(2,1)S(1)}, u32[]{:S(2)}, u32[]{:S(2)}) collective-permute-start(bf16[4,2,96,128]{3,2,1,0:T(8,128)(2,1)S(1)} %copy-done.4), channel_id=1, source_target_pairs={{0,32},{16,48},{32,0},{48,16},{64,96},{80,112},{96,64},{112,80},{1... | collective-permute-start | bytes 589832 | tf_op jit(solution)/shard_map/ppermute | solution.py:506
  62.0 8.1 %collective-permute-start.1 = (bf16[2,96,128]{2,1,0:T(8,128)(2,1)S(1)}, bf16[2,96,128]{2,1,0:T(8,128)(2,1)S(1)}, u32[]{:S(2)}, u32[]{:S(2)}) collective-permute-start(bf16[2,96,128]{2,1,0:T(8,128)(2,1)S(1)} %get-tuple-element.52), channel_id=1, source_target_pairs={{0,128},{16,144},{32,160},{48,176},{64,192},{80,208},{96,224},{112... | collective-permute-start | bytes 147464 | tf_op jit(solution)/shard_map/ppermute | solution.py:506
  67.0 6.2 %collective-permute-start.3 = (bf16[2,96,128]{2,1,0:T(8,128)(2,1)S(1)}, bf16[2,96,128]{2,1,0:T(8,128)(2,1)S(1)}, u32[]{:S(2)}, u32[]{:S(2)}) collective-permute-start(bf16[2,96,128]{2,1,0:T(8,128)(2,1)S(1)} %get-tuple-element.53), channel_id=1, source_target_pairs={{0,192},{16,208},{32,224},{48,240},{64,128},{80,144},{96,160},{112... | collective-permute-start | bytes 147464 | tf_op jit(solution)/shard_map/ppermute | solution.py:506
  67.8 5.4 %collective-permute-start.2 = (bf16[2,96,128]{2,1,0:T(8,128)(2,1)S(1)}, bf16[2,96,128]{2,1,0:T(8,128)(2,1)S(1)}, u32[]{:S(2)}, u32[]{:S(2)}) collective-permute-start(bf16[2,96,128]{2,1,0:T(8,128)(2,1)S(1)} %get-tuple-element.54), channel_id=1, source_target_pairs={{0,64},{16,80},{32,96},{48,112},{64,0},{80,16},{96,32},{112,48},{1... | collective-permute-start | bytes 147464 | tf_op jit(solution)/shard_map/ppermute | solution.py:506
  73.2 1.3 %collective-permute-start.4 = (f32[96,128]{1,0:T(8,128)S(1)}, f32[96,128]{1,0:T(8,128)S(1)}, u32[]{:S(2)}, u32[]{:S(2)}) collective-permute-start(f32[96,128]{1,0:T(8,128)S(1)} %get-tuple-element.55), channel_id=1, source_target_pairs={{0,16},{16,0},{32,48},{48,32},{64,80},{80,64},{96,112},{112,96},{1... | collective-permute-start | bytes 147464 | tf_op jit(solution)/shard_map/ppermute | solution.py:506
  73.6 0.7 copy-start
